TPU v7x, 32 devices: a whole 2x2x4 slice. The times are simulated.
32 devices in a mesh: rows: 8 (over z, y), band: 4 (over x, core).
Axes of the slice: x: 2, y: 2, z: 4, core: 2. Of those that a mesh axis runs over, the one named last changes fastest.
Arguments:
- frames: bfloat16 [2, 32, 512, 96], P(None, 'rows'), may hold values from -6 to 6
- conv_weight: bfloat16 [3, 3, 96, 128], replicated, may hold values from -0.21875 to 0.21875
- proj_weight: bfloat16 [128, 256], replicated, may hold values from -0.5 to 0.5
- band_start: int32 [8], P('rows'), may hold values from -4 to 4, as said below
- band_count: int32 [8], P('rows'), may hold values from 1 to 8, as said below
- pyramid_grad: bfloat16 [8, 2, 4, 512, 960], P('rows', None, 'band'), may hold values from -6 to 6
Outputs:
- pyramid: bfloat16 [8, 2, 4, 512, 960], P('rows', None, 'band')
- source_grad: float32 [16, 256, 256], P('rows', None, 'band')
- target_grad: float32 [16, 256, 256], P('rows', None, 'band')
Inputs may be any that keep to these rules, and one draw needn't show every extreme that they name: Row block b's band covers target blocks b + band_start[b] to b + band_start[b] + band_count[b] - 1, all within b - 4 to b + 4. `band_count`: some row block's band has 8 target blocks and some other's has 1.
All inputs are finite; a program needn't handle non-finite values.
Results may differ from a plain program's by a relative error of at most 0.0034.
Values may be sent and summed in bfloat16 or wider, within the bound.
No kernel may reach another device: no remote copies, remote signals or barrier semaphores. Data moves between devices by JAX's collectives and lax.ppermute only.
A program may use at most 128 MiB of HBM per device.

v0:
```python
import math

import jax
import jax.numpy as jnp
from jax import lax
from jax.sharding import PartitionSpec as P

LEVELS = 4
ROWS_DEV = 2
COLUMNS = 256
BAND_REACH = 4
PIXELS = 512


HIGHEST = lax.Precision.HIGHEST


def shifted(x, axis, by):
    size = lax.axis_size(axis)
    pairs = [(i, i + by) for i in range(size) if 0 <= i + by < size]
    return lax.ppermute(x, axis, pairs)


def convolve(extended, conv_weight, proj_weight):
    convolved = lax.conv_general_dilated(
        extended,
        conv_weight,
        (2, 2),
        ((0, 0), (1, 0)),
        dimension_numbers=("NHWC", "HWIO", "NHWC"),
        preferred_element_type=jnp.float32,
    )
    middle = jax.nn.relu(convolved).astype(jnp.bfloat16)
    batches = middle.shape[0]
    flattened = jnp.dot(
        middle.reshape(-1, middle.shape[3]), proj_weight, preferred_element_type=jnp.float32
    )
    return flattened.reshape(batches, -1, proj_weight.shape[1])


def pool_levels(correlation):
    row_count = correlation.shape[0]
    levels = []
    for level_index in range(LEVELS):
        group_size = 2**level_index
        pooled = correlation.reshape(row_count, ROWS_DEV, COLUMNS // group_size, group_size)
        levels.append(jnp.mean(pooled, axis=3).reshape(row_count, PIXELS // group_size))
    return jnp.concatenate(levels, axis=1)


def spread_levels(gradient):
    row_count = gradient.shape[0]
    summed = gradient[:, :PIXELS]
    column_start = PIXELS
    for level_index in range(1, LEVELS):
        group_size = 2**level_index
        level_width = PIXELS // group_size
        level_part = gradient[:, column_start : column_start + level_width].reshape(
            row_count, ROWS_DEV, level_width // ROWS_DEV, 1
        )
        spread = jnp.broadcast_to(
            level_part / group_size, (row_count, ROWS_DEV, level_width // ROWS_DEV, group_size)
        )
        summed = summed + spread.reshape(row_count, PIXELS)
        column_start = column_start + level_width
    return summed


def add_into(window_grad, window_place, target_part):
    current = lax.dynamic_index_in_dim(window_grad, window_place, 0, keepdims=False)
    return lax.dynamic_update_index_in_dim(window_grad, current + target_part, window_place, 0)


def shards(frames, conv_weight, proj_weight, band_start, band_count, pyramid_grad):
    band_size = lax.axis_size("band")
    position = lax.axis_index("band")
    channels = proj_weight.shape[1]
    share_width = channels // band_size
    factor = 1.0 / math.sqrt(channels)
    rim_row = shifted(frames[:, -1:], "rows", 1)
    extended = jnp.concatenate([rim_row, frames], axis=1)
    features = convolve(extended, conv_weight, proj_weight)
    source = features[0]
    own_target = features[1]
    pieces = []
    for offset in range(-BAND_REACH, BAND_REACH + 1):
        if offset == 0:
            pieces.append(own_target)
        else:
            pieces.append(shifted(own_target, "rows", -offset))
    window = jnp.stack(pieces)
    band_first = band_start[0]
    band_width = band_count[0]
    source_sum = jnp.zeros(source.shape, jnp.float32)
    slot_count = pyramid_grad.shape[1]
    outputs = []
    tile_parts = []
    tile_places = []
    for slot_local in range(slot_count):
        slot_index = slot_local * band_size + position
        window_place = band_first + slot_index + BAND_REACH
        target = lax.dynamic_index_in_dim(window, window_place, 0, keepdims=False)

        def compute(operands):
            source_block, target_block, grad_block = operands
            correlation = (
                lax.dot_general(
                    source_block, target_block, (((1,), (1,)), ((), ())), precision=HIGHEST
                )
                * factor
            )
            pyramid = pool_levels(correlation).astype(jnp.bfloat16)
            grad_corr = spread_levels(grad_block.astype(jnp.float32))
            source_part = jnp.dot(grad_corr, target_block, precision=HIGHEST) * factor
            target_part = (
                lax.dot_general(
                    grad_corr, source_block, (((0,), (0,)), ((), ())), precision=HIGHEST
                )
                * factor
            )
            return (pyramid, source_part, target_part)

        def skipped(operands):
            source_block, target_block, grad_block = operands
            return (
                jnp.zeros(grad_block.shape, jnp.bfloat16),
                jnp.zeros_like(source_block),
                jnp.zeros_like(source_block),
            )

        pyramid, source_part, target_part = lax.cond(
            slot_index < band_width,
            compute,
            skipped,
            (source, target, pyramid_grad[0, slot_local, 0]),
        )
        pyramid, source_part, target_part, window_place = (
            pyramid,
            source_part,
            target_part,
            window_place,
        )
        outputs.append(pyramid)
        source_sum = source_sum + source_part
        tile_parts.append(target_part)
        tile_places.append(window_place)
    pyramid_out = jnp.stack(outputs)[None, :, None]
    shape_out = (ROWS_DEV, COLUMNS, share_width)
    window_grad = jnp.zeros(window.shape, jnp.float32)
    for tile_index in range(len(tile_parts)):
        window_grad = add_into(window_grad, tile_places[tile_index], tile_parts[tile_index])
    received = window_grad[BAND_REACH]
    for offset in range(-BAND_REACH, BAND_REACH + 1):
        if offset != 0:
            received = received + shifted(window_grad[offset + BAND_REACH], "rows", offset)
    source_share, target_share = (
        lax.psum_scatter(source_sum, "band", scatter_dimension=1, tiled=True),
        lax.psum_scatter(received, "band", scatter_dimension=1, tiled=True),
    )
    return (pyramid_out, source_share.reshape(shape_out), target_share.reshape(shape_out))


def solution(mesh):
    in_specs = (
        P(None, "rows", None, None),
        P(),
        P(),
        P("rows"),
        P("rows"),
        P("rows", None, "band", None, None),
    )
    out_specs = (
        P("rows", None, "band", None, None),
        P("rows", None, "band"),
        P("rows", None, "band"),
    )
    return jax.shard_map(shards, mesh=mesh, in_specs=in_specs, out_specs=out_specs, check_vma=False)
```

profile of v0, /device:TPU:25, one launch (start us, length us, event | category | flops | bytes accessed | tf_op | source)
XLA Modules:
  0.0 275.5 jit_solution(7189201021048382405)
XLA Ops:
  7.2 1.0 slice.82
  8.2 3.1 %collective-permute-start = (bf16[2,1,512,96]{2,3,1,0:T(8,128)(2,1)S(1)}, bf16[2,1,512,96]{2,3,1,0:T(8,128)(2,1)S(1)}, u32[]{:S(2)}, u32[]{:S(2)}) collective-permute-start(bf16[2,1,512,96]{2,3,1,0:T(8,128)(2,1)S(1)} %slice.82), channel_id=1, source_target_pairs={{0,4},{4,8},{8,12},{12,16},{16,20},{20,24},{24,28},{1,5},{5,9},{9,... | collective-permute-start | bytes 589832 | tf_op jit(solution)/shard_map/ppermute | solution.py:21
  11.4 5.4 %collective-permute-done = bf16[2,1,512,96]{2,3,1,0:T(8,128)(2,1)S(1)} collective-permute-done((bf16[2,1,512,96]{2,3,1,0:T(8,128)(2,1)S(1)}, bf16[2,1,512,96]{2,3,1,0:T(8,128)(2,1)S(1)}, u32[]{:S(2)}, u32[]{:S(2)}) %collective-permute-start) | collective-permute-done | bytes 196640 | tf_op jit(solution)/shard_map/ppermute | solution.py:21
  16.8 1.2 maximum_bitcast_fusion.1
  18.0 1.1 copy.39
  19.1 1.4 pad.clone
  20.5 3.5 %fusion.17 = bf16[5,2,8,68,96]{4,1,3,2,0:T(2,128)(2,1)S(1)} fusion(bf16[5,2,7,2,96]{4,1,3,2,0:T(2,128)(2,1)S(1)} %slice.105, bf16[5,2,8,66,96]{4,1,3,2,0:T(2,128)(2,1)S(1)} %bitcast.173), kind=kLoop, calls=%fused_computation.47 | loop fusion | flops 3133440 | bytes 2085120 | tf_op jit(solution)/shard_map/conv_general_dilated | solution.py:25
  25.6 0.9 fusion.39
  26.4 1.3 collective-permute-start.1
  27.7 1.3 collective-permute-start.2
  29.0 1.3 collective-permute-start.3
  31.6 2.2 collective-permute-start.4
  33.9 3.9 %collective-permute-start.5 = (f32[512,256]{1,0:T(8,128)}, f32[512,256]{1,0:T(8,128)S(1)}, u32[]{:S(2)}, u32[]{:S(2)}) collective-permute-start(f32[512,256]{1,0:T(8,128)} %get-tuple-element.96), channel_id=1, source_target_pairs={{4,0},{8,4},{12,8},{16,12},{20,16},{24,20},{28,24},{5,1},{9,5},{13... | collective-permute-start | bytes 1572872 | tf_op jit(solution)/shard_map/ppermute | solution.py:21
  37.8 16.6 %collective-permute-done.1 = f32[512,256]{1,0:T(8,128)S(1)} collective-permute-done((f32[512,256]{1,0:T(8,128)}, f32[512,256]{1,0:T(8,128)S(1)}, u32[]{:S(2)}, u32[]{:S(2)}) %collective-permute-start.1) | collective-permute-done | bytes 524320 | tf_op jit(solution)/shard_map/ppermute | solution.py:21
  54.4 1.3 collective-permute-start.6
  56.6 20.4 %collective-permute-done.2 = f32[512,256]{1,0:T(8,128)S(1)} collective-permute-done((f32[512,256]{1,0:T(8,128)}, f32[512,256]{1,0:T(8,128)S(1)}, u32[]{:S(2)}, u32[]{:S(2)}) %collective-permute-start.2) | collective-permute-done | bytes 524320 | tf_op jit(solution)/shard_map/ppermute | solution.py:21
  77.0 1.3 collective-permute-start.7
  78.3 0.9 bitcast_dynamic-update-slice_fusion.7
  79.2 1.3 collective-permute-start.8
  80.5 0.8 bitcast_dynamic-update-slice_fusion.6
  83.8 0.9 bitcast_dynamic-update-slice_fusion.2
  84.7 4.7 %collective-permute-done.7 = f32[512,256]{1,0:T(8,128)S(1)} collective-permute-done((f32[512,256]{1,0:T(8,128)}, f32[512,256]{1,0:T(8,128)S(1)}, u32[]{:S(2)}, u32[]{:S(2)}) %collective-permute-start.7) | collective-permute-done | bytes 524320 | tf_op jit(solution)/shard_map/ppermute | solution.py:21
  89.3 0.9 bitcast_dynamic-update-slice_fusion.1
  90.2 10.4 %collective-permute-done.8 = f32[512,256]{1,0:T(8,128)S(1)} collective-permute-done((f32[512,256]{1,0:T(8,128)}, f32[512,256]{1,0:T(8,128)S(1)}, u32[]{:S(2)}, u32[]{:S(2)}) %collective-permute-start.8) | collective-permute-done | bytes 524320 | tf_op jit(solution)/shard_map/ppermute | solution.py:21
  100.6 0.9 bitcast_dynamic-update-slice_fusion
  101.5 22.3 %conditional.2 = (f32[512,256]{1,0:T(8,128)}, bf16[1,512,960]{1,2,0:T(8,128)(2,1)}, f32[1,512,256]{1,2,0:T(8,128)}) conditional(s32[]{:T(128)} %convert_element_type.37, () %tuple.34, (bf16[1,2,1,512,960]{3,4,2,1,0:T(8,128)(2,1)S(1)}, f32[9,512,256]{2,1,0:T(8,128)}, s32[]{:T(128)}, f32[512,256]{1,0:T(8,128)S(1)}) %tuple.63), branch_computations={%region_0.1_spmd, %region_1.5_spmd} | conditional | flops 2423160832 | bytes 35652640 | solution.py:131
  101.9 1.3 reshape.262
  103.7 1.7 reshape.261
  105.4 2.0 fusion.2
  107.4 3.7 %convolution_multiply_fusion.2 = f32[512,256]{1,0:T(8,128)} fusion(f32[512,512]{0,1:T(8,128)S(1)} %fusion.2, f32[9,512,256]{2,1,0:T(8,128)} %get-tuple-element.46, s32[]{:T(128)} %get-tuple-element.47), kind=kOutput, calls=%fused_computation.3 | convolution fusion | flops 805437440 | bytes 2097664 | tf_op jit(solution)/shard_map/cond/branch_1_fun/dot_general | solution.py:114
  111.0 2.3 bitcast_reduce_fusion
  113.4 1.3 reshape.265
  114.6 1.8 reduce_sum.59
  116.5 1.6 reshape.264
  118.1 2.5 reduce_sum.55
  120.7 1.0 pad_maximum_fusion
  121.7 1.0 fusion
  122.7 1.0 copy.38
  124.3 1.1 constant_dynamic-update-slice_fusion.1
  125.4 2.1 copy-done.2
  127.6 1.0 copy.29
  128.6 1.9 conditional.3
  129.4 1.0 stack.29
  130.4 1.3 fusion.38
  132.7 4.0 %slice_bitcast_fusion.7 = (f32[512,256]{0,1:T(8,128)S(1)}, f32[512,256]{0,1:T(8,128)}, f32[512,256]{0,1:T(8,128)}, f32[512,256]{0,1:T(8,128)}, f32[512,256]{0,1:...) fusion(f32[9,512,256]{1,2,0:T(8,128)} %constant_dynamic-update-slice_fusion), kind=kLoop, calls=%fused_computation.62 | loop fusion | bytes 8388608 | tf_op jit(solution)/shard_map/squeeze | solution.py:155
  136.8 1.3 collective-permute-start.16
  138.1 1.3 collective-permute-start.15
  139.4 1.3 collective-permute-start.14
  140.7 1.1 add.97
  141.8 1.0 copy.35
  142.8 21.4 %collective-permute-start.13 = (f32[512,256]{0,1:T(8,128)}, f32[512,256]{0,1:T(8,128)S(1)}, u32[]{:S(2)}, u32[]{:S(2)}) collective-permute-start(f32[512,256]{0,1:T(8,128)} %get-tuple-element.91), channel_id=1, source_target_pairs={{0,4},{4,8},{8,12},{12,16},{16,20},{20,24},{24,28},{1,5},{5,9},{9,... | collective-permute-start | bytes 1572872 | tf_op jit(solution)/shard_map/ppermute | solution.py:21
  164.3 3.7 %collective-permute-start.12 = (f32[512,256]{0,1:T(8,128)}, f32[512,256]{0,1:T(8,128)S(1)}, u32[]{:S(2)}, u32[]{:S(2)}) collective-permute-start(f32[512,256]{0,1:T(8,128)} %get-tuple-element.92), channel_id=1, source_target_pairs={{4,0},{8,4},{12,8},{16,12},{20,16},{24,20},{28,24},{5,1},{9,5},{13... | collective-permute-start | bytes 1572872 | tf_op jit(solution)/shard_map/ppermute | solution.py:21
  168.0 4.9 %collective-permute-start.11 = (f32[512,256]{0,1:T(8,128)}, f32[512,256]{0,1:T(8,128)S(1)}, u32[]{:S(2)}, u32[]{:S(2)}) collective-permute-start(f32[512,256]{0,1:T(8,128)} %get-tuple-element.93), channel_id=1, source_target_pairs={{8,0},{12,4},{16,8},{20,12},{24,16},{28,20},{9,1},{13,5},{17,9},{2... | collective-permute-start | bytes 1572872 | tf_op jit(solution)/shard_map/ppermute | solution.py:21
  172.9 25.9 %collective-permute-done.15 = f32[512,256]{0,1:T(8,128)S(1)} collective-permute-done((f32[512,256]{0,1:T(8,128)}, f32[512,256]{0,1:T(8,128)S(1)}, u32[]{:S(2)}, u32[]{:S(2)}) %collective-permute-start.15) | collective-permute-done | bytes 524320 | tf_op jit(solution)/shard_map/ppermute | solution.py:21
  198.8 1.3 collective-permute-start.10
  200.2 1.3 collective-permute-start.9
  201.5 5.0 %collective-permute-done.13 = f32[512,256]{0,1:T(8,128)S(1)} collective-permute-done((f32[512,256]{0,1:T(8,128)}, f32[512,256]{0,1:T(8,128)S(1)}, u32[]{:S(2)}, u32[]{:S(2)}) %collective-permute-start.13) | collective-permute-done | bytes 524320 | tf_op jit(solution)/shard_map/ppermute | solution.py:21
  206.5 4.4 %collective-permute-done.10 = f32[512,256]{0,1:T(8,128)S(1)} collective-permute-done((f32[512,256]{0,1:T(8,128)S(1)}, f32[512,256]{0,1:T(8,128)S(1)}, u32[]{:S(2)}, u32[]{:S(2)}) %collective-permute-start.10) | collective-permute-done | bytes 524320 | tf_op jit(solution)/shard_map/ppermute | solution.py:21
  210.9 11.2 %collective-permute-done.9 = f32[512,256]{0,1:T(8,128)S(1)} collective-permute-done((f32[512,256]{0,1:T(8,128)S(1)}, f32[512,256]{0,1:T(8,128)S(1)}, u32[]{:S(2)}, u32[]{:S(2)}) %collective-permute-start.9) | collective-permute-done | bytes 524320 | tf_op jit(solution)/shard_map/ppermute | solution.py:21
  222.1 2.6 fusion.37
  224.8 3.0 %maximum_bitcast_fusion = bf16[1,2,1,512,960]{3,4,2,1,0:T(8,128)(2,1)} fusion(bf16[1,512,960]{1,2,0:T(8,128)(2,1)} %get-tuple-element.63, bf16[1,512,960]{1,2,0:T(8,128)(2,1)} %get-tuple-element.62), kind=kLoop, calls=%fused_computation.46 | loop fusion | flops 983040 | bytes 3932160 | tf_op jit(solution)/shard_map/broadcast_in_dim | solution.py:147
  227.7 1.0 copy.36
  229.5 37.6 %reduce-scatter.5.cloned.1.call-done = f32[512,64]{0,1:T(8,128)} async-done(((f32[512,256]{0,1:T(8,128)}), f32[512,64]{0,1:T(8,128)}) %reduce-scatter.5.cloned.1.call-update) | async-done | bytes 131088 | tf_op jit(solution)/shard_map/reduce_scatter | solution.py:158
  267.1 1.6 copy.52
  (51 shorter events, 9.3 us)
Async XLA Ops:
  7.2 16.9 %copy-start = (bf16[3,3,96,128]{3,2,1,0:T(8,128)(2,1)S(1)}, bf16[3,3,96,128]{3,2,1,0:T(8,128)(2,1)}, u32[]{:S(2)}) copy-start(bf16[3,3,96,128]{3,2,1,0:T(8,128)(2,1)} %param.11) | copy-start | bytes 663556
  7.2 220.5 %reduce-scatter.7.cloned.1.call-start = ((), (), s32[]{:S(2)}) async-start(), calls=%async_computation.3 | async-start | bytes 655360
  8.2 8.6 %collective-permute-start = (bf16[2,1,512,96]{2,3,1,0:T(8,128)(2,1)S(1)}, bf16[2,1,512,96]{2,3,1,0:T(8,128)(2,1)S(1)}, u32[]{:S(2)}, u32[]{:S(2)}) collective-permute-start(bf16[2,1,512,96]{2,3,1,0:T(8,128)(2,1)S(1)} %slice.82), channel_id=1, source_target_pairs={{0,4},{4,8},{8,12},{12,16},{16,20},{20,24},{24,28},{1,5},{5,9},{9,... | collective-permute-start | bytes 589832 | tf_op jit(solution)/shard_map/ppermute | solution.py:21
  19.1 5.0 %copy-start.6 = (pred[16,33]{0,1:T(8,128)(4,1)S(1)}, pred[16,33]{0,1:T(8,128)(4,1)}, u32[]{:S(2)}) copy-start(pred[16,33]{0,1:T(8,128)(4,1)} %constant.104) | copy-start | bytes 1588
  20.5 4.8 %copy-start.5 = (bf16[128,256]{1,0:T(8,128)(2,1)S(1)}, bf16[128,256]{1,0:T(8,128)(2,1)}, u32[]{:S(2)}) copy-start(bf16[128,256]{1,0:T(8,128)(2,1)} %param.12) | copy-start | bytes 196612
  26.4 28.0 %collective-permute-start.1 = (f32[512,256]{1,0:T(8,128)}, f32[512,256]{1,0:T(8,128)S(1)}, u32[]{:S(2)}, u32[]{:S(2)}) collective-permute-start(f32[512,256]{1,0:T(8,128)} %get-tuple-element.96), channel_id=1, source_target_pairs={{0,16},{4,20},{8,24},{12,28},{1,17},{5,21},{9,25},{13,29},{2,18},{... | collective-permute-start | bytes 1572872 | tf_op jit(solution)/shard_map/ppermute | solution.py:21
  27.7 49.2 %collective-permute-start.2 = (f32[512,256]{1,0:T(8,128)}, f32[512,256]{1,0:T(8,128)S(1)}, u32[]{:S(2)}, u32[]{:S(2)}) collective-permute-start(f32[512,256]{1,0:T(8,128)} %get-tuple-element.96), channel_id=1, source_target_pairs={{0,12},{4,16},{8,20},{12,24},{16,28},{1,13},{5,17},{9,21},{13,25},... | collective-permute-start | bytes 1572872 | tf_op jit(solution)/shard_map/ppermute | solution.py:21
  29.0 50.1 %collective-permute-start.3 = (f32[512,256]{1,0:T(8,128)}, f32[512,256]{1,0:T(8,128)S(1)}, u32[]{:S(2)}, u32[]{:S(2)}) collective-permute-start(f32[512,256]{1,0:T(8,128)} %get-tuple-element.96), channel_id=1, source_target_pairs={{0,8},{4,12},{8,16},{12,20},{16,24},{20,28},{1,9},{5,13},{9,17},{1... | collective-permute-start | bytes 1572872 | tf_op jit(solution)/shard_map/ppermute | solution.py:21
  31.6 49.7 %collective-permute-start.4 = (f32[512,256]{1,0:T(8,128)}, f32[512,256]{1,0:T(8,128)S(1)}, u32[]{:S(2)}, u32[]{:S(2)}) collective-permute-start(f32[512,256]{1,0:T(8,128)} %get-tuple-element.96), channel_id=1, source_target_pairs={{0,4},{4,8},{8,12},{12,16},{16,20},{20,24},{24,28},{1,5},{5,9},{9,... | collective-permute-start | bytes 1572872 | tf_op jit(solution)/shard_map/ppermute | solution.py:21
  33.9 49.1 %collective-permute-start.5 = (f32[512,256]{1,0:T(8,128)}, f32[512,256]{1,0:T(8,128)S(1)}, u32[]{:S(2)}, u32[]{:S(2)}) collective-permute-start(f32[512,256]{1,0:T(8,128)} %get-tuple-element.96), channel_id=1, source_target_pairs={{4,0},{8,4},{12,8},{16,12},{20,16},{24,20},{28,24},{5,1},{9,5},{13... | collective-permute-start | bytes 1572872 | tf_op jit(solution)/shard_map/ppermute | solution.py:21
  54.4 29.4 %collective-permute-start.6 = (f32[512,256]{1,0:T(8,128)}, f32[512,256]{1,0:T(8,128)S(1)}, u32[]{:S(2)}, u32[]{:S(2)}) collective-permute-start(f32[512,256]{1,0:T(8,128)} %get-tuple-element.96), channel_id=1, source_target_pairs={{8,0},{12,4},{16,8},{20,12},{24,16},{28,20},{9,1},{13,5},{17,9},{2... | collective-permute-start | bytes 1572872 | tf_op jit(solution)/shard_map/ppermute | solution.py:21
  77.0 12.4 %collective-permute-start.7 = (f32[512,256]{1,0:T(8,128)}, f32[512,256]{1,0:T(8,128)S(1)}, u32[]{:S(2)}, u32[]{:S(2)}) collective-permute-start(f32[512,256]{1,0:T(8,128)} %get-tuple-element.96), channel_id=1, source_target_pairs={{12,0},{16,4},{20,8},{24,12},{28,16},{13,1},{17,5},{21,9},{25,13},... | collective-permute-start | bytes 1572872 | tf_op jit(solution)/shard_map/ppermute | solution.py:21
  79.2 21.4 %collective-permute-start.8 = (f32[512,256]{1,0:T(8,128)}, f32[512,256]{1,0:T(8,128)S(1)}, u32[]{:S(2)}, u32[]{:S(2)}) collective-permute-start(f32[512,256]{1,0:T(8,128)} %get-tuple-element.96), channel_id=1, source_target_pairs={{16,0},{20,4},{24,8},{28,12},{17,1},{21,5},{25,9},{29,13},{18,2},{... | collective-permute-start | bytes 1572872 | tf_op jit(solution)/shard_map/ppermute | solution.py:21
  82.2 19.3 %copy-start.4 = (bf16[1,2,1,512,960]{3,4,2,1,0:T(8,128)(2,1)S(1)}, bf16[1,2,1,512,960]{3,4,2,1,0:T(8,128)(2,1)}, u32[]{:S(2)}) copy-start(bf16[1,2,1,512,960]{3,4,2,1,0:T(8,128)(2,1)} %param.15) | copy-start | bytes 5898244
  125.4 2.1 copy-start.2
  136.8 31.2 %collective-permute-start.16 = (f32[512,256]{0,1:T(8,128)}, f32[512,256]{0,1:T(8,128)S(1)}, u32[]{:S(2)}, u32[]{:S(2)}) collective-permute-start(f32[512,256]{0,1:T(8,128)} %get-tuple-element.88), channel_id=1, source_target_pairs={{0,16},{4,20},{8,24},{12,28},{1,17},{5,21},{9,25},{13,29},{2,18},{... | collective-permute-start | bytes 1572872 | tf_op jit(solution)/shard_map/ppermute | solution.py:21
  138.1 60.8 %collective-permute-start.15 = (f32[512,256]{0,1:T(8,128)}, f32[512,256]{0,1:T(8,128)S(1)}, u32[]{:S(2)}, u32[]{:S(2)}) collective-permute-start(f32[512,256]{0,1:T(8,128)} %get-tuple-element.89), channel_id=1, source_target_pairs={{0,12},{4,16},{8,20},{12,24},{16,28},{1,13},{5,17},{9,21},{13,25},... | collective-permute-start | bytes 1572872 | tf_op jit(solution)/shard_map/ppermute | solution.py:21
  139.4 60.8 %collective-permute-start.14 = (f32[512,256]{0,1:T(8,128)}, f32[512,256]{0,1:T(8,128)}, u32[]{:S(2)}, u32[]{:S(2)}) collective-permute-start(f32[512,256]{0,1:T(8,128)} %get-tuple-element.90), channel_id=1, source_target_pairs={{0,8},{4,12},{8,16},{12,20},{16,24},{20,28},{1,9},{5,13},{9,17},{1... | collective-permute-start | bytes 1572872 | tf_op jit(solution)/shard_map/ppermute | solution.py:21
  142.8 124.3 %reduce-scatter.5.cloned.1.call-start = ((), (), s32[]{:S(2)}) async-start(), calls=%async_computation.2 | async-start | bytes 655360 | tf_op jit(solution)/shard_map/reduce_scatter | solution.py:158
  142.8 63.7 %collective-permute-start.13 = (f32[512,256]{0,1:T(8,128)}, f32[512,256]{0,1:T(8,128)S(1)}, u32[]{:S(2)}, u32[]{:S(2)}) collective-permute-start(f32[512,256]{0,1:T(8,128)} %get-tuple-element.91), channel_id=1, source_target_pairs={{0,4},{4,8},{8,12},{12,16},{16,20},{20,24},{24,28},{1,5},{5,9},{9,... | collective-permute-start | bytes 1572872 | tf_op jit(solution)/shard_map/ppermute | solution.py:21
  164.3 42.3 %collective-permute-start.12 = (f32[512,256]{0,1:T(8,128)}, f32[512,256]{0,1:T(8,128)S(1)}, u32[]{:S(2)}, u32[]{:S(2)}) collective-permute-start(f32[512,256]{0,1:T(8,128)} %get-tuple-element.92), channel_id=1, source_target_pairs={{4,0},{8,4},{12,8},{16,12},{20,16},{24,20},{28,24},{5,1},{9,5},{13... | collective-permute-start | bytes 1572872 | tf_op jit(solution)/shard_map/ppermute | solution.py:21
  168.0 38.5 %collective-permute-start.11 = (f32[512,256]{0,1:T(8,128)}, f32[512,256]{0,1:T(8,128)S(1)}, u32[]{:S(2)}, u32[]{:S(2)}) collective-permute-start(f32[512,256]{0,1:T(8,128)} %get-tuple-element.93), channel_id=1, source_target_pairs={{8,0},{12,4},{16,8},{20,12},{24,16},{28,20},{9,1},{13,5},{17,9},{2... | collective-permute-start | bytes 1572872 | tf_op jit(solution)/shard_map/ppermute | solution.py:21
  198.8 12.1 %collective-permute-start.10 = (f32[512,256]{0,1:T(8,128)S(1)}, f32[512,256]{0,1:T(8,128)S(1)}, u32[]{:S(2)}, u32[]{:S(2)}) collective-permute-start(f32[512,256]{0,1:T(8,128)S(1)} %get-tuple-element.94), channel_id=1, source_target_pairs={{12,0},{16,4},{20,8},{24,12},{28,16},{13,1},{17,5},{21,9},{25,13},... | collective-permute-start | bytes 1572872 | tf_op jit(solution)/shard_map/ppermute | solution.py:21
  200.2 22.0 %collective-permute-start.9 = (f32[512,256]{0,1:T(8,128)S(1)}, f32[512,256]{0,1:T(8,128)S(1)}, u32[]{:S(2)}, u32[]{:S(2)}) collective-permute-start(f32[512,256]{0,1:T(8,128)S(1)} %get-tuple-element.87), channel_id=1, source_target_pairs={{16,0},{20,4},{24,8},{28,12},{17,1},{21,5},{25,9},{29,13},{18,2},{... | collective-permute-start | bytes 1572872 | tf_op jit(solution)/shard_map/ppermute | solution.py:21
  222.1 46.5 %copy-start.1 = (bf16[3,3,96,128]{3,2,1,0:T(8,128)(2,1)S(1)}, bf16[3,3,96,128]{3,2,1,0:T(8,128)(2,1)}, u32[]{:S(2)}) copy-start(bf16[3,3,96,128]{3,2,1,0:T(8,128)(2,1)} %param.11) | copy-start | bytes 663556
Sparse Core Ops, SparseCore 0:
  142.9 45.2 reduce-scatter.6
  224.9 42.1 reduce-scatter.4
where the time goes:
time: 278 us; the launch traced here: 276 us
  waiting for transfers between devices  142 us (51%)
  starting transfers between devices  53.8 us (19%)
  local copies, waits for them, and re-layouts  36 us (13%)
  other arithmetic  20.4 us (7%)
  between operations  15.7 us (6%)
  matrix products  7.98 us (3%)
    ppermute x17, waiting for transfers between devices, shifted(): return lax.ppermute(x, axis, pairs)  104 us
    ppermute x17, starting transfers between devices, shifted(): return lax.ppermute(x, axis, pairs)  53.7 us
    reduce_scatter x1, waiting for transfers between devices, shards(): lax.psum_scatter(received, 'band', scatter_dimension=1, tiled=True)  37.6 us
    unnamed x24, local copies, waits for them, and re-layouts  12.8 us
  transfers between devices with their start and end apart: 19, of which 10 were waited for; matrix products, arithmetic and copies ran while one was open for 6% of the time, Pallas kernels for 0%

commit v1 on v0

v1 whole, which is shorter than its diff:
```python
import math

import jax
import jax.numpy as jnp
import numpy as np
from jax import lax
from jax.experimental import pallas as pl
from jax.experimental.pallas import tpu as pltpu
from jax.sharding import PartitionSpec as P

LEVELS = 4
BAND_REACH = 4
F32 = jnp.float32
BF16 = jnp.bfloat16
VMEM_LIMIT = 56 * 1024 * 1024
NN = (((1,), (0,)), ((), ()))
NT = (((1,), (1,)), ((), ()))


def product(a, b, dims=NN):
    return lax.dot_general(a, b, dims, preferred_element_type=F32)


def halves(x):
    high = x.astype(BF16)
    return high, (x - high.astype(F32)).astype(BF16)


def spread_matrix(pixels):
    parts = []
    for level in range(LEVELS):
        group = 2**level
        parts.append(np.repeat(np.eye(pixels // group, dtype=np.float32), group, axis=0) / group)
    return np.concatenate(parts, axis=1).astype(jnp.bfloat16)


def convolve_row(rows, weight_ref, scratch):
    columns = rows[0].shape[0]
    mid = weight_ref.shape[3]
    total = None
    for dy in range(3):
        weight = jnp.concatenate([weight_ref[dy, dx] for dx in range(3)], axis=1)
        part = product(rows[dy], weight)
        total = part if total is None else total + part
    for dx in range(3):
        scratch[dx][8 : 8 + columns, :] = total[:, dx * mid : (dx + 1) * mid]
    out = sum(scratch[dx][pl.ds(7 + dx, columns // 2, stride=2), :] for dx in range(3))
    return jnp.maximum(out, 0.0)


def lower_rows_kernel(frames_ref, weight_ref, mid_ref, *scratch):
    scratch[0][0:8, :] = jnp.zeros((8, scratch[0].shape[1]), F32)
    for frame in range(2):
        rows = [frames_ref[frame, 1 + dy] for dy in range(3)]
        mid_ref[frame] = convolve_row(rows, weight_ref, scratch).astype(BF16)


def upper_rows_kernel(frames_ref, rim_ref, weight_ref, lower_ref, source_ref, source_t_ref, target_t_ref, *scratch):
    scratch[0][0:8, :] = jnp.zeros((8, scratch[0].shape[1]), F32)
    half = lower_ref.shape[1]
    for frame in range(2):
        rows = [rim_ref[frame, 0], frames_ref[frame, 0], frames_ref[frame, 1]]
        upper = convolve_row(rows, weight_ref, scratch)
        lower = lower_ref[frame]
        out_t = source_t_ref if frame == 0 else target_t_ref
        out_t[:, :half] = upper.T.astype(BF16)
        out_t[:, half:] = lower.astype(F32).T.astype(BF16)
        if frame == 0:
            source_ref[:half, :] = upper.astype(BF16)
            source_ref[half:, :] = lower


def encode(frames, rim, conv_weight):
    _, rows, columns, _ = frames.shape
    mid = conv_weight.shape[3]
    half = columns // 2
    scratch = [pltpu.VMEM((8 + columns + 8, mid), F32) for _ in range(3)]
    params = pltpu.CompilerParams(vmem_limit_bytes=VMEM_LIMIT)
    lower = pl.pallas_call(
        lower_rows_kernel,
        out_shape=jax.ShapeDtypeStruct((2, half, mid), BF16),
        scratch_shapes=scratch,
        compiler_params=params,
        cost_estimate=pl.CostEstimate(flops=2**29, bytes_accessed=2**20, transcendentals=0),
    )(frames, conv_weight)
    pixels = 2 * half
    return pl.pallas_call(
        upper_rows_kernel,
        out_shape=(
            jax.ShapeDtypeStruct((pixels, mid), BF16),
            jax.ShapeDtypeStruct((mid, pixels), BF16),
            jax.ShapeDtypeStruct((mid, pixels), BF16),
        ),
        scratch_shapes=scratch,
        compiler_params=params,
        cost_estimate=pl.CostEstimate(flops=2**29, bytes_accessed=2**20, transcendentals=0),
    )(frames, rim, conv_weight, lower)


def target_kernel(band, factor, count_ref, source_ref, source_t_ref, grad_ref, spread_ref, proj_ref, tile_ref, scaled_ref):
    slot = pl.program_id(0)
    active = slot * band + lax.axis_index("band") < count_ref[0]
    mid = source_ref.shape[1]

    @pl.when(slot == 0)
    def _():
        gram_high, gram_low = halves(product(proj_ref[...], proj_ref[...], NT))
        both = product(source_ref[...], jnp.concatenate([gram_high, gram_low], axis=1))
        high, low = halves((both[:, :mid] + both[:, mid:]) * factor)
        scaled_ref[:, :mid] = high
        scaled_ref[:, mid:] = low

    @pl.when(active)
    def _():
        high, low = halves(product(source_t_ref[...], grad_ref[0, 0, 0]))
        both = product(spread_ref[...], jnp.concatenate([high, low], axis=0), NT)
        tile_ref[0] = (both[:, :mid] + both[:, mid:]).astype(BF16)

    @pl.when(jnp.logical_not(active))
    def _():
        tile_ref[0] = jnp.zeros(tile_ref.shape[1:], BF16)


def pyramid_kernel(band, start_ref, count_ref, held_ref, other_ref, scaled_ref, grad_ref, spread_ref, pyramid_ref, sum_ref):
    slot = pl.program_id(0)
    active = slot * band + lax.axis_index("band") < count_ref[0]
    even = lax.rem(start_ref[0] + 2 * BAND_REACH, 2) == 0
    mid = held_ref.shape[1]

    @pl.when(slot == 0)
    def _():
        sum_ref[...] = jnp.zeros(sum_ref.shape, F32)

    @pl.when(active)
    def _():
        target = jnp.where(even, held_ref[0], other_ref[0])
        high, low = halves(product(target, spread_ref[...]))
        corr = product(scaled_ref[...], jnp.concatenate([high, high], axis=0))
        corr = corr + product(scaled_ref[:, :mid], low)
        pyramid_ref[0, 0, 0] = corr.astype(BF16)
        both = product(grad_ref[0, 0, 0], jnp.concatenate([high, low], axis=0), NT)
        sum_ref[...] += both[:, :mid] + both[:, mid:]

    @pl.when(jnp.logical_not(active))
    def _():
        pyramid_ref[0, 0, 0] = jnp.zeros(pyramid_ref.shape[3:], BF16)


def project_kernel(factor, sum_ref, own_ref, *refs):
    band = refs[-1].shape[0] + 1
    parts, weight_ref, kept_ref, sent_ref = refs[:-3], refs[-3], refs[-2], refs[-1]
    place = lax.axis_index("band")
    target = own_ref[...].astype(F32)
    for part in parts:
        target = target + part[...].astype(F32)
    high, low = halves(jnp.concatenate([sum_ref[...], target], axis=1))
    for k in range(band):
        weight = weight_ref[jnp.bitwise_xor(place, k)]
        out = (product(high, weight) + product(low, weight)) * factor
        if k == 0:
            kept_ref[...] = out
        else:
            sent_ref[k - 1] = out.astype(BF16)


def shards(frames, conv_weight, proj_weight, band_start, band_count, pyramid_grad):
    band = lax.axis_size("band")
    row_blocks = lax.axis_size("rows")
    place = lax.axis_index("band")
    channels = proj_weight.shape[1]
    mid = proj_weight.shape[0]
    share = channels // band
    factor = 1.0 / math.sqrt(channels)
    slots = pyramid_grad.shape[1]
    pixels, entries = pyramid_grad.shape[3:]
    columns = frames.shape[2] // 2
    params = pltpu.CompilerParams(vmem_limit_bytes=VMEM_LIMIT)
    smem = pl.BlockSpec(memory_space=pltpu.SMEM)
    spread = jnp.asarray(spread_matrix(pixels))

    offsets = ([], [])
    for reach in range(1, BAND_REACH + 1):
        offsets[reach % 2].extend([reach, -reach])

    def along_rows(x, step, sign):
        pairs = []
        for row in range(row_blocks):
            for p in range(band):
                to = row + sign * offsets[p % 2][step]
                if 0 <= to < row_blocks:
                    pairs.append((row * band + p, to * band + p))
        return lax.ppermute(x, ("rows", "band"), pairs)

    def across(x, k):
        return lax.ppermute(x, "band", [(p, p ^ k) for p in range(band)])

    parity = place % 2
    step_offsets = [jnp.where(parity == 0, offsets[0][i], offsets[1][i]) for i in range(len(offsets[0]))]
    start = band_start[0]
    swap = start % 2
    held_offsets = [start + j * band + (place - parity) + (parity + swap) % 2 for j in range(slots)]

    rim = lax.ppermute(frames[:, -1:], "rows", [(i, i + 1) for i in range(row_blocks - 1)])
    source, source_t, target_t = encode(frames, rim, conv_weight)

    arrived = [along_rows(target_t, i, -1) for i in range(len(step_offsets))]

    grad_spec = pl.BlockSpec((1, 1, 1, pixels, entries), lambda j: (0, j, 0, 0, 0))

    def whole(shape):
        return pl.BlockSpec(shape, lambda j: (0,) * len(shape))

    tiles, scaled = pl.pallas_call(
        lambda *refs: target_kernel(band, factor, *refs),
        grid=(slots,),
        in_specs=[smem, whole((pixels, mid)), whole((mid, pixels)), grad_spec, whole((pixels, entries)), whole((mid, channels))],
        out_specs=(pl.BlockSpec((1, pixels, mid), lambda j: (j, 0, 0)), whole((pixels, 2 * mid))),
        out_shape=(
            jax.ShapeDtypeStruct((slots, pixels, mid), BF16),
            jax.ShapeDtypeStruct((pixels, 2 * mid), BF16),
        ),
        compiler_params=params,
        cost_estimate=pl.CostEstimate(flops=2**30, bytes_accessed=2**22, transcendentals=0),
    )(band_count, source, source_t, pyramid_grad, spread, proj_weight)

    other_tiles = across(tiles, 1)
    moved = [jnp.where(swap == 0, tiles[j], other_tiles[j]) for j in range(slots)]

    def term(offset):
        out = jnp.zeros((pixels, mid), BF16)
        for j in range(slots):
            out = jnp.where(held_offsets[j] == offset, moved[j], out)
        return out

    own_term = term(0)
    received = [along_rows(term(step_offsets[i]), i, 1) for i in range(len(step_offsets))]

    def pick(offset):
        out = target_t
        for i in range(len(step_offsets)):
            out = jnp.where(offset == step_offsets[i], arrived[i], out)
        return out

    held = jnp.stack([pick(offset) for offset in held_offsets])
    other = across(held, 1)

    target_spec = pl.BlockSpec((1, mid, pixels), lambda j: (j, 0, 0))
    pyramid, source_sum = pl.pallas_call(
        lambda *refs: pyramid_kernel(band, *refs),
        grid=(slots,),
        in_specs=[smem, smem, target_spec, target_spec, whole((pixels, 2 * mid)), grad_spec, whole((pixels, entries))],
        out_specs=(grad_spec, whole((pixels, mid))),
        out_shape=(
            jax.ShapeDtypeStruct(pyramid_grad.shape, BF16),
            jax.ShapeDtypeStruct((pixels, mid), F32),
        ),
        compiler_params=params,
        cost_estimate=pl.CostEstimate(flops=2**31, bytes_accessed=2**22, transcendentals=0),
    )(band_start, band_count, held, other, scaled, pyramid_grad, spread)

    empty = jnp.zeros((mid, share), BF16)
    weights = jnp.stack(
        [
            jnp.block([[proj_weight[:, q * share : (q + 1) * share], empty], [empty, proj_weight[:, q * share : (q + 1) * share]]])
            for q in range(band)
        ]
    )
    kept, sent = pl.pallas_call(
        lambda *refs: project_kernel(factor, *refs),
        out_shape=(
            jax.ShapeDtypeStruct((pixels, 2 * share), F32),
            jax.ShapeDtypeStruct((band - 1, pixels, 2 * share), BF16),
        ),
        compiler_params=params,
        cost_estimate=pl.CostEstimate(flops=2**29, bytes_accessed=2**21, transcendentals=0),
    )(source_sum, own_term, *received, weights)
    total = kept
    for k in range(1, band):
        total = total + across(sent[k - 1], k).astype(F32)
    shape_out = (pixels // columns, columns, share)
    return (pyramid, total[:, :share].reshape(shape_out), total[:, share:].reshape(shape_out))


def solution(mesh):
    in_specs = (
        P(None, "rows", None, None),
        P(),
        P(),
        P("rows"),
        P("rows"),
        P("rows", None, "band", None, None),
    )
    out_specs = (
        P("rows", None, "band", None, None),
        P("rows", None, "band"),
        P("rows", None, "band"),
    )
    return jax.shard_map(shards, mesh=mesh, in_specs=in_specs, out_specs=out_specs, check_vma=False)
```

time: 278 us -> 79.4 us (0.29)
  the two profiles are of different devices: /device:TPU:25 before, /device:TPU:0 now
where the time goes in v1:
time: 79.4 us; the launch traced here: 79 us
  starting transfers between devices  34.1 us (43%)
  Pallas kernels  16.6 us (21%)
  waiting for transfers between devices  11.7 us (15%)
  local copies, waits for them, and re-layouts  11.4 us (14%)
  other arithmetic  2.8 us (4%)
  between operations  2.36 us (3%)
    ppermute x8, starting transfers between devices, along_rows(): return lax.ppermute(x, ('rows', 'band'), pairs)  26.8 us
    unnamed x33, local copies, waits for them, and re-layouts  10.2 us
    ppermute x8, waiting for transfers between devices, along_rows(): return lax.ppermute(x, ('rows', 'band'), pairs)  5.39 us
    ppermute x1, starting transfers between devices, shards(): lax.ppermute(frames[:, -1:], 'rows', [(i, i + 1) for i in range(row_block...  4.89 us
    pallas_call x1, Pallas kernels, shards(): pl.pallas_call(lambda *refs: pyramid_kernel(band, *refs), grid=(slots,),...  4.4 us
    ppermute x5, waiting for transfers between devices, across(): return lax.ppermute(x, 'band', [(p, p ^ k) for p in range(band)])  3.98 us
    pallas_call x1, Pallas kernels, shards(): pl.pallas_call(lambda *refs: target_kernel(band, factor, *refs), grid=(sl...  3.59 us
    pallas_call x1, Pallas kernels, encode(): pl.pallas_call(upper_rows_kernel, out_shape=(jax.ShapeDtypeStruct((pixels...  2.91 us
  transfers between devices with their start and end apart: 14, of which 5 were waited for; matrix products, arithmetic and copies ran while one was open for 10% of the time, Pallas kernels for 14%

profile of v1, /device:TPU:0, one launch (start us, length us, event | category | flops | bytes accessed | tf_op | source)
XLA Modules:
  0.0 79.0 jit_solution(7187775165874465240)
XLA Ops:
  0.6 0.0 copy-start.7
  0.6 0.0 copy-start.3
  0.7 1.6 %copy.12.frames_ref = bf16[2,4,512,96]{3,2,1,0:T(8,128)(2,1)S(1)} copy(bf16[2,4,512,96]{2,3,1,0:T(8,128)(2,1)} %param.7) | data formatting | bytes 1572864 | tf_op args[0]
  2.3 0.0 copy-start.2
  2.3 4.9 %collective-permute-start = (bf16[2,1,512,96]{3,2,1,0:T(8,128)(2,1)S(1)}, bf16[2,1,512,96]{3,2,1,0:T(8,128)(2,1)S(1)}, u32[]{:S(2)}, u32[]{:S(2)}) collective-permute-start(bf16[2,1,512,96]{3,2,1,0:T(8,128)(2,1)S(1)} %slice.64), channel_id=1, source_target_pairs={{0,4},{4,8},{8,12},{12,16},{16,20},{20,24},{24,28},{1,5},{5,9},{9,... | collective-permute-start | bytes 589832 | tf_op jit(solution)/shard_map/ppermute | solution.py:203
  7.2 0.0 copy-done.3
  7.2 0.1 fusion.16
  7.3 0.0 copy-done.7
  7.3 0.1 fusion.12
  7.4 0.0 copy-done.2
  7.4 0.0 copy-start.1
  7.5 2.9 %shard_map.94.lower_ref = bf16[2,256,128]{2,1,0:T(8,128)(2,1)} custom-call(bf16[2,4,512,96]{3,2,1,0:T(8,128)(2,1)} %copy-done.2, bf16[3,3,96,128]{3,2,1,0:T(8,128)(2,1)} %weight_ref.3), custom_call_target="tpu_custom_call" | custom-call | flops 536870912 | bytes 1048576 | tf_op jit(solution)/shard_map/pallas_call | solution.py:79
  10.3 0.1 fusion.8
  10.4 2.3 %collective-permute-done.rim_ref = bf16[2,1,512,96]{3,2,1,0:T(8,128)(2,1)S(1)} collective-permute-done((bf16[2,1,512,96]{3,2,1,0:T(8,128)(2,1)S(1)}, bf16[2,1,512,96]{3,2,1,0:T(8,128)(2,1)S(1)}, u32[]{:S(2)}, u32[]{:S(2)}) %collective-permute-start) | collective-permute-done | bytes 196640 | tf_op jit(solution)/shard_map/ppermute | solution.py:203
  12.7 0.7 copy-done.9
  13.4 2.9 %shard_map.95 = (bf16[512,128]{1,0:T(8,128)(2,1)}, bf16[128,512]{1,0:T(8,128)(2,1)}, bf16[128,512]{1,0:T(8,128)(2,1)}) custom-call(bf16[2,4,512,96]{3,2,1,0:T(8,128)(2,1)} %copy-done.2, bf16[2,1,512,96]{3,2,1,0:T(8,128)(2,1)} %copy-done.9, bf16[3,3,96,128]{3,2,1,0:T(8,128)(2,1)} %weight_ref.3, bf16[2,256,128]{2,1,0:T(8,128)(2,1)} %shard_map.94.lower_ref), custom_call_target="tpu_custom_call" | custom-call | flops 536870912 | bytes 1048576 | tf_op jit(solution)/shard_map/pallas_call | solution.py:87
  16.3 6.3 %collective-permute-start.1 = (bf16[128,512]{1,0:T(8,128)(2,1)}, bf16[128,512]{1,0:T(8,128)(2,1)S(1)}, u32[]{:S(2)}, u32[]{:S(2)}) collective-permute-start(bf16[128,512]{1,0:T(8,128)(2,1)} %get-tuple-element.12), channel_id=1, source_target_pairs={{0,16},{1,13},{2,18},{3,15},{4,20},{5,17},{6,22},{7,19},{8,24},{9,... | collective-permute-start | bytes 393224 | tf_op jit(solution)/shard_map/ppermute | solution.py:192
  22.7 1.3 %collective-permute-start.2 = (bf16[128,512]{1,0:T(8,128)(2,1)}, bf16[128,512]{1,0:T(8,128)(2,1)S(1)}, u32[]{:S(2)}, u32[]{:S(2)}) collective-permute-start(bf16[128,512]{1,0:T(8,128)(2,1)} %get-tuple-element.12), channel_id=1, source_target_pairs={{13,1},{15,3},{16,0},{17,5},{18,2},{19,7},{20,4},{21,9},{22,6},{23... | collective-permute-start | bytes 393224 | tf_op jit(solution)/shard_map/ppermute | solution.py:192
  24.0 3.5 %collective-permute-start.3 = (bf16[128,512]{1,0:T(8,128)(2,1)}, bf16[128,512]{1,0:T(8,128)(2,1)S(1)}, u32[]{:S(2)}, u32[]{:S(2)}) collective-permute-start(bf16[128,512]{1,0:T(8,128)(2,1)} %get-tuple-element.12), channel_id=1, source_target_pairs={{0,8},{1,5},{2,10},{3,7},{4,12},{5,9},{6,14},{7,11},{8,16},{9,13},... | collective-permute-start | bytes 393224 | tf_op jit(solution)/shard_map/ppermute | solution.py:192
  27.5 1.3 %collective-permute-start.4 = (bf16[128,512]{1,0:T(8,128)(2,1)}, bf16[128,512]{1,0:T(8,128)(2,1)S(1)}, u32[]{:S(2)}, u32[]{:S(2)}) collective-permute-start(bf16[128,512]{1,0:T(8,128)(2,1)} %get-tuple-element.12), channel_id=1, source_target_pairs={{5,1},{7,3},{8,0},{9,5},{10,2},{11,7},{12,4},{13,9},{14,6},{15,11}... | collective-permute-start | bytes 393224 | tf_op jit(solution)/shard_map/ppermute | solution.py:192
  28.8 0.8 pad_maximum_fusion.1.refs_6_
  30.9 0.0 copy-done.1
  30.9 2.4 %copy.13.refs_3_.refs_5_ = bf16[1,2,1,512,960]{4,3,2,1,0:T(8,128)(2,1)} copy(bf16[1,2,1,512,960]{3,4,2,1,0:T(8,128)(2,1)S(1)} %copy-done.1) | data formatting | bytes 3932160 | tf_op args[5]
  33.4 3.6 %shard_map.96 = (bf16[2,512,128]{2,1,0:T(8,128)(2,1)}, bf16[512,256]{1,0:T(8,128)(2,1)}) custom-call(s32[1]{0:T(128)S(6)} %copy.19.refs_0_.refs_1_, bf16[512,128]{1,0:T(8,128)(2,1)} %get-tuple-element.13.refs_1_, bf16[128,512]{1,0:T(8,128)(2,1)} %get-tuple-element.14.refs_2_, bf16[1,2,1,512,960]{4,3,2,1,0:T(8,128)(2,1)} %copy.13.refs_3_.refs_5_, ...), custom_call_target="tpu_custom_call" | custom-call | flops 1073741824 | bytes 4194304 | tf_op jit(solution)/shard_map/pallas_call | solution.py:213
  37.0 0.0 collective-permute-start.6
  37.0 0.0 collective-permute-done.1
  37.0 0.0 collective-permute-done.2
  37.0 0.0 collective-permute-done.3
  37.0 0.0 collective-permute-done.4
  37.0 0.0 copy-done.6
  37.1 0.0 copy-start.5
  37.1 0.6 collective-permute-start.5
  37.7 1.0 %collective-permute-done.6 = bf16[2,512,128]{2,1,0:T(8,128)(2,1)S(1)} collective-permute-done((bf16[2,512,128]{2,1,0:T(8,128)(2,1)}, bf16[2,512,128]{2,1,0:T(8,128)(2,1)S(1)}, u32[]{:S(2)}, u32[]{:S(2)}) %collective-permute-start.6) | collective-permute-done | bytes 262176 | tf_op jit(solution)/shard_map/ppermute | solution.py:195
  38.7 1.0 %select_bitcast_fusion = (bf16[512,128]{1,0:T(8,128)(2,1)S(1)}, bf16[1,512,128]{2,1,0:T(8,128)(2,1)S(1)}, bf16[1,512,128]{2,1,0:T(8,128)(2,1)S(1)}) fusion(pred[]{:T(512)S(6)} %eq.54, pred[]{:T(512)S(6)} %eq.58, bf16[2,512,128]{2,1,0:T(8,128)(2,1)S(1)} %collective-permute-done.6, bf16[2,512,128]{2,1,0:T(8,128)(2,1)} %get-tuple-element.18, pred[]{:T(512)S(6)} %eq.63), kind=kLoop, calls=%fused_computation.17 | loop fusion | flops 262144 | bytes 917507 | tf_op jit(solution)/shard_map/jit(_where)/select_n | solution.py:232
  39.7 0.7 select_bitcast_fusion.1
  40.4 5.0 %collective-permute-start.7 = (bf16[512,128]{1,0:T(8,128)(2,1)S(1)}, bf16[512,128]{1,0:T(8,128)(2,1)S(1)}, u32[]{:S(2)}, u32[]{:S(2)}) collective-permute-start(bf16[512,128]{1,0:T(8,128)(2,1)S(1)} %get-tuple-element.36), channel_id=1, source_target_pairs={{0,8},{1,5},{2,10},{3,7},{4,12},{5,9},{6,14},{7,11},{8,16},{9,13},... | collective-permute-start | bytes 393224 | tf_op jit(solution)/shard_map/ppermute | solution.py:192
  45.5 1.3 %collective-permute-start.8 = (bf16[512,128]{1,0:T(8,128)(2,1)S(1)}, bf16[512,128]{1,0:T(8,128)(2,1)S(1)}, u32[]{:S(2)}, u32[]{:S(2)}) collective-permute-start(bf16[512,128]{1,0:T(8,128)(2,1)S(1)} %get-tuple-element.35), channel_id=1, source_target_pairs={{5,1},{7,3},{8,0},{9,5},{10,2},{11,7},{12,4},{13,9},{14,6},{15,11}... | collective-permute-start | bytes 393224 | tf_op jit(solution)/shard_map/ppermute | solution.py:192
  46.8 6.7 %collective-permute-start.9 = (bf16[512,128]{1,0:T(8,128)(2,1)S(1)}, bf16[512,128]{1,0:T(8,128)(2,1)S(1)}, u32[]{:S(2)}, u32[]{:S(2)}) collective-permute-start(bf16[512,128]{1,0:T(8,128)(2,1)S(1)} %get-tuple-element.34), channel_id=1, source_target_pairs={{0,16},{1,13},{2,18},{3,15},{4,20},{5,17},{6,22},{7,19},{8,24},{9,... | collective-permute-start | bytes 393224 | tf_op jit(solution)/shard_map/ppermute | solution.py:192
  53.5 1.3 %collective-permute-start.10 = (bf16[512,128]{1,0:T(8,128)(2,1)S(1)}, bf16[512,128]{1,0:T(8,128)(2,1)S(1)}, u32[]{:S(2)}, u32[]{:S(2)}) collective-permute-start(bf16[512,128]{1,0:T(8,128)(2,1)S(1)} %get-tuple-element.24), channel_id=1, source_target_pairs={{13,1},{15,3},{16,0},{17,5},{18,2},{19,7},{20,4},{21,9},{22,6},{23... | collective-permute-start | bytes 393224 | tf_op jit(solution)/shard_map/ppermute | solution.py:192
  54.8 0.0 collective-permute-done.5.refs_3_
  54.8 0.7 copy-done.8
  55.5 4.4 %shard_map.97 = (bf16[1,2,1,512,960]{4,3,2,1,0:T(8,128)(2,1)}, f32[512,128]{1,0:T(8,128)}) custom-call(s32[1]{0:T(128)} %copy.18.refs_0_, s32[1]{0:T(128)S(6)} %copy.19.refs_0_.refs_1_, bf16[2,128,512]{2,1,0:T(8,128)(2,1)} %copy-done.5, bf16[2,128,512]{2,1,0:T(8,128)(2,1)} %copy-done.8, bf16[512,256]{1,0:T(8,128)(2,1)} %get-tuple-element.15.refs_4_, ...), custom_call_target="tpu_custom_call" | custom-call | flops 2147483648 | bytes 4194304 | tf_op jit(solution)/shard_map/pallas_call | solution.py:248
  59.9 0.0 collective-permute-done.7.refs_2_
  59.9 0.0 copy-start.10
  59.9 0.0 collective-permute-done.8.refs_3_
  60.0 0.0 collective-permute-done.9.refs_4_
  60.0 5.4 %collective-permute-done.10.refs_5_ = bf16[512,128]{1,0:T(8,128)(2,1)S(1)} collective-permute-done((bf16[512,128]{1,0:T(8,128)(2,1)S(1)}, bf16[512,128]{1,0:T(8,128)(2,1)S(1)}, u32[]{:S(2)}, u32[]{:S(2)}) %collective-permute-start.10) | collective-permute-done | bytes 131104 | tf_op jit(solution)/shard_map/ppermute | solution.py:192
  65.4 0.0 copy-done.11
  65.4 0.6 copy-done.13
  66.0 2.8 %shard_map.98 = (f32[512,128]{1,0:T(8,128)}, bf16[3,512,128]{2,1,0:T(8,128)(2,1)}) custom-call(f32[512,128]{1,0:T(8,128)} %get-tuple-element.17.refs_0_, bf16[512,128]{1,0:T(8,128)(2,1)} %get-tuple-element.37.refs_1_, bf16[512,128]{1,0:T(8,128)(2,1)} %copy-done.10, bf16[512,128]{1,0:T(8,128)(2,1)} %copy-done.11, bf16[512,128]{1,0:T(8,128)(2,1)} %copy-done.12, ...), custom_call_target="tpu_custom_call" | custom-call | flops 536870912 | bytes 2097152 | tf_op jit(solution)/shard_map/pallas_call | solution.py:268
  68.8 1.1 %slice_bitcast_fusion.2 = (bf16[512,128]{1,0:T(8,128)(2,1)S(1)}, bf16[512,128]{1,0:T(8,128)(2,1)S(1)}, bf16[512,128]{1,0:T(8,128)(2,1)S(1)}) fusion(bf16[3,512,128]{2,1,0:T(8,128)(2,1)} %get-tuple-element.20), kind=kLoop, calls=%fused_computation.16 | loop fusion | bytes 786432 | tf_op jit(solution)/shard_map/squeeze | solution.py:279
  69.8 0.1 collective-permute-start.13
  69.9 0.8 %collective-permute-start.12 = (bf16[512,128]{1,0:T(8,128)(2,1)S(1)}, bf16[512,128]{1,0:T(8,128)(2,1)S(1)}, u32[]{:S(2)}, u32[]{:S(2)}) collective-permute-start(bf16[512,128]{1,0:T(8,128)(2,1)S(1)} %get-tuple-element.31), channel_id=1, source_target_pairs={{0,2},{1,3},{2,0},{3,1},{4,6},{5,7},{6,4},{7,5},{8,10},{9,11},{10,... | collective-permute-start | bytes 393224 | tf_op jit(solution)/shard_map/ppermute | solution.py:195
  70.8 1.0 %collective-permute-start.11 = (bf16[512,128]{1,0:T(8,128)(2,1)S(1)}, bf16[512,128]{1,0:T(8,128)(2,1)S(1)}, u32[]{:S(2)}, u32[]{:S(2)}) collective-permute-start(bf16[512,128]{1,0:T(8,128)(2,1)S(1)} %get-tuple-element.29), channel_id=1, source_target_pairs={{0,1},{1,0},{2,3},{3,2},{4,5},{5,4},{6,7},{7,6},{8,9},{9,8},{10,11... | collective-permute-start | bytes 393224 | tf_op jit(solution)/shard_map/ppermute | solution.py:195
  71.8 0.0 copy-done
  71.8 2.5 %copy.15 = bf16[1,2,1,512,960]{3,4,2,1,0:T(8,128)(2,1)} copy(bf16[1,2,1,512,960]{4,3,2,1,0:T(8,128)(2,1)S(1)} %copy-done) | data formatting | bytes 3932160
  74.3 1.4 %collective-permute-done.13 = bf16[512,128]{1,0:T(8,128)(2,1)S(1)} collective-permute-done((bf16[512,128]{1,0:T(8,128)(2,1)S(1)}, bf16[512,128]{1,0:T(8,128)(2,1)S(1)}, u32[]{:S(2)}, u32[]{:S(2)}) %collective-permute-start.13) | collective-permute-done | bytes 131104 | tf_op jit(solution)/shard_map/ppermute | solution.py:195
  75.7 1.6 %collective-permute-done.12 = bf16[512,128]{1,0:T(8,128)(2,1)S(1)} collective-permute-done((bf16[512,128]{1,0:T(8,128)(2,1)S(1)}, bf16[512,128]{1,0:T(8,128)(2,1)S(1)}, u32[]{:S(2)}, u32[]{:S(2)}) %collective-permute-start.12) | collective-permute-done | bytes 131104 | tf_op jit(solution)/shard_map/ppermute | solution.py:195
  77.2 0.0 collective-permute-done.11
  77.2 0.0 copy-done.4
  77.2 0.1 convert_add_fusion
  77.3 0.1 fusion.15
  77.4 0.8 copy.16
  78.2 0.8 copy.17
  (15 shorter events, 0.1 us)
Async XLA Ops:
  0.6 6.7 %copy-start.7 = (pred[128]{0:T(512)(128)(4,1)S(1)}, pred[128]{0:T(512)(128)(4,1)}, u32[]{:S(2)}) copy-start(pred[128]{0:T(512)(128)(4,1)} %constant.47.clone.1) | copy-start | bytes 388
  0.6 6.6 %copy-start.3 = (bf16[128,256]{1,0:T(8,128)(2,1)S(1)}, bf16[128,256]{1,0:T(8,128)(2,1)}, u32[]{:S(2)}) copy-start(bf16[128,256]{1,0:T(8,128)(2,1)} %refs_5_.2) | copy-start | bytes 196612
  2.3 5.2 %copy-start.2 = (bf16[2,4,512,96]{3,2,1,0:T(8,128)(2,1)}, bf16[2,4,512,96]{3,2,1,0:T(8,128)(2,1)S(1)}, u32[]{:S(2)}) copy-start(bf16[2,4,512,96]{3,2,1,0:T(8,128)(2,1)S(1)} %copy.12.frames_ref) | copy-start | bytes 2359300
  2.3 10.4 %collective-permute-start = (bf16[2,1,512,96]{3,2,1,0:T(8,128)(2,1)S(1)}, bf16[2,1,512,96]{3,2,1,0:T(8,128)(2,1)S(1)}, u32[]{:S(2)}, u32[]{:S(2)}) collective-permute-start(bf16[2,1,512,96]{3,2,1,0:T(8,128)(2,1)S(1)} %slice.64), channel_id=1, source_target_pairs={{0,4},{4,8},{8,12},{12,16},{16,20},{20,24},{24,28},{1,5},{5,9},{9,... | collective-permute-start | bytes 589832 | tf_op jit(solution)/shard_map/ppermute | solution.py:203
  7.4 23.5 %copy-start.1 = (bf16[1,2,1,512,960]{3,4,2,1,0:T(8,128)(2,1)S(1)}, bf16[1,2,1,512,960]{3,4,2,1,0:T(8,128)(2,1)}, u32[]{:S(2)}) copy-start(bf16[1,2,1,512,960]{3,4,2,1,0:T(8,128)(2,1)} %param.12) | copy-start | bytes 5898244
  12.7 0.7 copy-start.9
  16.3 20.6 %collective-permute-start.1 = (bf16[128,512]{1,0:T(8,128)(2,1)}, bf16[128,512]{1,0:T(8,128)(2,1)S(1)}, u32[]{:S(2)}, u32[]{:S(2)}) collective-permute-start(bf16[128,512]{1,0:T(8,128)(2,1)} %get-tuple-element.12), channel_id=1, source_target_pairs={{0,16},{1,13},{2,18},{3,15},{4,20},{5,17},{6,22},{7,19},{8,24},{9,... | collective-permute-start | bytes 393224 | tf_op jit(solution)/shard_map/ppermute | solution.py:192
  22.7 14.3 %collective-permute-start.2 = (bf16[128,512]{1,0:T(8,128)(2,1)}, bf16[128,512]{1,0:T(8,128)(2,1)S(1)}, u32[]{:S(2)}, u32[]{:S(2)}) collective-permute-start(bf16[128,512]{1,0:T(8,128)(2,1)} %get-tuple-element.12), channel_id=1, source_target_pairs={{13,1},{15,3},{16,0},{17,5},{18,2},{19,7},{20,4},{21,9},{22,6},{23... | collective-permute-start | bytes 393224 | tf_op jit(solution)/shard_map/ppermute | solution.py:192
  24.0 13.0 %collective-permute-start.3 = (bf16[128,512]{1,0:T(8,128)(2,1)}, bf16[128,512]{1,0:T(8,128)(2,1)S(1)}, u32[]{:S(2)}, u32[]{:S(2)}) collective-permute-start(bf16[128,512]{1,0:T(8,128)(2,1)} %get-tuple-element.12), channel_id=1, source_target_pairs={{0,8},{1,5},{2,10},{3,7},{4,12},{5,9},{6,14},{7,11},{8,16},{9,13},... | collective-permute-start | bytes 393224 | tf_op jit(solution)/shard_map/ppermute | solution.py:192
  27.5 9.5 %collective-permute-start.4 = (bf16[128,512]{1,0:T(8,128)(2,1)}, bf16[128,512]{1,0:T(8,128)(2,1)S(1)}, u32[]{:S(2)}, u32[]{:S(2)}) collective-permute-start(bf16[128,512]{1,0:T(8,128)(2,1)} %get-tuple-element.12), channel_id=1, source_target_pairs={{5,1},{7,3},{8,0},{9,5},{10,2},{11,7},{12,4},{13,9},{14,6},{15,11}... | collective-permute-start | bytes 393224 | tf_op jit(solution)/shard_map/ppermute | solution.py:192
  33.4 3.6 %copy-start.6 = (bf16[128,512]{1,0:T(8,128)(2,1)S(1)}, bf16[128,512]{1,0:T(8,128)(2,1)}, u32[]{:S(2)}) copy-start(bf16[128,512]{1,0:T(8,128)(2,1)} %get-tuple-element.12) | copy-start | bytes 393220
  37.0 1.7 %collective-permute-start.6 = (bf16[2,512,128]{2,1,0:T(8,128)(2,1)}, bf16[2,512,128]{2,1,0:T(8,128)(2,1)S(1)}, u32[]{:S(2)}, u32[]{:S(2)}) collective-permute-start(bf16[2,512,128]{2,1,0:T(8,128)(2,1)} %get-tuple-element.18), channel_id=1, source_target_pairs={{0,1},{1,0},{2,3},{3,2},{4,5},{5,4},{6,7},{7,6},{8,9},{9,8},{10,11... | collective-permute-start | bytes 786440 | tf_op jit(solution)/shard_map/ppermute | solution.py:195
  37.1 17.7 %copy-start.5 = (bf16[2,128,512]{2,1,0:T(8,128)(2,1)}, bf16[2,128,512]{2,1,0:T(8,128)(2,1)S(1)}, u32[]{:S(2)}) copy-start(bf16[2,128,512]{2,1,0:T(8,128)(2,1)S(1)} %pad_maximum_fusion.refs_2_) | copy-start | bytes 786436
  37.1 17.7 %collective-permute-start.5 = (bf16[2,128,512]{2,1,0:T(8,128)(2,1)S(1)}, bf16[2,128,512]{2,1,0:T(8,128)(2,1)S(1)}, u32[]{:S(2)}, u32[]{:S(2)}) collective-permute-start(bf16[2,128,512]{2,1,0:T(8,128)(2,1)S(1)} %pad_maximum_fusion.refs_2_), channel_id=1, source_target_pairs={{0,1},{1,0},{2,3},{3,2},{4,5},{5,4},{6,7},{7,6},{8,9},{9,8},{10,11... | collective-permute-start | bytes 786440 | tf_op jit(solution)/shard_map/ppermute | solution.py:195
  40.4 19.5 %collective-permute-start.7 = (bf16[512,128]{1,0:T(8,128)(2,1)S(1)}, bf16[512,128]{1,0:T(8,128)(2,1)S(1)}, u32[]{:S(2)}, u32[]{:S(2)}) collective-permute-start(bf16[512,128]{1,0:T(8,128)(2,1)S(1)} %get-tuple-element.36), channel_id=1, source_target_pairs={{0,8},{1,5},{2,10},{3,7},{4,12},{5,9},{6,14},{7,11},{8,16},{9,13},... | collective-permute-start | bytes 393224 | tf_op jit(solution)/shard_map/ppermute | solution.py:192
  45.5 14.5 %collective-permute-start.8 = (bf16[512,128]{1,0:T(8,128)(2,1)S(1)}, bf16[512,128]{1,0:T(8,128)(2,1)S(1)}, u32[]{:S(2)}, u32[]{:S(2)}) collective-permute-start(bf16[512,128]{1,0:T(8,128)(2,1)S(1)} %get-tuple-element.35), channel_id=1, source_target_pairs={{5,1},{7,3},{8,0},{9,5},{10,2},{11,7},{12,4},{13,9},{14,6},{15,11}... | collective-permute-start | bytes 393224 | tf_op jit(solution)/shard_map/ppermute | solution.py:192
  46.8 13.2 %collective-permute-start.9 = (bf16[512,128]{1,0:T(8,128)(2,1)S(1)}, bf16[512,128]{1,0:T(8,128)(2,1)S(1)}, u32[]{:S(2)}, u32[]{:S(2)}) collective-permute-start(bf16[512,128]{1,0:T(8,128)(2,1)S(1)} %get-tuple-element.34), channel_id=1, source_target_pairs={{0,16},{1,13},{2,18},{3,15},{4,20},{5,17},{6,22},{7,19},{8,24},{9,... | collective-permute-start | bytes 393224 | tf_op jit(solution)/shard_map/ppermute | solution.py:192
  53.5 11.8 %collective-permute-start.10 = (bf16[512,128]{1,0:T(8,128)(2,1)S(1)}, bf16[512,128]{1,0:T(8,128)(2,1)S(1)}, u32[]{:S(2)}, u32[]{:S(2)}) collective-permute-start(bf16[512,128]{1,0:T(8,128)(2,1)S(1)} %get-tuple-element.24), channel_id=1, source_target_pairs={{13,1},{15,3},{16,0},{17,5},{18,2},{19,7},{20,4},{21,9},{22,6},{23... | collective-permute-start | bytes 393224 | tf_op jit(solution)/shard_map/ppermute | solution.py:192
  54.8 0.7 copy-start.8
  59.9 11.9 %copy-start = (bf16[1,2,1,512,960]{4,3,2,1,0:T(8,128)(2,1)S(1)}, bf16[1,2,1,512,960]{4,3,2,1,0:T(8,128)(2,1)}, u32[]{:S(2)}) copy-start(bf16[1,2,1,512,960]{4,3,2,1,0:T(8,128)(2,1)} %get-tuple-element.21) | copy-start | bytes 5898244
  59.9 5.4 %copy-start.10 = (bf16[512,128]{1,0:T(8,128)(2,1)}, bf16[512,128]{1,0:T(8,128)(2,1)S(1)}, u32[]{:S(2)}) copy-start(bf16[512,128]{1,0:T(8,128)(2,1)S(1)} %collective-permute-done.7.refs_2_) | copy-start | bytes 393220
  59.9 5.4 %copy-start.11 = (bf16[512,128]{1,0:T(8,128)(2,1)}, bf16[512,128]{1,0:T(8,128)(2,1)S(1)}, u32[]{:S(2)}) copy-start(bf16[512,128]{1,0:T(8,128)(2,1)S(1)} %collective-permute-done.8.refs_3_) | copy-start | bytes 393220
  60.0 5.4 %copy-start.12 = (bf16[512,128]{1,0:T(8,128)(2,1)}, bf16[512,128]{1,0:T(8,128)(2,1)S(1)}, u32[]{:S(2)}) copy-start(bf16[512,128]{1,0:T(8,128)(2,1)S(1)} %collective-permute-done.9.refs_4_) | copy-start | bytes 393220
  65.4 0.6 copy-start.13
  69.8 7.4 %copy-start.4 = (f32[512,128]{1,0:T(8,128)S(1)}, f32[512,128]{1,0:T(8,128)}, u32[]{:S(2)}) copy-start(f32[512,128]{1,0:T(8,128)} %get-tuple-element.19) | copy-start | bytes 786436
  69.8 5.8 %collective-permute-start.13 = (bf16[512,128]{1,0:T(8,128)(2,1)S(1)}, bf16[512,128]{1,0:T(8,128)(2,1)S(1)}, u32[]{:S(2)}, u32[]{:S(2)}) collective-permute-start(bf16[512,128]{1,0:T(8,128)(2,1)S(1)} %get-tuple-element.30), channel_id=1, source_target_pairs={{0,3},{1,2},{2,1},{3,0},{4,7},{5,6},{6,5},{7,4},{8,11},{9,10},{10,... | collective-permute-start | bytes 393224 | tf_op jit(solution)/shard_map/ppermute | solution.py:195
  69.9 7.3 %collective-permute-start.12 = (bf16[512,128]{1,0:T(8,128)(2,1)S(1)}, bf16[512,128]{1,0:T(8,128)(2,1)S(1)}, u32[]{:S(2)}, u32[]{:S(2)}) collective-permute-start(bf16[512,128]{1,0:T(8,128)(2,1)S(1)} %get-tuple-element.31), channel_id=1, source_target_pairs={{0,2},{1,3},{2,0},{3,1},{4,6},{5,7},{6,4},{7,5},{8,10},{9,11},{10,... | collective-permute-start | bytes 393224 | tf_op jit(solution)/shard_map/ppermute | solution.py:195
  70.8 6.5 %collective-permute-start.11 = (bf16[512,128]{1,0:T(8,128)(2,1)S(1)}, bf16[512,128]{1,0:T(8,128)(2,1)S(1)}, u32[]{:S(2)}, u32[]{:S(2)}) collective-permute-start(bf16[512,128]{1,0:T(8,128)(2,1)S(1)} %get-tuple-element.29), channel_id=1, source_target_pairs={{0,1},{1,0},{2,3},{3,2},{4,5},{5,4},{6,7},{7,6},{8,9},{9,8},{10,11... | collective-permute-start | bytes 393224 | tf_op jit(solution)/shard_map/ppermute | solution.py:195

commit v2 on v1

v2 whole, which is shorter than its diff:
```python
import math

import jax
import jax.numpy as jnp
import numpy as np
from jax import lax
from jax.experimental import pallas as pl
from jax.experimental.pallas import tpu as pltpu
from jax.sharding import PartitionSpec as P

LEVELS = 4
BAND_REACH = 4
F32 = jnp.float32
BF16 = jnp.bfloat16
VMEM_LIMIT = 28 * 1024 * 1024
NN = (((1,), (0,)), ((), ()))
NT = (((1,), (1,)), ((), ()))
TN = (((0,), (0,)), ((), ()))


def product(a, b, dims=NN):
    return lax.dot_general(a, b, dims, preferred_element_type=F32)


def halves(x):
    high = x.astype(BF16)
    return high, (x - high.astype(F32)).astype(BF16)


def spread_matrix(pixels):
    parts = []
    for level in range(LEVELS):
        group = 2**level
        parts.append(np.repeat(np.eye(pixels // group, dtype=np.float32), group, axis=1) / group)
    return np.concatenate(parts, axis=0).astype(jnp.bfloat16)


def column_picker(columns):
    half = columns // 2
    taps = [
        (
            lax.broadcasted_iota(jnp.int32, (columns, half), 0)
            == 2 * lax.broadcasted_iota(jnp.int32, (columns, half), 1) + (dx - 1)
        )
        for dx in range(3)
    ]
    return jnp.concatenate([jnp.where(tap, 1.0, 0.0).astype(BF16) for tap in taps], axis=1)


def gathered(picked, rows, half):
    return jnp.concatenate(
        [
            jnp.concatenate([picked(frame, row)[:, dx * half : (dx + 1) * half] for frame in range(2)], axis=1)
            for row in rows
            for dx in range(3)
        ],
        axis=0,
    )


def stacked_weight(weight_ref, taps):
    return jnp.concatenate([weight_ref[dy, dx] for dy in taps for dx in range(3)], axis=0)


def local_rows_kernel(frames_ref, weight_ref, proj_ref, lower_ref, partial_ref, picker_ref, gram_ref, pick_ref):
    _, rows, channels, columns = frames_ref.shape
    half = columns // 2
    mid = weight_ref.shape[3]
    picker_ref[...] = column_picker(columns)
    flat = frames_ref[...].reshape(2 * rows * channels, columns)
    pick_ref[...] = product(flat, picker_ref[...]).astype(BF16).reshape(pick_ref.shape)

    def picked(frame, row):
        return pick_ref[frame, row]

    lower = product(stacked_weight(weight_ref, range(3)), gathered(picked, (1, 2, 3), half), TN)
    lower_ref[...] = jnp.maximum(lower, 0.0).astype(BF16)
    partial_ref[...] = product(stacked_weight(weight_ref, (1, 2)), gathered(picked, (0, 1), half), TN)
    gram_high, gram_low = halves(product(proj_ref[...], proj_ref[...], NT))
    gram_ref[:mid, :] = gram_high
    gram_ref[mid:, :] = gram_low


def target_kernel(
    band, factor, count_ref, rim_ref, weight_ref, lower_ref, partial_ref, picker_ref, gram_ref, grad_ref, spread_ref,
    target_ref, tile_ref, scaled_ref
):
    half = lower_ref.shape[1] // 2
    mid = lower_ref.shape[0]
    channels = rim_ref.shape[2]
    pick = product(rim_ref[...].reshape(2 * channels, 2 * half), picker_ref[...]).astype(BF16)

    def picked(frame, row):
        return pick[frame * channels : (frame + 1) * channels]

    upper = product(stacked_weight(weight_ref, (0,)), gathered(picked, (0,), half), TN) + partial_ref[...]
    upper = jnp.maximum(upper, 0.0).astype(BF16)
    source = jnp.concatenate([upper[:, :half], lower_ref[:, :half]], axis=1)
    target_ref[:, :half] = upper[:, half:]
    target_ref[:, half:] = lower_ref[:, half:]
    both = product(gram_ref[...], source)
    high, low = halves((both[:mid] + both[mid:]) * factor)
    scaled_ref[:mid, :] = high
    scaled_ref[mid : 2 * mid, :] = low
    scaled_ref[2 * mid :, :] = high
    for slot in range(tile_ref.shape[0]):
        active = slot * band + lax.axis_index("band") < count_ref[0]

        @pl.when(active)
        def _():
            high, low = halves(product(source, grad_ref[0, slot, 0], NT))
            both = product(jnp.concatenate([high, low], axis=0), spread_ref[...])
            tile_ref[slot] = (both[:mid] + both[mid:]).astype(BF16)

        @pl.when(jnp.logical_not(active))
        def _():
            tile_ref[slot] = jnp.zeros(tile_ref.shape[1:], BF16)


def pyramid_kernel(
    band, factor, start_ref, count_ref, held_ref, other_ref, scaled_ref, grad_ref, spread_ref, proj_ref, own_ref, *refs
):
    parts, (pyramid_ref, kept_ref, sent_ref, sum_ref, out_ref) = refs[:-5], refs[-5:]
    slot = pl.program_id(0)
    place = lax.axis_index("band")
    active = slot * band + place < count_ref[0]
    even = lax.rem(start_ref[0] + 2 * BAND_REACH, 2) == 0
    mid, pixels = held_ref.shape[1:]

    @pl.when(slot == 0)
    def _():
        sum_ref[...] = jnp.zeros(sum_ref.shape, F32)

    @pl.when(active)
    def _():
        target = jnp.where(even, held_ref[0], other_ref[0])
        high, low = halves(product(spread_ref[...], target, NT))
        corr = product(jnp.concatenate([high, high, low], axis=1), scaled_ref[...])
        pyramid_ref[0, 0, 0] = corr.astype(BF16)
        high, low = halves(product(target, spread_ref[...], NT))
        both = product(jnp.concatenate([high, low], axis=0), grad_ref[0, 0, 0])
        sum_ref[...] += both[:mid] + both[mid:]

    @pl.when(jnp.logical_not(active))
    def _():
        pyramid_ref[0, 0, 0] = jnp.zeros(pyramid_ref.shape[3:], BF16)

    @pl.when(slot == pl.num_programs(0) - 1)
    def _():
        target = own_ref[...].astype(F32)
        for part in parts:
            target = target + part[1].astype(F32)
        high, low = halves(jnp.concatenate([sum_ref[...], target], axis=1))
        out_ref[...] = (product(proj_ref[...], high, TN) + product(proj_ref[...], low, TN)) * factor
        share, width = kept_ref.shape[1:]
        for k in range(band):
            first = pl.multiple_of(jnp.bitwise_xor(place, k) * share, share)
            for part in range(kept_ref.shape[0]):
                out = out_ref[pl.ds(first, share), part * width : (part + 1) * width]
                if k == 0:
                    kept_ref[part] = out
                else:
                    sent_ref[k - 1, part] = out.astype(BF16)


def shards(frames, conv_weight, proj_weight, band_start, band_count, pyramid_grad):
    band = lax.axis_size("band")
    row_blocks = lax.axis_size("rows")
    place = lax.axis_index("band")
    mid, channels = proj_weight.shape
    share = channels // band
    factor = 1.0 / math.sqrt(channels)
    frames = jnp.swapaxes(frames, 2, 3)
    grad = jnp.swapaxes(pyramid_grad, 3, 4)
    slots = grad.shape[1]
    entries, pixels = grad.shape[3:]
    columns = frames.shape[3]
    half = columns // 2
    params = pltpu.CompilerParams(vmem_limit_bytes=VMEM_LIMIT)
    smem = pl.BlockSpec(memory_space=pltpu.SMEM)
    vmem = pl.BlockSpec(memory_space=pltpu.VMEM)
    spread = jnp.asarray(spread_matrix(pixels))

    offsets = ([], [])
    for reach in range(1, BAND_REACH + 1):
        offsets[reach % 2].extend([reach, -reach])

    def along_rows(x, step):
        pairs = []
        for row in range(row_blocks):
            for p in range(band):
                to = row - offsets[p % 2][step]
                if 0 <= to < row_blocks:
                    pairs.append((row * band + p, to * band + p))
        return lax.ppermute(x, ("rows", "band"), pairs)

    def across(x, k):
        return lax.ppermute(x, "band", [(p, p ^ k) for p in range(band)])

    parity = place % 2
    step_offsets = [jnp.where(parity == 0, offsets[0][i], offsets[1][i]) for i in range(len(offsets[0]))]
    start = band_start[0]
    swap = start % 2
    held_offsets = [start + j * band + (place - parity) + (parity + swap) % 2 for j in range(slots)]

    rim = lax.ppermute(frames[:, -1:], "rows", [(i, i + 1) for i in range(row_blocks - 1)])
    lower, partial, picker, gram = pl.pallas_call(
        local_rows_kernel,
        out_shape=(
            jax.ShapeDtypeStruct((mid, columns), BF16),
            jax.ShapeDtypeStruct((mid, columns), F32),
            jax.ShapeDtypeStruct((columns, 3 * half), BF16),
            jax.ShapeDtypeStruct((2 * mid, mid), BF16),
        ),
        scratch_shapes=[pltpu.VMEM(frames.shape[:3] + (3 * half,), BF16)],
        compiler_params=params,
        cost_estimate=pl.CostEstimate(flops=2**31, bytes_accessed=2**21, transcendentals=0),
    )(frames, conv_weight, proj_weight)

    target, tiles, scaled = pl.pallas_call(
        lambda *refs: target_kernel(band, factor, *refs),
        in_specs=[smem] + [vmem] * 8,
        out_shape=(
            jax.ShapeDtypeStruct((mid, pixels), BF16),
            jax.ShapeDtypeStruct((slots, mid, pixels), BF16),
            jax.ShapeDtypeStruct((3 * mid, pixels), BF16),
        ),
        compiler_params=params,
        cost_estimate=pl.CostEstimate(flops=2**31, bytes_accessed=2**22, transcendentals=0),
    )(band_count, rim, conv_weight, lower, partial, picker, gram, grad, spread)

    other_tiles = across(tiles, 1)
    moved = [jnp.where(swap == 0, tiles[j], other_tiles[j]) for j in range(slots)]

    def term(offset):
        out = jnp.zeros((mid, pixels), BF16)
        for j in range(slots):
            out = jnp.where(held_offsets[j] == offset, moved[j], out)
        return out

    own_term = term(0)
    arrived = [
        along_rows(jnp.stack([target, term(-step_offsets[i])]), i) for i in range(len(step_offsets))
    ]

    def pick(offset):
        out = target
        for i in range(len(step_offsets)):
            out = jnp.where(offset == step_offsets[i], arrived[i][0], out)
        return out

    held = jnp.stack([pick(offset) for offset in held_offsets])
    other = across(held, 1)

    def whole(shape):
        return pl.BlockSpec(shape, lambda j: (0,) * len(shape))

    target_spec = pl.BlockSpec((1, mid, pixels), lambda j: (j, 0, 0))
    grad_spec = pl.BlockSpec((1, 1, 1, entries, pixels), lambda j: (0, j, 0, 0, 0))
    out_parts = 2 * pixels // half
    pyramid, kept, sent = pl.pallas_call(
        lambda *refs: pyramid_kernel(band, factor, *refs),
        grid=(slots,),
        in_specs=[smem, smem, target_spec, target_spec, whole((3 * mid, pixels)), grad_spec, whole((entries, pixels))]
        + [whole((mid, channels)), whole((mid, pixels))]
        + [whole((2, mid, pixels)) for _ in arrived],
        out_specs=(grad_spec, whole((out_parts, share, half)), whole((band - 1, out_parts, share, half))),
        out_shape=(
            jax.ShapeDtypeStruct(grad.shape, BF16),
            jax.ShapeDtypeStruct((out_parts, share, half), F32),
            jax.ShapeDtypeStruct((band - 1, out_parts, share, half), BF16),
        ),
        scratch_shapes=[pltpu.VMEM((mid, pixels), F32), pltpu.VMEM((channels, 2 * pixels), F32)],
        compiler_params=params,
        cost_estimate=pl.CostEstimate(flops=2**31, bytes_accessed=2**22, transcendentals=0),
    )(band_start, band_count, held, other, scaled, grad, spread, proj_weight, own_term, *arrived)

    total = kept
    for k in range(1, band):
        total = total + across(sent[k - 1], k).astype(F32)
    total = jnp.swapaxes(total, 1, 2)
    return (jnp.swapaxes(pyramid, 3, 4), total[: out_parts // 2], total[out_parts // 2 :])


def solution(mesh):
    in_specs = (
        P(None, "rows", None, None),
        P(),
        P(),
        P("rows"),
        P("rows"),
        P("rows", None, "band", None, None),
    )
    out_specs = (
        P("rows", None, "band", None, None),
        P("rows", None, "band"),
        P("rows", None, "band"),
    )
    return jax.shard_map(shards, mesh=mesh, in_specs=in_specs, out_specs=out_specs, check_vma=False)
```

time: 79.4 us -> 59.2 us (0.75)
  the two profiles are of different devices: /device:TPU:0 before, /device:TPU:25 now
where the time goes in v2:
time: 59.2 us; the launch traced here: 58.3 us
  waiting for transfers between devices  25.9 us (44%)
  starting transfers between devices  15.8 us (27%)
  local copies, waits for them, and re-layouts  6.82 us (12%)
  Pallas kernels  6.31 us (11%)
  between operations  2.18 us (4%)
  other arithmetic  1.29 us (2%)
    ppermute x4, waiting for transfers between devices, along_rows(): return lax.ppermute(x, ('rows', 'band'), pairs)  17 us
    ppermute x4, starting transfers between devices, along_rows(): return lax.ppermute(x, ('rows', 'band'), pairs)  9.08 us
    ppermute x5, waiting for transfers between devices, across(): return lax.ppermute(x, 'band', [(p, p ^ k) for p in range(band)])  8.5 us
    unnamed x20, local copies, waits for them, and re-layouts  5.13 us
    ppermute x5, starting transfers between devices, across(): return lax.ppermute(x, 'band', [(p, p ^ k) for p in range(band)])  3.6 us
    pallas_call x1, Pallas kernels, shards(): pl.pallas_call(lambda *refs: pyramid_kernel(band, factor, *refs), grid=(s...  3.45 us
    ppermute x1, starting transfers between devices, shards(): lax.ppermute(frames[:, -1:], 'rows', [(i, i + 1) for i in range(row_block...  3.15 us
    pallas_call x1, Pallas kernels, shards(): pl.pallas_call(lambda *refs: target_kernel(band, factor, *refs), in_specs...  1.44 us
  transfers between devices with their start and end apart: 10, of which 8 were waited for; matrix products, arithmetic and copies ran while one was open for 0% of the time, Pallas kernels for 2%

profile of v2, /device:TPU:25, one launch (start us, length us, event | category | flops | bytes accessed | tf_op | source)
XLA Modules:
  0.0 58.3 jit_solution(16878542561395633419)
XLA Ops:
  0.6 0.9 %slice.60 = bf16[2,1,96,512]{3,2,1,0:T(8,128)(2,1)S(1)} slice(bf16[2,4,96,512]{3,2,1,0:T(8,128)(2,1)} %bitcast.49), slice={[0:2], [3:4], [0:96], [0:512]} | slice | bytes 393216 | tf_op jit(solution)/shard_map/slice | solution.py:206
  1.6 3.1 %collective-permute-start = (bf16[2,1,96,512]{3,2,1,0:T(8,128)(2,1)S(1)}, bf16[2,1,96,512]{3,2,1,0:T(8,128)(2,1)S(1)}, u32[]{:S(2)}, u32[]{:S(2)}) collective-permute-start(bf16[2,1,96,512]{3,2,1,0:T(8,128)(2,1)S(1)} %slice.60), channel_id=1, source_target_pairs={{0,4},{4,8},{8,12},{12,16},{16,20},{20,24},{24,28},{1,5},{5,9},{9,... | collective-permute-start | bytes 589832 | tf_op jit(solution)/shard_map/ppermute | solution.py:206
  5.4 0.0 copy-start
  5.4 1.1 %copy-done = bf16[2,4,512,96]{2,3,1,0:T(8,128)(2,1)S(1)} copy-done((bf16[2,4,512,96]{2,3,1,0:T(8,128)(2,1)S(1)}, bf16[2,4,512,96]{2,3,1,0:T(8,128)(2,1)}, u32[]{:S(2)}) %copy-start) | copy-done | bytes 786456
  6.5 0.0 copy-start.2
  6.5 0.9 %copy-done.2 = bf16[3,3,96,128]{3,2,1,0:T(8,128)(2,1)S(1)} copy-done((bf16[3,3,96,128]{3,2,1,0:T(8,128)(2,1)S(1)}, bf16[3,3,96,128]{3,2,1,0:T(8,128)(2,1)}, u32[]{:S(2)}) %copy-start.2) | copy-done | bytes 221208
  7.5 0.0 copy-start.4
  7.5 0.8 %copy-done.4 = bf16[128,256]{1,0:T(8,128)(2,1)S(1)} copy-done((bf16[128,256]{1,0:T(8,128)(2,1)S(1)}, bf16[128,256]{1,0:T(8,128)(2,1)}, u32[]{:S(2)}) %copy-start.4) | copy-done | bytes 65560
  8.3 0.0 copy-start.1
  8.3 0.0 copy-start.3
  8.3 0.0 copy-start.6
  8.3 1.4 %shard_map.94 = (bf16[128,512]{1,0:T(8,128)(2,1)S(1)}, f32[128,512]{1,0:T(8,128)S(1)}, bf16[512,768]{1,0:T(8,128)(2,1)S(1)}, bf16[256,128]{1,0:T(8,128)(2,1)S(1)}) custom-call(bf16[2,4,96,512]{3,2,1,0:T(8,128)(2,1)S(1)} %bitcast.50, bf16[3,3,96,128]{3,2,1,0:T(8,128)(2,1)S(1)} %copy-done.2, bf16[128,256]{1,0:T(8,128)(2,1)S(1)} %copy-done.4), custom_call_target="tpu_custom_call" | custom-call | flops 2147483648 | bytes 2097152 | tf_op jit(solution)/shard_map/pallas_call | solution.py:207
  9.7 0.4 collective-permute-done.refs_1_
  10.1 0.0 copy-done.1
  10.1 0.0 copy-done.3
  10.1 0.0 copy-done.6
  10.2 1.4 %shard_map.95 = (bf16[128,512]{1,0:T(8,128)(2,1)S(1)}, bf16[2,128,512]{2,1,0:T(8,128)(2,1)S(1)}, bf16[384,512]{1,0:T(8,128)(2,1)S(1)}) custom-call(s32[1]{0:T(128)S(6)} %copy.11.refs_0_.refs_1_, bf16[2,1,96,512]{3,2,1,0:T(8,128)(2,1)S(1)} %collective-permute-done.refs_1_, bf16[3,3,96,128]{3,2,1,0:T(8,128)(2,1)S(1)} %copy-done.3, ...), custom_call_target="tpu_custom_call" | custom-call | flops 2147483648 | bytes 4194304 | tf_op jit(solution)/shard_map/pallas_call | solution.py:220
  11.6 0.0 copy-start.8
  11.6 1.6 %collective-permute-start.1 = (bf16[2,128,512]{2,1,0:T(8,128)(2,1)S(1)}, bf16[2,128,512]{2,1,0:T(8,128)(2,1)S(1)}, u32[]{:S(2)}, u32[]{:S(2)}) collective-permute-start(bf16[2,128,512]{2,1,0:T(8,128)(2,1)S(1)} %get-tuple-element.18), channel_id=1, source_target_pairs={{0,1},{1,0},{2,3},{3,2},{4,5},{5,4},{6,7},{7,6},{8,9},{9,8},{10,11... | collective-permute-start | bytes 786440 | tf_op jit(solution)/shard_map/ppermute | solution.py:198
  13.9 0.4 collective-permute-done.1
  14.4 0.0 copy-start.5
  14.4 0.1 select_select_fusion
  14.5 1.1 %pad_maximum_fusion = (bf16[2,128,512]{2,1,0:T(8,128)(2,1)}, bf16[2,128,512]{2,1,0:T(8,128)(2,1)}, bf16[2,128,512]{2,1,0:T(8,128)(2,1)}, bf16[2,128,512]{2,1,0:T(8,128)(2,1)}) fusion(bf16[1,128,512]{2,1,0:T(8,128)(2,1)S(1)} %bitcast.48, bf16[1,128,512]{2,1,0:T(8,128)(2,1)S(1)} %get-tuple-element.33, bf16[1,128,512]{2,1,0:T(8,128)(2,1)S(1)} %get-tuple-element.35, ...), kind=kLoop, calls=%fused_computation | loop fusion | flops 524288 | bytes 1703936 | tf_op jit(solution)/shard_map/stack | solution.py:243
  15.6 2.4 %collective-permute-start.5 = (bf16[2,128,512]{2,1,0:T(8,128)(2,1)}, bf16[2,128,512]{2,1,0:T(8,128)(2,1)S(1)}, u32[]{:S(2)}, u32[]{:S(2)}) collective-permute-start(bf16[2,128,512]{2,1,0:T(8,128)(2,1)} %get-tuple-element.37), channel_id=1, source_target_pairs={{5,1},{7,3},{8,0},{9,5},{10,2},{11,7},{12,4},{13,9},{14,6},{15,11}... | collective-permute-start | bytes 786440 | tf_op jit(solution)/shard_map/ppermute | solution.py:195
  18.0 0.0 copy-done.8
  18.0 3.3 %collective-permute-start.3 = (bf16[2,128,512]{2,1,0:T(8,128)(2,1)}, bf16[2,128,512]{2,1,0:T(8,128)(2,1)S(1)}, u32[]{:S(2)}, u32[]{:S(2)}) collective-permute-start(bf16[2,128,512]{2,1,0:T(8,128)(2,1)} %get-tuple-element.38), channel_id=1, source_target_pairs={{13,1},{15,3},{16,0},{17,5},{18,2},{19,7},{20,4},{21,9},{22,6},{23... | collective-permute-start | bytes 786440 | tf_op jit(solution)/shard_map/ppermute | solution.py:195
  21.3 2.0 %collective-permute-start.4 = (bf16[2,128,512]{2,1,0:T(8,128)(2,1)}, bf16[2,128,512]{2,1,0:T(8,128)(2,1)S(1)}, u32[]{:S(2)}, u32[]{:S(2)}) collective-permute-start(bf16[2,128,512]{2,1,0:T(8,128)(2,1)} %get-tuple-element.39), channel_id=1, source_target_pairs={{0,8},{1,5},{2,10},{3,7},{4,12},{5,9},{6,14},{7,11},{8,16},{9,13},... | collective-permute-start | bytes 786440 | tf_op jit(solution)/shard_map/ppermute | solution.py:195
  23.4 1.3 %collective-permute-start.2 = (bf16[2,128,512]{2,1,0:T(8,128)(2,1)}, bf16[2,128,512]{2,1,0:T(8,128)(2,1)S(1)}, u32[]{:S(2)}, u32[]{:S(2)}) collective-permute-start(bf16[2,128,512]{2,1,0:T(8,128)(2,1)} %get-tuple-element.40), channel_id=1, source_target_pairs={{0,16},{1,13},{2,18},{3,15},{4,20},{5,17},{6,22},{7,19},{8,24},{9,... | collective-permute-start | bytes 786440 | tf_op jit(solution)/shard_map/ppermute | solution.py:195
  24.7 0.0 collective-permute-done.5.refs_9_
  24.7 4.2 %collective-permute-done.3.refs_11_ = bf16[2,128,512]{2,1,0:T(8,128)(2,1)S(1)} collective-permute-done((bf16[2,128,512]{2,1,0:T(8,128)(2,1)}, bf16[2,128,512]{2,1,0:T(8,128)(2,1)S(1)}, u32[]{:S(2)}, u32[]{:S(2)}) %collective-permute-start.3) | collective-permute-done | bytes 262176 | tf_op jit(solution)/shard_map/ppermute | solution.py:195
  28.9 3.1 %collective-permute-done.4.refs_10_ = bf16[2,128,512]{2,1,0:T(8,128)(2,1)S(1)} collective-permute-done((bf16[2,128,512]{2,1,0:T(8,128)(2,1)}, bf16[2,128,512]{2,1,0:T(8,128)(2,1)S(1)}, u32[]{:S(2)}, u32[]{:S(2)}) %collective-permute-start.4) | collective-permute-done | bytes 262176 | tf_op jit(solution)/shard_map/ppermute | solution.py:195
  32.0 9.6 %collective-permute-done.2.refs_12_ = bf16[2,128,512]{2,1,0:T(8,128)(2,1)S(1)} collective-permute-done((bf16[2,128,512]{2,1,0:T(8,128)(2,1)}, bf16[2,128,512]{2,1,0:T(8,128)(2,1)S(1)}, u32[]{:S(2)}, u32[]{:S(2)}) %collective-permute-start.2) | collective-permute-done | bytes 262176 | tf_op jit(solution)/shard_map/ppermute | solution.py:195
  41.8 0.1 collective-permute-start.6
  41.8 1.5 %collective-permute-done.6.refs_3_ = bf16[2,128,512]{2,1,0:T(8,128)(2,1)S(1)} collective-permute-done((bf16[2,128,512]{2,1,0:T(8,128)(2,1)S(1)}, bf16[2,128,512]{2,1,0:T(8,128)(2,1)S(1)}, u32[]{:S(2)}, u32[]{:S(2)}) %collective-permute-start.6) | collective-permute-done | bytes 262176 | tf_op jit(solution)/shard_map/ppermute | solution.py:198
  43.4 0.0 copy-done.5
  43.4 0.0 copy-start.7
  43.4 1.2 %copy-done.7 = bf16[960,512]{1,0:T(8,128)(2,1)S(1)} copy-done((bf16[960,512]{1,0:T(8,128)(2,1)S(1)}, bf16[960,512]{1,0:T(8,128)(2,1)}, u32[]{:S(2)}) %copy-start.7) | copy-done | bytes 983064
  44.6 0.0 copy-start.9
  44.6 1.0 %copy-done.9 = bf16[384,512]{1,0:T(8,128)(2,1)S(1)} copy-done((bf16[384,512]{1,0:T(8,128)(2,1)S(1)}, bf16[384,512]{1,0:T(8,128)(2,1)}, u32[]{:S(2)}) %copy-start.9) | copy-done | bytes 393240
  45.6 3.5 %shard_map.96 = (bf16[1,2,1,960,512]{4,3,2,1,0:T(8,128)(2,1)}, f32[4,64,256]{2,1,0:T(8,128)S(1)}, bf16[3,4,64,256]{3,2,1,0:T(8,128)(2,1)S(1)}) custom-call(s32[1]{0:T(128)} %copy.10.refs_0_, s32[1]{0:T(128)S(6)} %copy.11.refs_0_.refs_1_, bf16[2,128,512]{2,1,0:T(8,128)(2,1)S(1)} %pad_maximum_fusion.4.refs_2_, ...), custom_call_target="tpu_custom_call" | custom-call | flops 2147483648 | bytes 4194304 | tf_op jit(solution)/shard_map/pallas_call | solution.py:261
  49.1 0.2 collective-permute-start.7
  49.3 1.4 %collective-permute-start.9 = (bf16[4,64,256]{2,1,0:T(8,128)(2,1)S(1)}, bf16[4,64,256]{2,1,0:T(8,128)(2,1)S(1)}, u32[]{:S(2)}, u32[]{:S(2)}) collective-permute-start(bf16[4,64,256]{2,1,0:T(8,128)(2,1)S(1)} %get-tuple-element.29), channel_id=1, source_target_pairs={{0,3},{1,2},{2,1},{3,0},{4,7},{5,6},{6,5},{7,4},{8,11},{9,10},{10,... | collective-permute-start | bytes 393224 | tf_op jit(solution)/shard_map/ppermute | solution.py:198
  50.6 0.3 collective-permute-start.8
  51.0 0.0 collective-permute-done.7
  51.0 4.1 %collective-permute-done.9 = bf16[4,64,256]{2,1,0:T(8,128)(2,1)S(1)} collective-permute-done((bf16[4,64,256]{2,1,0:T(8,128)(2,1)S(1)}, bf16[4,64,256]{2,1,0:T(8,128)(2,1)S(1)}, u32[]{:S(2)}, u32[]{:S(2)}) %collective-permute-start.9) | collective-permute-done | bytes 131104 | tf_op jit(solution)/shard_map/ppermute | solution.py:198
  55.1 2.5 %collective-permute-done.8 = bf16[4,64,256]{2,1,0:T(8,128)(2,1)S(1)} collective-permute-done((bf16[4,64,256]{2,1,0:T(8,128)(2,1)S(1)}, bf16[4,64,256]{2,1,0:T(8,128)(2,1)S(1)}, u32[]{:S(2)}, u32[]{:S(2)}) %collective-permute-start.8) | collective-permute-done | bytes 131104 | tf_op jit(solution)/shard_map/ppermute | solution.py:198
  57.5 0.1 add_bitcast_fusion
  57.6 0.7 %fusion = (f32[2,256,64]{1,2,0:T(8,128)}, f32[2,256,64]{1,2,0:T(8,128)}) fusion(f32[4,256,64]{1,2,0:T(8,128)S(1)} %add_bitcast_fusion), kind=kLoop, calls=%fused_computation.22 | loop fusion | bytes 524288 | tf_op jit(solution)/shard_map/slice | solution.py:282
  (4 shorter events, 0.1 us)
Async XLA Ops:
  1.6 8.6 %collective-permute-start = (bf16[2,1,96,512]{3,2,1,0:T(8,128)(2,1)S(1)}, bf16[2,1,96,512]{3,2,1,0:T(8,128)(2,1)S(1)}, u32[]{:S(2)}, u32[]{:S(2)}) collective-permute-start(bf16[2,1,96,512]{3,2,1,0:T(8,128)(2,1)S(1)} %slice.60), channel_id=1, source_target_pairs={{0,4},{4,8},{8,12},{12,16},{16,20},{20,24},{24,28},{1,5},{5,9},{9,... | collective-permute-start | bytes 589832 | tf_op jit(solution)/shard_map/ppermute | solution.py:206
  5.4 1.1 %copy-start = (bf16[2,4,512,96]{2,3,1,0:T(8,128)(2,1)S(1)}, bf16[2,4,512,96]{2,3,1,0:T(8,128)(2,1)}, u32[]{:S(2)}) copy-start(bf16[2,4,512,96]{2,3,1,0:T(8,128)(2,1)} %param.7) | copy-start | bytes 2359300
  6.5 0.9 %copy-start.2 = (bf16[3,3,96,128]{3,2,1,0:T(8,128)(2,1)S(1)}, bf16[3,3,96,128]{3,2,1,0:T(8,128)(2,1)}, u32[]{:S(2)}) copy-start(bf16[3,3,96,128]{3,2,1,0:T(8,128)(2,1)} %refs_2_.1) | copy-start | bytes 663556
  7.5 0.8 %copy-start.4 = (bf16[128,256]{1,0:T(8,128)(2,1)S(1)}, bf16[128,256]{1,0:T(8,128)(2,1)}, u32[]{:S(2)}) copy-start(bf16[128,256]{1,0:T(8,128)(2,1)} %refs_7_.1) | copy-start | bytes 196612
  8.3 1.8 %copy-start.1 = (bf16[1,2,1,512,960]{3,4,2,1,0:T(8,128)(2,1)S(1)}, bf16[1,2,1,512,960]{3,4,2,1,0:T(8,128)(2,1)}, u32[]{:S(2)}) copy-start(bf16[1,2,1,512,960]{3,4,2,1,0:T(8,128)(2,1)} %param.12) | copy-start | bytes 5898244
  8.3 1.8 %copy-start.3 = (bf16[3,3,96,128]{3,2,1,0:T(8,128)(2,1)S(1)}, bf16[3,3,96,128]{3,2,1,0:T(8,128)(2,1)}, u32[]{:S(2)}) copy-start(bf16[3,3,96,128]{3,2,1,0:T(8,128)(2,1)} %refs_2_.1) | copy-start | bytes 663556
  8.3 1.9 %copy-start.6 = (bf16[960,512]{1,0:T(8,128)(2,1)S(1)}, bf16[960,512]{1,0:T(8,128)(2,1)}, u32[]{:S(2)}) copy-start(bf16[960,512]{1,0:T(8,128)(2,1)} %constant.45.clone.refs_8_.refs_6_) | copy-start | bytes 2949124
  11.6 6.4 %copy-start.8 = (bf16[384,512]{1,0:T(8,128)(2,1)}, bf16[384,512]{1,0:T(8,128)(2,1)S(1)}, u32[]{:S(2)}) copy-start(bf16[384,512]{1,0:T(8,128)(2,1)S(1)} %get-tuple-element.19.refs_4_) | copy-start | bytes 1179652
  11.6 2.8 %collective-permute-start.1 = (bf16[2,128,512]{2,1,0:T(8,128)(2,1)S(1)}, bf16[2,128,512]{2,1,0:T(8,128)(2,1)S(1)}, u32[]{:S(2)}, u32[]{:S(2)}) collective-permute-start(bf16[2,128,512]{2,1,0:T(8,128)(2,1)S(1)} %get-tuple-element.18), channel_id=1, source_target_pairs={{0,1},{1,0},{2,3},{3,2},{4,5},{5,4},{6,7},{7,6},{8,9},{9,8},{10,11... | collective-permute-start | bytes 786440 | tf_op jit(solution)/shard_map/ppermute | solution.py:198
  14.4 29.0 %copy-start.5 = (bf16[128,256]{1,0:T(8,128)(2,1)S(1)}, bf16[128,256]{1,0:T(8,128)(2,1)}, u32[]{:S(2)}) copy-start(bf16[128,256]{1,0:T(8,128)(2,1)} %refs_7_.1) | copy-start | bytes 196612
  15.6 9.2 %collective-permute-start.5 = (bf16[2,128,512]{2,1,0:T(8,128)(2,1)}, bf16[2,128,512]{2,1,0:T(8,128)(2,1)S(1)}, u32[]{:S(2)}, u32[]{:S(2)}) collective-permute-start(bf16[2,128,512]{2,1,0:T(8,128)(2,1)} %get-tuple-element.37), channel_id=1, source_target_pairs={{5,1},{7,3},{8,0},{9,5},{10,2},{11,7},{12,4},{13,9},{14,6},{15,11}... | collective-permute-start | bytes 786440 | tf_op jit(solution)/shard_map/ppermute | solution.py:195
  18.0 10.9 %collective-permute-start.3 = (bf16[2,128,512]{2,1,0:T(8,128)(2,1)}, bf16[2,128,512]{2,1,0:T(8,128)(2,1)S(1)}, u32[]{:S(2)}, u32[]{:S(2)}) collective-permute-start(bf16[2,128,512]{2,1,0:T(8,128)(2,1)} %get-tuple-element.38), channel_id=1, source_target_pairs={{13,1},{15,3},{16,0},{17,5},{18,2},{19,7},{20,4},{21,9},{22,6},{23... | collective-permute-start | bytes 786440 | tf_op jit(solution)/shard_map/ppermute | solution.py:195
  21.3 10.7 %collective-permute-start.4 = (bf16[2,128,512]{2,1,0:T(8,128)(2,1)}, bf16[2,128,512]{2,1,0:T(8,128)(2,1)S(1)}, u32[]{:S(2)}, u32[]{:S(2)}) collective-permute-start(bf16[2,128,512]{2,1,0:T(8,128)(2,1)} %get-tuple-element.39), channel_id=1, source_target_pairs={{0,8},{1,5},{2,10},{3,7},{4,12},{5,9},{6,14},{7,11},{8,16},{9,13},... | collective-permute-start | bytes 786440 | tf_op jit(solution)/shard_map/ppermute | solution.py:195
  23.4 18.3 %collective-permute-start.2 = (bf16[2,128,512]{2,1,0:T(8,128)(2,1)}, bf16[2,128,512]{2,1,0:T(8,128)(2,1)S(1)}, u32[]{:S(2)}, u32[]{:S(2)}) collective-permute-start(bf16[2,128,512]{2,1,0:T(8,128)(2,1)} %get-tuple-element.40), channel_id=1, source_target_pairs={{0,16},{1,13},{2,18},{3,15},{4,20},{5,17},{6,22},{7,19},{8,24},{9,... | collective-permute-start | bytes 786440 | tf_op jit(solution)/shard_map/ppermute | solution.py:195
  41.8 1.6 %collective-permute-start.6 = (bf16[2,128,512]{2,1,0:T(8,128)(2,1)S(1)}, bf16[2,128,512]{2,1,0:T(8,128)(2,1)S(1)}, u32[]{:S(2)}, u32[]{:S(2)}) collective-permute-start(bf16[2,128,512]{2,1,0:T(8,128)(2,1)S(1)} %pad_maximum_fusion.4.refs_2_), channel_id=1, source_target_pairs={{0,1},{1,0},{2,3},{3,2},{4,5},{5,4},{6,7},{7,6},{8,9},{9,8},{10,11... | collective-permute-start | bytes 786440 | tf_op jit(solution)/shard_map/ppermute | solution.py:198
  43.4 1.2 %copy-start.7 = (bf16[960,512]{1,0:T(8,128)(2,1)S(1)}, bf16[960,512]{1,0:T(8,128)(2,1)}, u32[]{:S(2)}) copy-start(bf16[960,512]{1,0:T(8,128)(2,1)} %constant.45.clone.refs_8_.refs_6_) | copy-start | bytes 2949124
  44.6 1.0 %copy-start.9 = (bf16[384,512]{1,0:T(8,128)(2,1)S(1)}, bf16[384,512]{1,0:T(8,128)(2,1)}, u32[]{:S(2)}) copy-start(bf16[384,512]{1,0:T(8,128)(2,1)} %copy-done.8) | copy-start | bytes 1179652
  49.1 1.9 %collective-permute-start.7 = (bf16[4,64,256]{2,1,0:T(8,128)(2,1)S(1)}, bf16[4,64,256]{2,1,0:T(8,128)(2,1)S(1)}, u32[]{:S(2)}, u32[]{:S(2)}) collective-permute-start(bf16[4,64,256]{2,1,0:T(8,128)(2,1)S(1)} %get-tuple-element.28), channel_id=1, source_target_pairs={{0,1},{1,0},{2,3},{3,2},{4,5},{5,4},{6,7},{7,6},{8,9},{9,8},{10,11... | collective-permute-start | bytes 393224 | tf_op jit(solution)/shard_map/ppermute | solution.py:198
  49.3 5.8 %collective-permute-start.9 = (bf16[4,64,256]{2,1,0:T(8,128)(2,1)S(1)}, bf16[4,64,256]{2,1,0:T(8,128)(2,1)S(1)}, u32[]{:S(2)}, u32[]{:S(2)}) collective-permute-start(bf16[4,64,256]{2,1,0:T(8,128)(2,1)S(1)} %get-tuple-element.29), channel_id=1, source_target_pairs={{0,3},{1,2},{2,1},{3,0},{4,7},{5,6},{6,5},{7,4},{8,11},{9,10},{10,... | collective-permute-start | bytes 393224 | tf_op jit(solution)/shard_map/ppermute | solution.py:198
  50.6 6.9 %collective-permute-start.8 = (bf16[4,64,256]{2,1,0:T(8,128)(2,1)S(1)}, bf16[4,64,256]{2,1,0:T(8,128)(2,1)S(1)}, u32[]{:S(2)}, u32[]{:S(2)}) collective-permute-start(bf16[4,64,256]{2,1,0:T(8,128)(2,1)S(1)} %get-tuple-element.30), channel_id=1, source_target_pairs={{0,2},{1,3},{2,0},{3,1},{4,6},{5,7},{6,4},{7,5},{8,10},{9,11},{10,... | collective-permute-start | bytes 393224 | tf_op jit(solution)/shard_map/ppermute | solution.py:198

commit v3 on v2

v3 whole, which is shorter than its diff:
```python
import math

import jax
import jax.numpy as jnp
import numpy as np
from jax import lax
from jax.experimental import pallas as pl
from jax.experimental.pallas import tpu as pltpu
from jax.sharding import PartitionSpec as P

LEVELS = 4
BAND_REACH = 4
F32 = jnp.float32
BF16 = jnp.bfloat16
VMEM_LIMIT = 28 * 1024 * 1024
NN = (((1,), (0,)), ((), ()))
NT = (((1,), (1,)), ((), ()))
TN = (((0,), (0,)), ((), ()))


def product(a, b, dims=NN):
    return lax.dot_general(a, b, dims, preferred_element_type=F32)


def halves(x):
    high = x.astype(BF16)
    return high, (x - high.astype(F32)).astype(BF16)


def spread_matrix(pixels):
    parts = []
    for level in range(LEVELS):
        group = 2**level
        parts.append(np.repeat(np.eye(pixels // group, dtype=np.float32), group, axis=1) / group)
    return np.concatenate(parts, axis=0).astype(jnp.bfloat16)


def column_picker(columns):
    half = columns // 2
    taps = [
        (
            lax.broadcasted_iota(jnp.int32, (columns, half), 0)
            == 2 * lax.broadcasted_iota(jnp.int32, (columns, half), 1) + (dx - 1)
        )
        for dx in range(3)
    ]
    return jnp.concatenate([jnp.where(tap, 1.0, 0.0).astype(BF16) for tap in taps], axis=1)


def gathered(picked, rows, half):
    return jnp.concatenate(
        [
            jnp.concatenate([picked(frame, row)[:, dx * half : (dx + 1) * half] for frame in range(2)], axis=1)
            for row in rows
            for dx in range(3)
        ],
        axis=0,
    )


def stacked_weight(weight_ref, taps):
    return jnp.concatenate([weight_ref[dy, dx] for dy in taps for dx in range(3)], axis=0)


def local_rows_kernel(frames_ref, weight_ref, proj_ref, lower_ref, partial_ref, picker_ref, gram_ref, pick_ref):
    _, rows, channels, columns = frames_ref.shape
    half = columns // 2
    mid = weight_ref.shape[3]
    picker_ref[...] = column_picker(columns)
    flat = frames_ref[...].reshape(2 * rows * channels, columns)
    pick_ref[...] = product(flat, picker_ref[...]).astype(BF16).reshape(pick_ref.shape)

    def picked(frame, row):
        return pick_ref[frame, row]

    lower = product(stacked_weight(weight_ref, range(3)), gathered(picked, (1, 2, 3), half), TN)
    lower_ref[...] = jnp.maximum(lower, 0.0).astype(BF16)
    partial_ref[...] = product(stacked_weight(weight_ref, (1, 2)), gathered(picked, (0, 1), half), TN)
    gram_high, gram_low = halves(product(proj_ref[...], proj_ref[...], NT))
    gram_ref[:mid, :] = gram_high
    gram_ref[mid:, :] = gram_low


def held_class(band, start_ref, count_ref, offsets, slots):
    place = lax.axis_index("band")
    core = lax.rem(place, 2)
    start = start_ref[0]
    swap = lax.rem(start + 2 * BAND_REACH, 2)
    slot_of = [j * band + place - core + lax.rem(core + swap, 2) for j in range(slots)]
    steps = [jnp.where(core == 0, even, odd) for even, odd in zip(*offsets)]
    return swap == 0, [start + k for k in slot_of], [k < count_ref[0] for k in slot_of], steps


def target_kernel(
    band, offsets, factor, start_ref, count_ref, rim_ref, weight_ref, lower_ref, partial_ref, picker_ref, gram_ref,
    grad_ref, other_ref, spread_ref, target_ref, scaled_ref, own_ref, *refs
):
    message_refs, tile_ref = refs[:-1], refs[-1]
    half = lower_ref.shape[1] // 2
    mid = lower_ref.shape[0]
    channels = rim_ref.shape[2]
    slots = tile_ref.shape[0]
    pick = product(rim_ref[...].reshape(2 * channels, 2 * half), picker_ref[...]).astype(BF16)

    def picked(frame, row):
        return pick[frame * channels : (frame + 1) * channels]

    upper = product(stacked_weight(weight_ref, (0,)), gathered(picked, (0,), half), TN) + partial_ref[...]
    upper = jnp.maximum(upper, 0.0).astype(BF16)
    source = jnp.concatenate([upper[:, :half], lower_ref[:, :half]], axis=1)
    target = jnp.concatenate([upper[:, half:], lower_ref[:, half:]], axis=1)
    both = product(gram_ref[...], source)
    high, low = halves((both[:mid] + both[mid:]) * factor)
    scaled_ref[:mid, :] = high
    scaled_ref[mid : 2 * mid, :] = low
    scaled_ref[2 * mid :, :] = high
    same, held, active, steps = held_class(band, start_ref, count_ref, offsets, slots)

    def term(slot, block_ref):
        high, low = halves(product(source, block_ref[0, slot, 0], NT))
        both = product(jnp.concatenate([high, low], axis=0), spread_ref[...])
        tile_ref[slot] = (both[:mid] + both[mid:]).astype(BF16)

    for slot in range(slots):
        pl.when(jnp.logical_and(active[slot], same))(lambda: term(slot, grad_ref))
        pl.when(jnp.logical_and(active[slot], jnp.logical_not(same)))(lambda: term(slot, other_ref))

    def chosen(offset):
        out = jnp.zeros(tile_ref.shape[1:], BF16)
        for slot in range(slots):
            out = jnp.where(jnp.logical_and(active[slot], held[slot] == offset), tile_ref[slot], out)
        return out

    target_ref[...] = target
    own_ref[...] = chosen(0)
    for step, message_ref in zip(steps, message_refs):
        message_ref[0] = target
        message_ref[1] = chosen(-step)


def gradient_kernel(
    band, offsets, factor, start_ref, count_ref, grad_ref, other_ref, spread_ref, proj_ref, target_ref, own_ref, *refs
):
    arrived, (held_ref, kept_ref, *sent_refs, sum_ref, out_ref) = refs[: len(offsets[0])], refs[len(offsets[0]) :]
    slots, mid, pixels = held_ref.shape
    same, held, active, steps = held_class(band, start_ref, count_ref, offsets, slots)
    sum_ref[...] = jnp.zeros(sum_ref.shape, F32)

    def add(slot, block_ref):
        high, low = halves(product(held_ref[slot], spread_ref[...], NT))
        both = product(jnp.concatenate([high, low], axis=0), block_ref[0, slot, 0])
        sum_ref[...] += both[:mid] + both[mid:]

    for slot in range(slots):
        block = target_ref[...]
        for step, part in zip(steps, arrived):
            block = jnp.where(held[slot] == step, part[0], block)
        held_ref[slot] = block
        pl.when(jnp.logical_and(active[slot], same))(lambda: add(slot, grad_ref))
        pl.when(jnp.logical_and(active[slot], jnp.logical_not(same)))(lambda: add(slot, other_ref))

    total = own_ref[...].astype(F32)
    for part in arrived:
        total = total + part[1].astype(F32)
    high, low = halves(jnp.concatenate([sum_ref[...], total], axis=1))
    out_ref[...] = (product(proj_ref[...], high, TN) + product(proj_ref[...], low, TN)) * factor
    parts, share, width = kept_ref.shape
    place = lax.axis_index("band")
    for k in range(band):
        first = pl.multiple_of(jnp.bitwise_xor(place, k) * share, share)
        for part in range(parts):
            out = out_ref[pl.ds(first, share), part * width : (part + 1) * width]
            if k == 0:
                kept_ref[part] = out
            else:
                sent_refs[k - 1][part] = out.astype(BF16)


def pyramid_kernel(band, start_ref, count_ref, held_ref, other_ref, scaled_ref, spread_ref, pyramid_ref):
    slot = pl.program_id(0)
    active = slot * band + lax.axis_index("band") < count_ref[0]
    same = lax.rem(start_ref[0] + 2 * BAND_REACH, 2) == 0

    @pl.when(active)
    def _():
        target = jnp.where(same, held_ref[0], other_ref[0])
        high, low = halves(product(spread_ref[...], target, NT))
        corr = product(jnp.concatenate([high, high, low], axis=1), scaled_ref[...])
        pyramid_ref[0, 0, 0] = corr.astype(BF16)

    @pl.when(jnp.logical_not(active))
    def _():
        pyramid_ref[0, 0, 0] = jnp.zeros(pyramid_ref.shape[3:], BF16)


def shards(frames, conv_weight, proj_weight, band_start, band_count, pyramid_grad):
    band = lax.axis_size("band")
    row_blocks = lax.axis_size("rows")
    mid, channels = proj_weight.shape
    share = channels // band
    factor = 1.0 / math.sqrt(channels)
    frames = jnp.swapaxes(frames, 2, 3)
    grad = jnp.swapaxes(pyramid_grad, 3, 4)
    slots = grad.shape[1]
    entries, pixels = grad.shape[3:]
    columns = frames.shape[3]
    half = columns // 2
    params = pltpu.CompilerParams(vmem_limit_bytes=VMEM_LIMIT)
    smem = pl.BlockSpec(memory_space=pltpu.SMEM)
    vmem = pl.BlockSpec(memory_space=pltpu.VMEM)
    spread = jnp.asarray(spread_matrix(pixels))

    offsets = ([], [])
    for reach in range(1, BAND_REACH + 1):
        offsets[reach % 2].extend([reach, -reach])
    steps = len(offsets[0])

    def along_rows(x, step):
        pairs = []
        for row in range(row_blocks):
            for p in range(band):
                to = row - offsets[p % 2][step]
                if 0 <= to < row_blocks:
                    pairs.append((row * band + p, to * band + p))
        return lax.ppermute(x, ("rows", "band"), pairs)

    def across(x, k):
        return lax.ppermute(x, "band", [(p, p ^ k) for p in range(band)])

    rim = lax.ppermute(frames[:, -1:], "rows", [(i, i + 1) for i in range(row_blocks - 1)])
    other_grad = across(grad, 1)
    lower, partial, picker, gram = pl.pallas_call(
        local_rows_kernel,
        out_shape=(
            jax.ShapeDtypeStruct((mid, columns), BF16),
            jax.ShapeDtypeStruct((mid, columns), F32),
            jax.ShapeDtypeStruct((columns, 3 * half), BF16),
            jax.ShapeDtypeStruct((2 * mid, mid), BF16),
        ),
        scratch_shapes=[pltpu.VMEM(frames.shape[:3] + (3 * half,), BF16)],
        compiler_params=params,
        cost_estimate=pl.CostEstimate(flops=2**31, bytes_accessed=2**21, transcendentals=0),
    )(frames, conv_weight, proj_weight)

    block = jax.ShapeDtypeStruct((mid, pixels), BF16)
    message = jax.ShapeDtypeStruct((2, mid, pixels), BF16)
    target, scaled, own_term, *messages = pl.pallas_call(
        lambda *refs: target_kernel(band, offsets, factor, *refs),
        in_specs=[smem] * 2 + [vmem] * 9,
        out_shape=(block, jax.ShapeDtypeStruct((3 * mid, pixels), BF16), block) + (message,) * steps,
        scratch_shapes=[pltpu.VMEM((slots, mid, pixels), BF16)],
        compiler_params=params,
        cost_estimate=pl.CostEstimate(flops=2**31, bytes_accessed=2**22, transcendentals=0),
    )(band_start, band_count, rim, conv_weight, lower, partial, picker, gram, grad, other_grad, spread)

    arrived = [along_rows(messages[i], i) for i in range(steps)]

    out_parts = 2 * pixels // half
    part = (out_parts, share, half)
    held, kept, *sent = pl.pallas_call(
        lambda *refs: gradient_kernel(band, offsets, factor, *refs),
        in_specs=[smem] * 2 + [vmem] * (6 + steps),
        out_shape=(jax.ShapeDtypeStruct((slots, mid, pixels), BF16), jax.ShapeDtypeStruct(part, F32))
        + (jax.ShapeDtypeStruct(part, BF16),) * (band - 1),
        scratch_shapes=[pltpu.VMEM((mid, pixels), F32), pltpu.VMEM((channels, 2 * pixels), F32)],
        compiler_params=params,
        cost_estimate=pl.CostEstimate(flops=2**31, bytes_accessed=2**22, transcendentals=0),
    )(band_start, band_count, grad, other_grad, spread, proj_weight, target, own_term, *arrived)

    received = [across(sent[k - 1], k) for k in reversed(range(1, band))]
    other = across(held, 1)

    def whole(shape):
        return pl.BlockSpec(shape, lambda j: (0,) * len(shape))

    target_spec = pl.BlockSpec((1, mid, pixels), lambda j: (j, 0, 0))
    grad_spec = pl.BlockSpec((1, 1, 1, entries, pixels), lambda j: (0, j, 0, 0, 0))
    pyramid = pl.pallas_call(
        lambda *refs: pyramid_kernel(band, *refs),
        grid=(slots,),
        in_specs=[smem, smem, target_spec, target_spec, whole((3 * mid, pixels)), whole((entries, pixels))],
        out_specs=grad_spec,
        out_shape=jax.ShapeDtypeStruct(grad.shape, BF16),
        compiler_params=params,
        cost_estimate=pl.CostEstimate(flops=2**31, bytes_accessed=2**22, transcendentals=0),
    )(band_start, band_count, held, other, scaled, spread)

    total, pyramid = lax.optimization_barrier((kept, pyramid))
    for x in received:
        total = total + x.astype(F32)
    total = jnp.swapaxes(total, 1, 2)
    return (jnp.swapaxes(pyramid, 3, 4), total[: out_parts // 2], total[out_parts // 2 :])


def solution(mesh):
    in_specs = (
        P(None, "rows", None, None),
        P(),
        P(),
        P("rows"),
        P("rows"),
        P("rows", None, "band", None, None),
    )
    out_specs = (
        P("rows", None, "band", None, None),
        P("rows", None, "band"),
        P("rows", None, "band"),
    )
    return jax.shard_map(shards, mesh=mesh, in_specs=in_specs, out_specs=out_specs, check_vma=False)
```

time: 59.2 us -> 49.9 us (0.84); the launches traced: 58.3 us -> 49.7 us
  waiting for transfers between devices: 25.9 us -> 20.1 us
  local copies, waits for them, and re-layouts: 6.82 us -> 4.58 us
  other arithmetic: 1.29 us -> 0.07 us
  starting transfers between devices: 15.8 us -> 16.4 us
    ppermute x5, waiting for transfers between devices: 8.5 us -> 4.04 us  [across(): return lax.ppermute(x, 'band', [(p, p ^ k) for p in range(band)])]
    unnamed x20 -> x14, local copies, waits for them, and re-layouts: 5.13 us -> 2.92 us
    ppermute x4, waiting for transfers between devices: 17 us -> 15.5 us  [along_rows(): return lax.ppermute(x, ('rows', 'band'), pairs)]
    ppermute x4, starting transfers between devices: 9.08 us -> 10.3 us  [along_rows(): return lax.ppermute(x, ('rows', 'band'), pairs)]
    another operation x3 -> x0, other arithmetic: 1.13 us -> none  [the longest x1 1.07 us: shards(): jnp.stack([target, term(-step_offsets[i])])]
    pallas_call x2 -> x3, Pallas kernels: 4.89 us -> 5.1 us  [the longest x1 2.2 us: shards(): pl.pallas_call(lambda *refs: pyramid_kernel(band, *refs), grid=(slots,),...]
  transfers between devices with their start and end apart: 10 -> 10, of which waited for: 8 -> 6; matrix products, arithmetic and copies ran while one was open for 0% -> 2% of each run, Pallas kernels for 2% -> 7%
where the time goes in v3:
time: 49.9 us; the launch traced here: 49.7 us
  waiting for transfers between devices  20.1 us (40%)
  starting transfers between devices  16.4 us (33%)
  Pallas kernels  6.51 us (13%)
  local copies, waits for them, and re-layouts  4.58 us (9%)
  between operations  2.05 us (4%)
    ppermute x4, waiting for transfers between devices, along_rows(): return lax.ppermute(x, ('rows', 'band'), pairs)  15.5 us
    ppermute x4, starting transfers between devices, along_rows(): return lax.ppermute(x, ('rows', 'band'), pairs)  10.3 us
    ppermute x5, waiting for transfers between devices, across(): return lax.ppermute(x, 'band', [(p, p ^ k) for p in range(band)])  4.04 us
    ppermute x1, starting transfers between devices, shards(): lax.ppermute(frames[:, -1:], 'rows', [(i, i + 1) for i in range(row_block...  3.15 us
    ppermute x5, starting transfers between devices, across(): return lax.ppermute(x, 'band', [(p, p ^ k) for p in range(band)])  3.02 us
    unnamed x14, local copies, waits for them, and re-layouts  2.92 us
    pallas_call x1, Pallas kernels, shards(): pl.pallas_call(lambda *refs: pyramid_kernel(band, *refs), grid=(slots,),...  2.2 us
    pallas_call x1, Pallas kernels, shards(): pl.pallas_call(lambda *refs: target_kernel(band, offsets, factor, *refs),...  1.54 us
  transfers between devices with their start and end apart: 10, of which 6 were waited for; matrix products, arithmetic and copies ran while one was open for 2% of the time, Pallas kernels for 7%

profile of v3, /device:TPU:25, one launch (start us, length us, event | category | flops | bytes accessed | tf_op | source)
XLA Modules:
  0.0 49.7 jit_solution(6309747646362490270)
XLA Ops:
  0.6 0.7 %collective-permute-start = (bf16[1,2,1,960,512]{4,3,2,1,0:T(8,128)(2,1)}, bf16[1,2,1,960,512]{4,3,2,1,0:T(8,128)(2,1)S(1)}, u32[]{:S(2)}, u32[]{:S(2)}) collective-permute-start(bf16[1,2,1,960,512]{4,3,2,1,0:T(8,128)(2,1)} %bitcast.7), channel_id=1, source_target_pairs={{0,1},{1,0},{2,3},{3,2},{4,5},{5,4},{6,7},{7,6},{8,9},{9,8},{10,11... | collective-permute-start | bytes 5898248 | tf_op jit(solution)/shard_map/ppermute | solution.py:228
  1.4 0.9 %slice.12 = bf16[2,1,96,512]{3,2,1,0:T(8,128)(2,1)S(1)} slice(bf16[2,4,96,512]{3,2,1,0:T(8,128)(2,1)} %bitcast.5), slice={[0:2], [3:4], [0:96], [0:512]} | slice | bytes 393216 | tf_op jit(solution)/shard_map/slice | solution.py:230
  2.3 3.1 %collective-permute-start.1 = (bf16[2,1,96,512]{3,2,1,0:T(8,128)(2,1)S(1)}, bf16[2,1,96,512]{3,2,1,0:T(8,128)(2,1)S(1)}, u32[]{:S(2)}, u32[]{:S(2)}) collective-permute-start(bf16[2,1,96,512]{3,2,1,0:T(8,128)(2,1)S(1)} %slice.12), channel_id=1, source_target_pairs={{0,4},{4,8},{8,12},{12,16},{16,20},{20,24},{24,28},{1,5},{5,9},{9,... | collective-permute-start | bytes 589832 | tf_op jit(solution)/shard_map/ppermute | solution.py:230
  6.8 0.0 copy-start
  6.8 1.1 %copy-done = bf16[2,4,512,96]{2,3,1,0:T(8,128)(2,1)S(1)} copy-done((bf16[2,4,512,96]{2,3,1,0:T(8,128)(2,1)S(1)}, bf16[2,4,512,96]{2,3,1,0:T(8,128)(2,1)}, u32[]{:S(2)}) %copy-start) | copy-done | bytes 786456
  7.9 0.0 copy-start.2
  7.9 0.9 %copy-done.2 = bf16[3,3,96,128]{3,2,1,0:T(8,128)(2,1)S(1)} copy-done((bf16[3,3,96,128]{3,2,1,0:T(8,128)(2,1)S(1)}, bf16[3,3,96,128]{3,2,1,0:T(8,128)(2,1)}, u32[]{:S(2)}) %copy-start.2) | copy-done | bytes 221208
  8.8 0.0 copy-start.4
  8.8 0.8 %copy-done.4 = bf16[128,256]{1,0:T(8,128)(2,1)S(1)} copy-done((bf16[128,256]{1,0:T(8,128)(2,1)S(1)}, bf16[128,256]{1,0:T(8,128)(2,1)}, u32[]{:S(2)}) %copy-start.4) | copy-done | bytes 65560
  9.7 0.0 copy-start.1
  9.7 0.0 copy-start.3
  9.7 0.0 copy-start.6
  9.7 1.4 %shard_map.94 = (bf16[128,512]{1,0:T(8,128)(2,1)S(1)}, f32[128,512]{1,0:T(8,128)S(1)}, bf16[512,768]{1,0:T(8,128)(2,1)S(1)}, bf16[256,128]{1,0:T(8,128)(2,1)S(1)}) custom-call(bf16[2,4,96,512]{3,2,1,0:T(8,128)(2,1)S(1)} %bitcast.6, bf16[3,3,96,128]{3,2,1,0:T(8,128)(2,1)S(1)} %copy-done.2, bf16[128,256]{1,0:T(8,128)(2,1)S(1)} %copy-done.4), custom_call_target="tpu_custom_call" | custom-call | flops 2147483648 | bytes 2097152 | tf_op jit(solution)/shard_map/pallas_call | solution.py:232
  11.1 0.5 %collective-permute-done.1.refs_2_ = bf16[2,1,96,512]{3,2,1,0:T(8,128)(2,1)S(1)} collective-permute-done((bf16[2,1,96,512]{3,2,1,0:T(8,128)(2,1)S(1)}, bf16[2,1,96,512]{3,2,1,0:T(8,128)(2,1)S(1)}, u32[]{:S(2)}, u32[]{:S(2)}) %collective-permute-start.1) | collective-permute-done | bytes 196640 | tf_op jit(solution)/shard_map/ppermute | solution.py:230
  11.6 0.0 collective-permute-done.refs_9_.refs_3_
  11.6 0.0 copy-done.1
  11.6 0.0 copy-done.3
  11.6 0.0 copy-done.6
  11.6 0.0 copy-start.5
  11.7 1.5 %shard_map.95 = (bf16[128,512]{1,0:T(8,128)(2,1)S(1)}, bf16[384,512]{1,0:T(8,128)(2,1)S(1)}, bf16[128,512]{1,0:T(8,128)(2,1)S(1)}, bf16[2,128,512]{2,1,0:T(8,128...) custom-call(s32[1]{0:T(128)S(6)} %copy.10.refs_0_, ...), custom_call_target="tpu_custom_call" | custom-call | flops 2147483648 | bytes 4194304 | tf_op jit(solution)/shard_map/pallas_call | solution.py:247
  13.2 3.6 %collective-permute-start.2 = (bf16[2,128,512]{2,1,0:T(8,128)(2,1)S(1)}, bf16[2,128,512]{2,1,0:T(8,128)(2,1)S(1)}, u32[]{:S(2)}, u32[]{:S(2)}) collective-permute-start(bf16[2,128,512]{2,1,0:T(8,128)(2,1)S(1)} %get-tuple-element.27), channel_id=1, source_target_pairs={{5,1},{7,3},{8,0},{9,5},{10,2},{11,7},{12,4},{13,9},{14,6},{15,11}... | collective-permute-start | bytes 786440 | tf_op jit(solution)/shard_map/ppermute | solution.py:225
  16.8 1.9 %collective-permute-start.3 = (bf16[2,128,512]{2,1,0:T(8,128)(2,1)S(1)}, bf16[2,128,512]{2,1,0:T(8,128)(2,1)S(1)}, u32[]{:S(2)}, u32[]{:S(2)}) collective-permute-start(bf16[2,128,512]{2,1,0:T(8,128)(2,1)S(1)} %get-tuple-element.28), channel_id=1, source_target_pairs={{0,8},{1,5},{2,10},{3,7},{4,12},{5,9},{6,14},{7,11},{8,16},{9,13},... | collective-permute-start | bytes 786440 | tf_op jit(solution)/shard_map/ppermute | solution.py:225
  18.8 3.4 %collective-permute-start.4 = (bf16[2,128,512]{2,1,0:T(8,128)(2,1)S(1)}, bf16[2,128,512]{2,1,0:T(8,128)(2,1)S(1)}, u32[]{:S(2)}, u32[]{:S(2)}) collective-permute-start(bf16[2,128,512]{2,1,0:T(8,128)(2,1)S(1)} %get-tuple-element.29), channel_id=1, source_target_pairs={{13,1},{15,3},{16,0},{17,5},{18,2},{19,7},{20,4},{21,9},{22,6},{23... | collective-permute-start | bytes 786440 | tf_op jit(solution)/shard_map/ppermute | solution.py:225
  22.2 1.3 %collective-permute-start.5 = (bf16[2,128,512]{2,1,0:T(8,128)(2,1)S(1)}, bf16[2,128,512]{2,1,0:T(8,128)(2,1)S(1)}, u32[]{:S(2)}, u32[]{:S(2)}) collective-permute-start(bf16[2,128,512]{2,1,0:T(8,128)(2,1)S(1)} %get-tuple-element.30), channel_id=1, source_target_pairs={{0,16},{1,13},{2,18},{3,15},{4,20},{5,17},{6,22},{7,19},{8,24},{9,... | collective-permute-start | bytes 786440 | tf_op jit(solution)/shard_map/ppermute | solution.py:225
  23.5 0.0 collective-permute-done.2.refs_8_
  23.5 4.0 %collective-permute-done.3.refs_9_ = bf16[2,128,512]{2,1,0:T(8,128)(2,1)S(1)} collective-permute-done((bf16[2,128,512]{2,1,0:T(8,128)(2,1)S(1)}, bf16[2,128,512]{2,1,0:T(8,128)(2,1)S(1)}, u32[]{:S(2)}, u32[]{:S(2)}) %collective-permute-start.3) | collective-permute-done | bytes 262176 | tf_op jit(solution)/shard_map/ppermute | solution.py:225
  27.5 0.7 %collective-permute-done.4.refs_10_ = bf16[2,128,512]{2,1,0:T(8,128)(2,1)S(1)} collective-permute-done((bf16[2,128,512]{2,1,0:T(8,128)(2,1)S(1)}, bf16[2,128,512]{2,1,0:T(8,128)(2,1)S(1)}, u32[]{:S(2)}, u32[]{:S(2)}) %collective-permute-start.4) | collective-permute-done | bytes 262176 | tf_op jit(solution)/shard_map/ppermute | solution.py:225
  28.2 10.8 %collective-permute-done.5.refs_11_ = bf16[2,128,512]{2,1,0:T(8,128)(2,1)S(1)} collective-permute-done((bf16[2,128,512]{2,1,0:T(8,128)(2,1)S(1)}, bf16[2,128,512]{2,1,0:T(8,128)(2,1)S(1)}, u32[]{:S(2)}, u32[]{:S(2)}) %collective-permute-start.5) | collective-permute-done | bytes 262176 | tf_op jit(solution)/shard_map/ppermute | solution.py:225
  39.0 0.0 copy-done.5
  39.0 1.4 %shard_map.96 = (bf16[2,128,512]{2,1,0:T(8,128)(2,1)S(1)}, f32[4,64,256]{2,1,0:T(8,128)S(1)}, bf16[4,64,256]{2,1,0:T(8,128)(2,1)S(1)}, bf16[4,64,256]{2,1,0:T(8,128)(2,1)S(1)}, bf16[4,64,256]{2,1,0:T(8,128)(2,1)S(1)}) custom-call(s32[1]{0:T(128)S(6)} %copy.10.refs_0_, s32[1]{0:T(128)S(6)} %copy.11.refs_1_, bf16[1,2,1,960,512]{4,3,2,1,0:T(8,128)(2,1)S(1)} %bitcast.9, ...), custom_call_target="tpu_custom_call" | custom-call | flops 2147483648 | bytes 4194304 | tf_op jit(solution)/shard_map/pallas_call | solution.py:260
  40.4 0.1 collective-permute-start.6
  40.5 1.3 %collective-permute-start.7 = (bf16[4,64,256]{2,1,0:T(8,128)(2,1)S(1)}, bf16[4,64,256]{2,1,0:T(8,128)(2,1)S(1)}, u32[]{:S(2)}, u32[]{:S(2)}) collective-permute-start(bf16[4,64,256]{2,1,0:T(8,128)(2,1)S(1)} %get-tuple-element.36), channel_id=1, source_target_pairs={{0,3},{1,2},{2,1},{3,0},{4,7},{5,6},{6,5},{7,4},{8,11},{9,10},{10,... | collective-permute-start | bytes 393224 | tf_op jit(solution)/shard_map/ppermute | solution.py:228
  41.8 0.6 %collective-permute-start.8 = (bf16[4,64,256]{2,1,0:T(8,128)(2,1)S(1)}, bf16[4,64,256]{2,1,0:T(8,128)(2,1)S(1)}, u32[]{:S(2)}, u32[]{:S(2)}) collective-permute-start(bf16[4,64,256]{2,1,0:T(8,128)(2,1)S(1)} %get-tuple-element.37), channel_id=1, source_target_pairs={{0,2},{1,3},{2,0},{3,1},{4,6},{5,7},{6,4},{7,5},{8,10},{9,11},{10,... | collective-permute-start | bytes 393224 | tf_op jit(solution)/shard_map/ppermute | solution.py:228
  42.3 0.3 collective-permute-start.9
  42.7 0.0 collective-permute-done.6.refs_3_
  42.7 2.2 %shard_map.97 = bf16[1,2,1,960,512]{4,3,2,1,0:T(8,128)(2,1)} custom-call(s32[1]{0:T(128)S(6)} %copy.10.refs_0_, s32[1]{0:T(128)S(6)} %copy.11.refs_1_, bf16[2,128,512]{2,1,0:T(8,128)(2,1)S(1)} %get-tuple-element.32.refs_2_, bf16[2,128,512]{2,1,0:T(8,128)(2,1)S(1)} %collective-permute-done.6.refs_3_, bf16[384,512]{1,0:T(8,128)(2,1)S(1)} %get-tuple-element.33.refs_4_, ...), custom_call_target="tpu_custom_call" | custom-call | flops 2147483648 | bytes 4194304 | tf_op jit(solution)/shard_map/pallas_call | solution.py:278
  44.9 1.5 %collective-permute-done.7 = bf16[4,64,256]{2,1,0:T(8,128)(2,1)S(1)} collective-permute-done((bf16[4,64,256]{2,1,0:T(8,128)(2,1)S(1)}, bf16[4,64,256]{2,1,0:T(8,128)(2,1)S(1)}, u32[]{:S(2)}, u32[]{:S(2)}) %collective-permute-start.7) | collective-permute-done | bytes 131104 | tf_op jit(solution)/shard_map/ppermute | solution.py:228
  46.3 2.6 %collective-permute-done.8 = bf16[4,64,256]{2,1,0:T(8,128)(2,1)S(1)} collective-permute-done((bf16[4,64,256]{2,1,0:T(8,128)(2,1)S(1)}, bf16[4,64,256]{2,1,0:T(8,128)(2,1)S(1)}, u32[]{:S(2)}, u32[]{:S(2)}) %collective-permute-start.8) | collective-permute-done | bytes 131104 | tf_op jit(solution)/shard_map/ppermute | solution.py:228
  48.9 0.0 collective-permute-done.9
  48.9 0.1 add_bitcast_fusion
  49.0 0.7 %fusion = (f32[2,256,64]{1,2,0:T(8,128)}, f32[2,256,64]{1,2,0:T(8,128)}) fusion(f32[4,256,64]{1,2,0:T(8,128)S(1)} %add_bitcast_fusion), kind=kLoop, calls=%fused_computation.1 | loop fusion | bytes 524288 | tf_op jit(solution)/shard_map/slice | solution.py:292
Async XLA Ops:
  0.6 11.0 %collective-permute-start = (bf16[1,2,1,960,512]{4,3,2,1,0:T(8,128)(2,1)}, bf16[1,2,1,960,512]{4,3,2,1,0:T(8,128)(2,1)S(1)}, u32[]{:S(2)}, u32[]{:S(2)}) collective-permute-start(bf16[1,2,1,960,512]{4,3,2,1,0:T(8,128)(2,1)} %bitcast.7), channel_id=1, source_target_pairs={{0,1},{1,0},{2,3},{3,2},{4,5},{5,4},{6,7},{7,6},{8,9},{9,8},{10,11... | collective-permute-start | bytes 5898248 | tf_op jit(solution)/shard_map/ppermute | solution.py:228
  2.3 9.3 %collective-permute-start.1 = (bf16[2,1,96,512]{3,2,1,0:T(8,128)(2,1)S(1)}, bf16[2,1,96,512]{3,2,1,0:T(8,128)(2,1)S(1)}, u32[]{:S(2)}, u32[]{:S(2)}) collective-permute-start(bf16[2,1,96,512]{3,2,1,0:T(8,128)(2,1)S(1)} %slice.12), channel_id=1, source_target_pairs={{0,4},{4,8},{8,12},{12,16},{16,20},{20,24},{24,28},{1,5},{5,9},{9,... | collective-permute-start | bytes 589832 | tf_op jit(solution)/shard_map/ppermute | solution.py:230
  6.8 1.1 %copy-start = (bf16[2,4,512,96]{2,3,1,0:T(8,128)(2,1)S(1)}, bf16[2,4,512,96]{2,3,1,0:T(8,128)(2,1)}, u32[]{:S(2)}) copy-start(bf16[2,4,512,96]{2,3,1,0:T(8,128)(2,1)} %param.7) | copy-start | bytes 2359300
  7.9 0.9 %copy-start.2 = (bf16[3,3,96,128]{3,2,1,0:T(8,128)(2,1)S(1)}, bf16[3,3,96,128]{3,2,1,0:T(8,128)(2,1)}, u32[]{:S(2)}) copy-start(bf16[3,3,96,128]{3,2,1,0:T(8,128)(2,1)} %refs_3_.1) | copy-start | bytes 663556
  8.8 0.8 %copy-start.4 = (bf16[128,256]{1,0:T(8,128)(2,1)S(1)}, bf16[128,256]{1,0:T(8,128)(2,1)}, u32[]{:S(2)}) copy-start(bf16[128,256]{1,0:T(8,128)(2,1)} %refs_5_.2) | copy-start | bytes 196612
  9.7 1.9 %copy-start.1 = (bf16[1,2,1,512,960]{3,4,2,1,0:T(8,128)(2,1)S(1)}, bf16[1,2,1,512,960]{3,4,2,1,0:T(8,128)(2,1)}, u32[]{:S(2)}) copy-start(bf16[1,2,1,512,960]{3,4,2,1,0:T(8,128)(2,1)} %param.12) | copy-start | bytes 5898244
  9.7 1.9 %copy-start.3 = (bf16[3,3,96,128]{3,2,1,0:T(8,128)(2,1)S(1)}, bf16[3,3,96,128]{3,2,1,0:T(8,128)(2,1)}, u32[]{:S(2)}) copy-start(bf16[3,3,96,128]{3,2,1,0:T(8,128)(2,1)} %refs_3_.1) | copy-start | bytes 663556
  9.7 1.9 %copy-start.6 = (bf16[960,512]{1,0:T(8,128)(2,1)S(1)}, bf16[960,512]{1,0:T(8,128)(2,1)}, u32[]{:S(2)}) copy-start(bf16[960,512]{1,0:T(8,128)(2,1)} %constant.2.clone.refs_10_.refs_4_.refs_5_) | copy-start | bytes 2949124
  11.6 27.4 %copy-start.5 = (bf16[128,256]{1,0:T(8,128)(2,1)S(1)}, bf16[128,256]{1,0:T(8,128)(2,1)}, u32[]{:S(2)}) copy-start(bf16[128,256]{1,0:T(8,128)(2,1)} %refs_5_.2) | copy-start | bytes 196612
  13.2 10.3 %collective-permute-start.2 = (bf16[2,128,512]{2,1,0:T(8,128)(2,1)S(1)}, bf16[2,128,512]{2,1,0:T(8,128)(2,1)S(1)}, u32[]{:S(2)}, u32[]{:S(2)}) collective-permute-start(bf16[2,128,512]{2,1,0:T(8,128)(2,1)S(1)} %get-tuple-element.27), channel_id=1, source_target_pairs={{5,1},{7,3},{8,0},{9,5},{10,2},{11,7},{12,4},{13,9},{14,6},{15,11}... | collective-permute-start | bytes 786440 | tf_op jit(solution)/shard_map/ppermute | solution.py:225
  16.8 10.7 %collective-permute-start.3 = (bf16[2,128,512]{2,1,0:T(8,128)(2,1)S(1)}, bf16[2,128,512]{2,1,0:T(8,128)(2,1)S(1)}, u32[]{:S(2)}, u32[]{:S(2)}) collective-permute-start(bf16[2,128,512]{2,1,0:T(8,128)(2,1)S(1)} %get-tuple-element.28), channel_id=1, source_target_pairs={{0,8},{1,5},{2,10},{3,7},{4,12},{5,9},{6,14},{7,11},{8,16},{9,13},... | collective-permute-start | bytes 786440 | tf_op jit(solution)/shard_map/ppermute | solution.py:225
  18.8 9.5 %collective-permute-start.4 = (bf16[2,128,512]{2,1,0:T(8,128)(2,1)S(1)}, bf16[2,128,512]{2,1,0:T(8,128)(2,1)S(1)}, u32[]{:S(2)}, u32[]{:S(2)}) collective-permute-start(bf16[2,128,512]{2,1,0:T(8,128)(2,1)S(1)} %get-tuple-element.29), channel_id=1, source_target_pairs={{13,1},{15,3},{16,0},{17,5},{18,2},{19,7},{20,4},{21,9},{22,6},{23... | collective-permute-start | bytes 786440 | tf_op jit(solution)/shard_map/ppermute | solution.py:225
  22.2 16.8 %collective-permute-start.5 = (bf16[2,128,512]{2,1,0:T(8,128)(2,1)S(1)}, bf16[2,128,512]{2,1,0:T(8,128)(2,1)S(1)}, u32[]{:S(2)}, u32[]{:S(2)}) collective-permute-start(bf16[2,128,512]{2,1,0:T(8,128)(2,1)S(1)} %get-tuple-element.30), channel_id=1, source_target_pairs={{0,16},{1,13},{2,18},{3,15},{4,20},{5,17},{6,22},{7,19},{8,24},{9,... | collective-permute-start | bytes 786440 | tf_op jit(solution)/shard_map/ppermute | solution.py:225
  40.4 2.3 %collective-permute-start.6 = (bf16[2,128,512]{2,1,0:T(8,128)(2,1)S(1)}, bf16[2,128,512]{2,1,0:T(8,128)(2,1)S(1)}, u32[]{:S(2)}, u32[]{:S(2)}) collective-permute-start(bf16[2,128,512]{2,1,0:T(8,128)(2,1)S(1)} %get-tuple-element.32.refs_2_), channel_id=1, source_target_pairs={{0,1},{1,0},{2,3},{3,2},{4,5},{5,4},{6,7},{7,6},{8,9},{9,8},{10,11... | collective-permute-start | bytes 786440 | tf_op jit(solution)/shard_map/ppermute | solution.py:228
  40.5 5.9 %collective-permute-start.7 = (bf16[4,64,256]{2,1,0:T(8,128)(2,1)S(1)}, bf16[4,64,256]{2,1,0:T(8,128)(2,1)S(1)}, u32[]{:S(2)}, u32[]{:S(2)}) collective-permute-start(bf16[4,64,256]{2,1,0:T(8,128)(2,1)S(1)} %get-tuple-element.36), channel_id=1, source_target_pairs={{0,3},{1,2},{2,1},{3,0},{4,7},{5,6},{6,5},{7,4},{8,11},{9,10},{10,... | collective-permute-start | bytes 393224 | tf_op jit(solution)/shard_map/ppermute | solution.py:228
  41.8 7.2 %collective-permute-start.8 = (bf16[4,64,256]{2,1,0:T(8,128)(2,1)S(1)}, bf16[4,64,256]{2,1,0:T(8,128)(2,1)S(1)}, u32[]{:S(2)}, u32[]{:S(2)}) collective-permute-start(bf16[4,64,256]{2,1,0:T(8,128)(2,1)S(1)} %get-tuple-element.37), channel_id=1, source_target_pairs={{0,2},{1,3},{2,0},{3,1},{4,6},{5,7},{6,4},{7,5},{8,10},{9,11},{10,... | collective-permute-start | bytes 393224 | tf_op jit(solution)/shard_map/ppermute | solution.py:228
  42.3 6.6 %collective-permute-start.9 = (bf16[4,64,256]{2,1,0:T(8,128)(2,1)S(1)}, bf16[4,64,256]{2,1,0:T(8,128)(2,1)S(1)}, u32[]{:S(2)}, u32[]{:S(2)}) collective-permute-start(bf16[4,64,256]{2,1,0:T(8,128)(2,1)S(1)} %get-tuple-element.38), channel_id=1, source_target_pairs={{0,1},{1,0},{2,3},{3,2},{4,5},{5,4},{6,7},{7,6},{8,9},{9,8},{10,11... | collective-permute-start | bytes 393224 | tf_op jit(solution)/shard_map/ppermute | solution.py:228

commit v4 on v3

--- a/solution.py
+++ b/solution.py
@@ -62,10 +62,9 @@
     return jnp.concatenate([weight_ref[dy, dx] for dy in taps for dx in range(3)], axis=0)
 
 
-def local_rows_kernel(frames_ref, weight_ref, proj_ref, lower_ref, partial_ref, picker_ref, gram_ref, pick_ref):
+def local_rows_kernel(frames_ref, weight_ref, lower_ref, partial_ref, picker_ref, pick_ref):
     _, rows, channels, columns = frames_ref.shape
     half = columns // 2
-    mid = weight_ref.shape[3]
     picker_ref[...] = column_picker(columns)
     flat = frames_ref[...].reshape(2 * rows * channels, columns)
     pick_ref[...] = product(flat, picker_ref[...]).astype(BF16).reshape(pick_ref.shape)
@@ -76,9 +75,16 @@
     lower = product(stacked_weight(weight_ref, range(3)), gathered(picked, (1, 2, 3), half), TN)
     lower_ref[...] = jnp.maximum(lower, 0.0).astype(BF16)
     partial_ref[...] = product(stacked_weight(weight_ref, (1, 2)), gathered(picked, (0, 1), half), TN)
-    gram_high, gram_low = halves(product(proj_ref[...], proj_ref[...], NT))
-    gram_ref[:mid, :] = gram_high
-    gram_ref[mid:, :] = gram_low
+
+
+def step_offsets(band):
+    even, odd = BAND_REACH, BAND_REACH - 1
+    table = []
+    for p in range(band):
+        far = odd if p % 2 else even
+        sign = -1 if (p % 2 + p // 2) % 2 else 1
+        table.append([sign * far, sign * (far - 2), -sign * far, -sign * (far - 2)])
+    return table
 
 
 def held_class(band, start_ref, count_ref, offsets, slots):
@@ -87,12 +93,17 @@
     start = start_ref[0]
     swap = lax.rem(start + 2 * BAND_REACH, 2)
     slot_of = [j * band + place - core + lax.rem(core + swap, 2) for j in range(slots)]
-    steps = [jnp.where(core == 0, even, odd) for even, odd in zip(*offsets)]
+    steps = []
+    for choices in zip(*offsets):
+        step = choices[-1]
+        for p in range(len(choices) - 1):
+            step = jnp.where(place == p, choices[p], step)
+        steps.append(step)
     return swap == 0, [start + k for k in slot_of], [k < count_ref[0] for k in slot_of], steps
 
 
 def target_kernel(
-    band, offsets, factor, start_ref, count_ref, rim_ref, weight_ref, lower_ref, partial_ref, picker_ref, gram_ref,
+    band, offsets, factor, start_ref, count_ref, rim_ref, weight_ref, lower_ref, partial_ref, picker_ref, proj_ref,
     grad_ref, other_ref, spread_ref, target_ref, scaled_ref, own_ref, *refs
 ):
     message_refs, tile_ref = refs[:-1], refs[-1]
@@ -109,7 +120,8 @@
     upper = jnp.maximum(upper, 0.0).astype(BF16)
     source = jnp.concatenate([upper[:, :half], lower_ref[:, :half]], axis=1)
     target = jnp.concatenate([upper[:, half:], lower_ref[:, half:]], axis=1)
-    both = product(gram_ref[...], source)
+    gram = product(proj_ref[...], proj_ref[...], NT)
+    both = product(jnp.concatenate(halves(gram), axis=0), source)
     high, low = halves((both[:mid] + both[mid:]) * factor)
     scaled_ref[:mid, :] = high
     scaled_ref[mid : 2 * mid, :] = low
@@ -210,16 +222,14 @@
     vmem = pl.BlockSpec(memory_space=pltpu.VMEM)
     spread = jnp.asarray(spread_matrix(pixels))
 
-    offsets = ([], [])
-    for reach in range(1, BAND_REACH + 1):
-        offsets[reach % 2].extend([reach, -reach])
+    offsets = step_offsets(band)
     steps = len(offsets[0])
 
     def along_rows(x, step):
         pairs = []
         for row in range(row_blocks):
             for p in range(band):
-                to = row - offsets[p % 2][step]
+                to = row - offsets[p][step]
                 if 0 <= to < row_blocks:
                     pairs.append((row * band + p, to * band + p))
         return lax.ppermute(x, ("rows", "band"), pairs)
@@ -229,18 +239,17 @@
 
     rim = lax.ppermute(frames[:, -1:], "rows", [(i, i + 1) for i in range(row_blocks - 1)])
     other_grad = across(grad, 1)
-    lower, partial, picker, gram = pl.pallas_call(
+    lower, partial, picker = pl.pallas_call(
         local_rows_kernel,
         out_shape=(
             jax.ShapeDtypeStruct((mid, columns), BF16),
             jax.ShapeDtypeStruct((mid, columns), F32),
             jax.ShapeDtypeStruct((columns, 3 * half), BF16),
-            jax.ShapeDtypeStruct((2 * mid, mid), BF16),
         ),
         scratch_shapes=[pltpu.VMEM(frames.shape[:3] + (3 * half,), BF16)],
         compiler_params=params,
         cost_estimate=pl.CostEstimate(flops=2**31, bytes_accessed=2**21, transcendentals=0),
-    )(frames, conv_weight, proj_weight)
+    )(frames, conv_weight)
 
     block = jax.ShapeDtypeStruct((mid, pixels), BF16)
     message = jax.ShapeDtypeStruct((2, mid, pixels), BF16)
@@ -251,7 +260,7 @@
         scratch_shapes=[pltpu.VMEM((slots, mid, pixels), BF16)],
         compiler_params=params,
         cost_estimate=pl.CostEstimate(flops=2**31, bytes_accessed=2**22, transcendentals=0),
-    )(band_start, band_count, rim, conv_weight, lower, partial, picker, gram, grad, other_grad, spread)
+    )(band_start, band_count, rim, conv_weight, lower, partial, picker, proj_weight, grad, other_grad, spread)
 
     arrived = [along_rows(messages[i], i) for i in range(steps)]
 

time: 49.9 us -> 46.7 us (0.936)
  the two profiles are of different devices: /device:TPU:25 before, /device:TPU:19 now
where the time goes in v4:
time: 46.7 us; the launch traced here: 45.9 us
  waiting for transfers between devices  19.3 us (41%)
  starting transfers between devices  16.4 us (35%)
  Pallas kernels  4.27 us (9%)
  local copies, waits for them, and re-layouts  3.73 us (8%)
  between operations  2.05 us (4%)
    ppermute x4, waiting for transfers between devices, along_rows(): return lax.ppermute(x, ('rows', 'band'), pairs)  13.1 us
    ppermute x4, starting transfers between devices, along_rows(): return lax.ppermute(x, ('rows', 'band'), pairs)  10.3 us
    ppermute x5, waiting for transfers between devices, across(): return lax.ppermute(x, 'band', [(p, p ^ k) for p in range(band)])  4.91 us
    ppermute x1, starting transfers between devices, shards(): lax.ppermute(frames[:, -1:], 'rows', [(i, i + 1) for i in range(row_block...  3.15 us
    ppermute x5, starting transfers between devices, across(): return lax.ppermute(x, 'band', [(p, p ^ k) for p in range(band)])  3.01 us
    unnamed x12, local copies, waits for them, and re-layouts  2.08 us
    pallas_call x1, Pallas kernels, shards(): pl.pallas_call(local_rows_kernel, out_shape=(jax.ShapeDtypeStruct((mid, c...  1.46 us
    pallas_call x1, Pallas kernels, shards(): pl.pallas_call(lambda *refs: pyramid_kernel(band, *refs), grid=(slots,),...  1.33 us
  transfers between devices with their start and end apart: 10, of which 6 were waited for; matrix products, arithmetic and copies ran while one was open for 2% of the time, Pallas kernels for 6%

profile of v4, /device:TPU:19, one launch (start us, length us, event | category | flops | bytes accessed | tf_op | source)
XLA Modules:
  0.0 45.9 jit_solution(8483254853256406549)
XLA Ops:
  0.6 0.7 %collective-permute-start = (bf16[1,2,1,960,512]{4,3,2,1,0:T(8,128)(2,1)}, bf16[1,2,1,960,512]{4,3,2,1,0:T(8,128)(2,1)S(1)}, u32[]{:S(2)}, u32[]{:S(2)}) collective-permute-start(bf16[1,2,1,960,512]{4,3,2,1,0:T(8,128)(2,1)} %bitcast.7), channel_id=1, source_target_pairs={{0,1},{1,0},{2,3},{3,2},{4,5},{5,4},{6,7},{7,6},{8,9},{9,8},{10,11... | collective-permute-start | bytes 5898248 | tf_op jit(solution)/shard_map/ppermute | solution.py:238
  1.4 0.9 %slice.12 = bf16[2,1,96,512]{3,2,1,0:T(8,128)(2,1)S(1)} slice(bf16[2,4,96,512]{3,2,1,0:T(8,128)(2,1)} %bitcast.5), slice={[0:2], [3:4], [0:96], [0:512]} | slice | bytes 393216 | tf_op jit(solution)/shard_map/slice | solution.py:240
  2.3 3.1 %collective-permute-start.1 = (bf16[2,1,96,512]{3,2,1,0:T(8,128)(2,1)S(1)}, bf16[2,1,96,512]{3,2,1,0:T(8,128)(2,1)S(1)}, u32[]{:S(2)}, u32[]{:S(2)}) collective-permute-start(bf16[2,1,96,512]{3,2,1,0:T(8,128)(2,1)S(1)} %slice.12), channel_id=1, source_target_pairs={{0,4},{4,8},{8,12},{12,16},{16,20},{20,24},{24,28},{1,5},{5,9},{9,... | collective-permute-start | bytes 589832 | tf_op jit(solution)/shard_map/ppermute | solution.py:240
  6.8 0.0 copy-start
  6.8 1.1 %copy-done = bf16[2,4,512,96]{2,3,1,0:T(8,128)(2,1)S(1)} copy-done((bf16[2,4,512,96]{2,3,1,0:T(8,128)(2,1)S(1)}, bf16[2,4,512,96]{2,3,1,0:T(8,128)(2,1)}, u32[]{:S(2)}) %copy-start) | copy-done | bytes 786456
  7.9 0.0 copy-start.2
  7.9 0.9 %copy-done.2 = bf16[3,3,96,128]{3,2,1,0:T(8,128)(2,1)S(1)} copy-done((bf16[3,3,96,128]{3,2,1,0:T(8,128)(2,1)S(1)}, bf16[3,3,96,128]{3,2,1,0:T(8,128)(2,1)}, u32[]{:S(2)}) %copy-start.2) | copy-done | bytes 221208
  8.8 0.0 copy-start.1
  8.8 0.0 copy-start.3
  8.8 0.0 copy-start.4
  8.8 0.0 copy-start.5
  8.8 1.5 %shard_map.94 = (bf16[128,512]{1,0:T(8,128)(2,1)S(1)}, f32[128,512]{1,0:T(8,128)S(1)}, bf16[512,768]{1,0:T(8,128)(2,1)S(1)}) custom-call(bf16[2,4,96,512]{3,2,1,0:T(8,128)(2,1)S(1)} %bitcast.6, bf16[3,3,96,128]{3,2,1,0:T(8,128)(2,1)S(1)} %copy-done.2), custom_call_target="tpu_custom_call" | custom-call | flops 2147483648 | bytes 2097152 | tf_op jit(solution)/shard_map/pallas_call | solution.py:242
  10.3 1.3 %collective-permute-done.1.refs_2_ = bf16[2,1,96,512]{3,2,1,0:T(8,128)(2,1)S(1)} collective-permute-done((bf16[2,1,96,512]{3,2,1,0:T(8,128)(2,1)S(1)}, bf16[2,1,96,512]{3,2,1,0:T(8,128)(2,1)S(1)}, u32[]{:S(2)}, u32[]{:S(2)}) %collective-permute-start.1) | collective-permute-done | bytes 196640 | tf_op jit(solution)/shard_map/ppermute | solution.py:240
  11.6 0.0 collective-permute-done.refs_9_.refs_3_
  11.6 0.0 copy-done.1
  11.6 0.0 copy-done.3
  11.6 0.0 copy-done.4
  11.6 0.0 copy-done.5
  11.6 0.8 %shard_map.95 = (bf16[128,512]{1,0:T(8,128)(2,1)S(1)}, bf16[384,512]{1,0:T(8,128)(2,1)S(1)}, bf16[128,512]{1,0:T(8,128)(2,1)S(1)}, bf16[2,128,512]{2,1,0:T(8,128...) custom-call(s32[1]{0:T(128)S(6)} %copy.10.refs_0_, ...), custom_call_target="tpu_custom_call" | custom-call | flops 2147483648 | bytes 4194304 | tf_op jit(solution)/shard_map/pallas_call | solution.py:256
  12.5 2.7 %collective-permute-start.2 = (bf16[2,128,512]{2,1,0:T(8,128)(2,1)S(1)}, bf16[2,128,512]{2,1,0:T(8,128)(2,1)S(1)}, u32[]{:S(2)}, u32[]{:S(2)}) collective-permute-start(bf16[2,128,512]{2,1,0:T(8,128)(2,1)S(1)} %get-tuple-element.25), channel_id=1, source_target_pairs={{1,13},{2,18},{5,17},{6,22},{9,21},{10,26},{13,25},{14,30},{15,3},... | collective-permute-start | bytes 786440 | tf_op jit(solution)/shard_map/ppermute | solution.py:235
  15.2 2.1 %collective-permute-start.3 = (bf16[2,128,512]{2,1,0:T(8,128)(2,1)S(1)}, bf16[2,128,512]{2,1,0:T(8,128)(2,1)S(1)}, u32[]{:S(2)}, u32[]{:S(2)}) collective-permute-start(bf16[2,128,512]{2,1,0:T(8,128)(2,1)S(1)} %get-tuple-element.26), channel_id=1, source_target_pairs={{1,5},{2,10},{5,9},{6,14},{7,3},{8,0},{9,13},{10,18},{11,7},{12,4}... | collective-permute-start | bytes 786440 | tf_op jit(solution)/shard_map/ppermute | solution.py:235
  17.3 3.5 %collective-permute-start.4 = (bf16[2,128,512]{2,1,0:T(8,128)(2,1)S(1)}, bf16[2,128,512]{2,1,0:T(8,128)(2,1)S(1)}, u32[]{:S(2)}, u32[]{:S(2)}) collective-permute-start(bf16[2,128,512]{2,1,0:T(8,128)(2,1)S(1)} %get-tuple-element.27), channel_id=1, source_target_pairs={{0,16},{3,15},{4,20},{7,19},{8,24},{11,23},{12,28},{13,1},{15,27},... | collective-permute-start | bytes 786440 | tf_op jit(solution)/shard_map/ppermute | solution.py:235
  20.8 1.9 %collective-permute-start.5 = (bf16[2,128,512]{2,1,0:T(8,128)(2,1)S(1)}, bf16[2,128,512]{2,1,0:T(8,128)(2,1)S(1)}, u32[]{:S(2)}, u32[]{:S(2)}) collective-permute-start(bf16[2,128,512]{2,1,0:T(8,128)(2,1)S(1)} %get-tuple-element.28), channel_id=1, source_target_pairs={{0,8},{3,7},{4,12},{5,1},{7,11},{8,16},{9,5},{10,2},{11,15},{12,20... | collective-permute-start | bytes 786440 | tf_op jit(solution)/shard_map/ppermute | solution.py:235
  22.8 0.0 collective-permute-done.2.refs_8_
  22.8 5.4 %collective-permute-done.3.refs_9_ = bf16[2,128,512]{2,1,0:T(8,128)(2,1)S(1)} collective-permute-done((bf16[2,128,512]{2,1,0:T(8,128)(2,1)S(1)}, bf16[2,128,512]{2,1,0:T(8,128)(2,1)S(1)}, u32[]{:S(2)}, u32[]{:S(2)}) %collective-permute-start.3) | collective-permute-done | bytes 262176 | tf_op jit(solution)/shard_map/ppermute | solution.py:235
  28.2 0.4 collective-permute-done.4.refs_10_
  28.6 7.3 %collective-permute-done.5.refs_11_ = bf16[2,128,512]{2,1,0:T(8,128)(2,1)S(1)} collective-permute-done((bf16[2,128,512]{2,1,0:T(8,128)(2,1)S(1)}, bf16[2,128,512]{2,1,0:T(8,128)(2,1)S(1)}, u32[]{:S(2)}, u32[]{:S(2)}) %collective-permute-start.5) | collective-permute-done | bytes 262176 | tf_op jit(solution)/shard_map/ppermute | solution.py:235
  35.9 0.6 %shard_map.96 = (bf16[2,128,512]{2,1,0:T(8,128)(2,1)S(1)}, f32[4,64,256]{2,1,0:T(8,128)S(1)}, bf16[4,64,256]{2,1,0:T(8,128)(2,1)S(1)}, bf16[4,64,256]{2,1,0:T(8,128)(2,1)S(1)}, bf16[4,64,256]{2,1,0:T(8,128)(2,1)S(1)}) custom-call(s32[1]{0:T(128)S(6)} %copy.10.refs_0_, s32[1]{0:T(128)S(6)} %copy.11.refs_1_, bf16[1,2,1,960,512]{4,3,2,1,0:T(8,128)(2,1)S(1)} %bitcast.9, ...), custom_call_target="tpu_custom_call" | custom-call | flops 2147483648 | bytes 4194304 | tf_op jit(solution)/shard_map/pallas_call | solution.py:269
  36.6 0.1 collective-permute-start.6
  36.6 0.1 collective-permute-start.7
  36.7 1.8 %collective-permute-start.8 = (bf16[4,64,256]{2,1,0:T(8,128)(2,1)S(1)}, bf16[4,64,256]{2,1,0:T(8,128)(2,1)S(1)}, u32[]{:S(2)}, u32[]{:S(2)}) collective-permute-start(bf16[4,64,256]{2,1,0:T(8,128)(2,1)S(1)} %get-tuple-element.35), channel_id=1, source_target_pairs={{0,2},{1,3},{2,0},{3,1},{4,6},{5,7},{6,4},{7,5},{8,10},{9,11},{10,... | collective-permute-start | bytes 393224 | tf_op jit(solution)/shard_map/ppermute | solution.py:238
  38.5 0.3 collective-permute-start.9
  38.9 0.0 collective-permute-done.6.refs_3_
  38.9 1.3 %shard_map.97 = bf16[1,2,1,960,512]{4,3,2,1,0:T(8,128)(2,1)} custom-call(s32[1]{0:T(128)S(6)} %copy.10.refs_0_, s32[1]{0:T(128)S(6)} %copy.11.refs_1_, bf16[2,128,512]{2,1,0:T(8,128)(2,1)S(1)} %get-tuple-element.30.refs_2_, bf16[2,128,512]{2,1,0:T(8,128)(2,1)S(1)} %collective-permute-done.6.refs_3_, bf16[384,512]{1,0:T(8,128)(2,1)S(1)} %get-tuple-element.31.refs_4_, ...), custom_call_target="tpu_custom_call" | custom-call | flops 2147483648 | bytes 4194304 | tf_op jit(solution)/shard_map/pallas_call | solution.py:287
  40.2 2.3 %collective-permute-done.7 = bf16[4,64,256]{2,1,0:T(8,128)(2,1)S(1)} collective-permute-done((bf16[4,64,256]{2,1,0:T(8,128)(2,1)S(1)}, bf16[4,64,256]{2,1,0:T(8,128)(2,1)S(1)}, u32[]{:S(2)}, u32[]{:S(2)}) %collective-permute-start.7) | collective-permute-done | bytes 131104 | tf_op jit(solution)/shard_map/ppermute | solution.py:238
  42.5 2.6 %collective-permute-done.8 = bf16[4,64,256]{2,1,0:T(8,128)(2,1)S(1)} collective-permute-done((bf16[4,64,256]{2,1,0:T(8,128)(2,1)S(1)}, bf16[4,64,256]{2,1,0:T(8,128)(2,1)S(1)}, u32[]{:S(2)}, u32[]{:S(2)}) %collective-permute-start.8) | collective-permute-done | bytes 131104 | tf_op jit(solution)/shard_map/ppermute | solution.py:238
  45.1 0.0 collective-permute-done.9
  45.1 0.1 add_bitcast_fusion
  45.2 0.7 %fusion = (f32[2,256,64]{1,2,0:T(8,128)}, f32[2,256,64]{1,2,0:T(8,128)}) fusion(f32[4,256,64]{1,2,0:T(8,128)S(1)} %add_bitcast_fusion), kind=kLoop, calls=%fused_computation.1 | loop fusion | bytes 524288 | tf_op jit(solution)/shard_map/slice | solution.py:301
Async XLA Ops:
  0.6 11.0 %collective-permute-start = (bf16[1,2,1,960,512]{4,3,2,1,0:T(8,128)(2,1)}, bf16[1,2,1,960,512]{4,3,2,1,0:T(8,128)(2,1)S(1)}, u32[]{:S(2)}, u32[]{:S(2)}) collective-permute-start(bf16[1,2,1,960,512]{4,3,2,1,0:T(8,128)(2,1)} %bitcast.7), channel_id=1, source_target_pairs={{0,1},{1,0},{2,3},{3,2},{4,5},{5,4},{6,7},{7,6},{8,9},{9,8},{10,11... | collective-permute-start | bytes 5898248 | tf_op jit(solution)/shard_map/ppermute | solution.py:238
  2.3 9.3 %collective-permute-start.1 = (bf16[2,1,96,512]{3,2,1,0:T(8,128)(2,1)S(1)}, bf16[2,1,96,512]{3,2,1,0:T(8,128)(2,1)S(1)}, u32[]{:S(2)}, u32[]{:S(2)}) collective-permute-start(bf16[2,1,96,512]{3,2,1,0:T(8,128)(2,1)S(1)} %slice.12), channel_id=1, source_target_pairs={{0,4},{4,8},{8,12},{12,16},{16,20},{20,24},{24,28},{1,5},{5,9},{9,... | collective-permute-start | bytes 589832 | tf_op jit(solution)/shard_map/ppermute | solution.py:240
  6.8 1.1 %copy-start = (bf16[2,4,512,96]{2,3,1,0:T(8,128)(2,1)S(1)}, bf16[2,4,512,96]{2,3,1,0:T(8,128)(2,1)}, u32[]{:S(2)}) copy-start(bf16[2,4,512,96]{2,3,1,0:T(8,128)(2,1)} %param.7) | copy-start | bytes 2359300
  7.9 0.9 %copy-start.2 = (bf16[3,3,96,128]{3,2,1,0:T(8,128)(2,1)S(1)}, bf16[3,3,96,128]{3,2,1,0:T(8,128)(2,1)}, u32[]{:S(2)}) copy-start(bf16[3,3,96,128]{3,2,1,0:T(8,128)(2,1)} %refs_3_.1) | copy-start | bytes 663556
  8.8 2.8 %copy-start.1 = (bf16[1,2,1,512,960]{3,4,2,1,0:T(8,128)(2,1)S(1)}, bf16[1,2,1,512,960]{3,4,2,1,0:T(8,128)(2,1)}, u32[]{:S(2)}) copy-start(bf16[1,2,1,512,960]{3,4,2,1,0:T(8,128)(2,1)} %param.12) | copy-start | bytes 5898244
  8.8 2.8 %copy-start.3 = (bf16[3,3,96,128]{3,2,1,0:T(8,128)(2,1)S(1)}, bf16[3,3,96,128]{3,2,1,0:T(8,128)(2,1)}, u32[]{:S(2)}) copy-start(bf16[3,3,96,128]{3,2,1,0:T(8,128)(2,1)} %refs_3_.1) | copy-start | bytes 663556
  8.8 2.8 %copy-start.4 = (bf16[128,256]{1,0:T(8,128)(2,1)S(1)}, bf16[128,256]{1,0:T(8,128)(2,1)}, u32[]{:S(2)}) copy-start(bf16[128,256]{1,0:T(8,128)(2,1)} %refs_5_.2) | copy-start | bytes 196612
  8.8 2.8 %copy-start.5 = (bf16[960,512]{1,0:T(8,128)(2,1)S(1)}, bf16[960,512]{1,0:T(8,128)(2,1)}, u32[]{:S(2)}) copy-start(bf16[960,512]{1,0:T(8,128)(2,1)} %constant.2.clone.refs_10_.refs_4_.refs_5_) | copy-start | bytes 2949124
  12.5 10.3 %collective-permute-start.2 = (bf16[2,128,512]{2,1,0:T(8,128)(2,1)S(1)}, bf16[2,128,512]{2,1,0:T(8,128)(2,1)S(1)}, u32[]{:S(2)}, u32[]{:S(2)}) collective-permute-start(bf16[2,128,512]{2,1,0:T(8,128)(2,1)S(1)} %get-tuple-element.25), channel_id=1, source_target_pairs={{1,13},{2,18},{5,17},{6,22},{9,21},{10,26},{13,25},{14,30},{15,3},... | collective-permute-start | bytes 786440 | tf_op jit(solution)/shard_map/ppermute | solution.py:235
  15.2 13.0 %collective-permute-start.3 = (bf16[2,128,512]{2,1,0:T(8,128)(2,1)S(1)}, bf16[2,128,512]{2,1,0:T(8,128)(2,1)S(1)}, u32[]{:S(2)}, u32[]{:S(2)}) collective-permute-start(bf16[2,128,512]{2,1,0:T(8,128)(2,1)S(1)} %get-tuple-element.26), channel_id=1, source_target_pairs={{1,5},{2,10},{5,9},{6,14},{7,3},{8,0},{9,13},{10,18},{11,7},{12,4}... | collective-permute-start | bytes 786440 | tf_op jit(solution)/shard_map/ppermute | solution.py:235
  17.3 11.3 %collective-permute-start.4 = (bf16[2,128,512]{2,1,0:T(8,128)(2,1)S(1)}, bf16[2,128,512]{2,1,0:T(8,128)(2,1)S(1)}, u32[]{:S(2)}, u32[]{:S(2)}) collective-permute-start(bf16[2,128,512]{2,1,0:T(8,128)(2,1)S(1)} %get-tuple-element.27), channel_id=1, source_target_pairs={{0,16},{3,15},{4,20},{7,19},{8,24},{11,23},{12,28},{13,1},{15,27},... | collective-permute-start | bytes 786440 | tf_op jit(solution)/shard_map/ppermute | solution.py:235
  20.8 15.1 %collective-permute-start.5 = (bf16[2,128,512]{2,1,0:T(8,128)(2,1)S(1)}, bf16[2,128,512]{2,1,0:T(8,128)(2,1)S(1)}, u32[]{:S(2)}, u32[]{:S(2)}) collective-permute-start(bf16[2,128,512]{2,1,0:T(8,128)(2,1)S(1)} %get-tuple-element.28), channel_id=1, source_target_pairs={{0,8},{3,7},{4,12},{5,1},{7,11},{8,16},{9,5},{10,2},{11,15},{12,20... | collective-permute-start | bytes 786440 | tf_op jit(solution)/shard_map/ppermute | solution.py:235
  36.6 2.3 %collective-permute-start.6 = (bf16[2,128,512]{2,1,0:T(8,128)(2,1)S(1)}, bf16[2,128,512]{2,1,0:T(8,128)(2,1)S(1)}, u32[]{:S(2)}, u32[]{:S(2)}) collective-permute-start(bf16[2,128,512]{2,1,0:T(8,128)(2,1)S(1)} %get-tuple-element.30.refs_2_), channel_id=1, source_target_pairs={{0,1},{1,0},{2,3},{3,2},{4,5},{5,4},{6,7},{7,6},{8,9},{9,8},{10,11... | collective-permute-start | bytes 786440 | tf_op jit(solution)/shard_map/ppermute | solution.py:238
  36.6 5.9 %collective-permute-start.7 = (bf16[4,64,256]{2,1,0:T(8,128)(2,1)S(1)}, bf16[4,64,256]{2,1,0:T(8,128)(2,1)S(1)}, u32[]{:S(2)}, u32[]{:S(2)}) collective-permute-start(bf16[4,64,256]{2,1,0:T(8,128)(2,1)S(1)} %get-tuple-element.34), channel_id=1, source_target_pairs={{0,3},{1,2},{2,1},{3,0},{4,7},{5,6},{6,5},{7,4},{8,11},{9,10},{10,... | collective-permute-start | bytes 393224 | tf_op jit(solution)/shard_map/ppermute | solution.py:238
  36.7 8.4 %collective-permute-start.8 = (bf16[4,64,256]{2,1,0:T(8,128)(2,1)S(1)}, bf16[4,64,256]{2,1,0:T(8,128)(2,1)S(1)}, u32[]{:S(2)}, u32[]{:S(2)}) collective-permute-start(bf16[4,64,256]{2,1,0:T(8,128)(2,1)S(1)} %get-tuple-element.35), channel_id=1, source_target_pairs={{0,2},{1,3},{2,0},{3,1},{4,6},{5,7},{6,4},{7,5},{8,10},{9,11},{10,... | collective-permute-start | bytes 393224 | tf_op jit(solution)/shard_map/ppermute | solution.py:238
  38.5 6.6 %collective-permute-start.9 = (bf16[4,64,256]{2,1,0:T(8,128)(2,1)S(1)}, bf16[4,64,256]{2,1,0:T(8,128)(2,1)S(1)}, u32[]{:S(2)}, u32[]{:S(2)}) collective-permute-start(bf16[4,64,256]{2,1,0:T(8,128)(2,1)S(1)} %get-tuple-element.36), channel_id=1, source_target_pairs={{0,1},{1,0},{2,3},{3,2},{4,5},{5,4},{6,7},{7,6},{8,9},{9,8},{10,11... | collective-permute-start | bytes 393224 | tf_op jit(solution)/shard_map/ppermute | solution.py:238

commit v5 on v4

--- a/solution.py
+++ b/solution.py
@@ -62,10 +62,13 @@
     return jnp.concatenate([weight_ref[dy, dx] for dy in taps for dx in range(3)], axis=0)
 
 
-def local_rows_kernel(frames_ref, weight_ref, lower_ref, partial_ref, picker_ref, pick_ref):
+def picker_kernel(picker_ref):
+    picker_ref[...] = column_picker(picker_ref.shape[0])
+
+
+def local_rows_kernel(picker_ref, frames_ref, weight_ref, lower_ref, partial_ref, pick_ref):
     _, rows, channels, columns = frames_ref.shape
     half = columns // 2
-    picker_ref[...] = column_picker(columns)
     flat = frames_ref[...].reshape(2 * rows * channels, columns)
     pick_ref[...] = product(flat, picker_ref[...]).astype(BF16).reshape(pick_ref.shape)
 
@@ -77,34 +80,52 @@
     partial_ref[...] = product(stacked_weight(weight_ref, (1, 2)), gathered(picked, (0, 1), half), TN)
 
 
-def step_offsets(band):
-    even, odd = BAND_REACH, BAND_REACH - 1
-    table = []
-    for p in range(band):
-        far = odd if p % 2 else even
-        sign = -1 if (p % 2 + p // 2) % 2 else 1
-        table.append([sign * far, sign * (far - 2), -sign * far, -sign * (far - 2)])
-    return table
-
-
-def held_class(band, start_ref, count_ref, offsets, slots):
+def step_table(band):
+    even = [(4, 0), (2, 0), (2, 1), (4, 1)]
+    odd = [(3, 0), (1, 0), (3, 1), (1, 1)]
+    table = [even, odd]
+    return [table[p % len(table)] for p in range(band)]
+
+
+SPLIT_BLOCKS = (0,)
+SPLIT_TERMS = (2, 3)
+
+
+def pixel_halves(block):
+    width = block.shape[1] // 2
+    return block[:, :width], block[:, width:]
+
+
+def own_half(block, swapped=False):
+    first, second = pixel_halves(block)
+    return jnp.where((lax.div(lax.axis_index("band"), 2) == 0) != swapped, first, second)
+
+
+def joined(mine, others):
+    is_first = lax.div(lax.axis_index("band"), 2) == 0
+    return jnp.concatenate([jnp.where(is_first, mine, others), jnp.where(is_first, others, mine)], axis=1)
+
+
+def held_class(band, start_ref, count_ref, table, slots):
     place = lax.axis_index("band")
     core = lax.rem(place, 2)
     start = start_ref[0]
     swap = lax.rem(start + 2 * BAND_REACH, 2)
     slot_of = [j * band + place - core + lax.rem(core + swap, 2) for j in range(slots)]
+    row = lax.axis_index("rows")
     steps = []
-    for choices in zip(*offsets):
-        step = choices[-1]
-        for p in range(len(choices) - 1):
-            step = jnp.where(place == p, choices[p], step)
+    for choices in zip(*table):
+        step = 0
+        for p, (distance, turn) in enumerate(choices):
+            lower = lax.rem(lax.div(row, distance), 2) == turn
+            step = jnp.where(place == p, jnp.where(lower, distance, -distance), step)
         steps.append(step)
     return swap == 0, [start + k for k in slot_of], [k < count_ref[0] for k in slot_of], steps
 
 
 def target_kernel(
-    band, offsets, factor, start_ref, count_ref, rim_ref, weight_ref, lower_ref, partial_ref, picker_ref, proj_ref,
-    grad_ref, other_ref, spread_ref, target_ref, scaled_ref, own_ref, *refs
+    band, table, factor, start_ref, count_ref, rim_ref, weight_ref, lower_ref, partial_ref, picker_ref, proj_ref,
+    grad_ref, other_ref, spread_ref, target_ref, scaled_ref, own_ref, kept_ref, crossing_ref, *refs
 ):
     message_refs, tile_ref = refs[:-1], refs[-1]
     half = lower_ref.shape[1] // 2
@@ -126,7 +147,7 @@
     scaled_ref[:mid, :] = high
     scaled_ref[mid : 2 * mid, :] = low
     scaled_ref[2 * mid :, :] = high
-    same, held, active, steps = held_class(band, start_ref, count_ref, offsets, slots)
+    same, held, active, steps = held_class(band, start_ref, count_ref, table, slots)
 
     def term(slot, block_ref):
         high, low = halves(product(source, block_ref[0, slot, 0], NT))
@@ -145,17 +166,28 @@
 
     target_ref[...] = target
     own_ref[...] = chosen(0)
-    for step, message_ref in zip(steps, message_refs):
-        message_ref[0] = target
-        message_ref[1] = chosen(-step)
+    for i, (step, message_ref) in enumerate(zip(steps, message_refs)):
+        blocks = [own_half(target)] if i in SPLIT_BLOCKS else pixel_halves(target)
+        tile = chosen(step)
+        if i in SPLIT_TERMS:
+            kept_ref[SPLIT_TERMS.index(i)] = own_half(tile)
+            crossing_ref[SPLIT_TERMS.index(i)] = own_half(tile, True)
+        else:
+            blocks = [*blocks, *pixel_halves(tile)]
+        for j, part in enumerate(blocks):
+            message_ref[j] = part
 
 
 def gradient_kernel(
-    band, offsets, factor, start_ref, count_ref, grad_ref, other_ref, spread_ref, proj_ref, target_ref, own_ref, *refs
+    band, table, factor, start_ref, count_ref, grad_ref, other_ref, spread_ref, proj_ref, target_ref, own_ref, *refs
 ):
-    arrived, (held_ref, kept_ref, *sent_refs, sum_ref, out_ref) = refs[: len(offsets[0])], refs[len(offsets[0]) :]
+    arrived, others, (held_ref, kept_ref, *sent_refs, sum_ref, out_ref) = (
+        refs[: len(table[0])],
+        refs[len(table[0]) : len(table[0]) + len(SPLIT_BLOCKS)],
+        refs[len(table[0]) + len(SPLIT_BLOCKS) :],
+    )
     slots, mid, pixels = held_ref.shape
-    same, held, active, steps = held_class(band, start_ref, count_ref, offsets, slots)
+    same, held, active, steps = held_class(band, start_ref, count_ref, table, slots)
     sum_ref[...] = jnp.zeros(sum_ref.shape, F32)
 
     def add(slot, block_ref):
@@ -165,15 +197,25 @@
 
     for slot in range(slots):
         block = target_ref[...]
-        for step, part in zip(steps, arrived):
-            block = jnp.where(held[slot] == step, part[0], block)
+        for i, (step, part) in enumerate(zip(steps, arrived)):
+            if i in SPLIT_BLOCKS:
+                came = joined(part[0], others[SPLIT_BLOCKS.index(i)][...])
+            else:
+                came = jnp.concatenate([part[0], part[1]], axis=1)
+            block = jnp.where(held[slot] == step, came, block)
         held_ref[slot] = block
         pl.when(jnp.logical_and(active[slot], same))(lambda: add(slot, grad_ref))
         pl.when(jnp.logical_and(active[slot], jnp.logical_not(same)))(lambda: add(slot, other_ref))
 
     total = own_ref[...].astype(F32)
-    for part in arrived:
-        total = total + part[1].astype(F32)
+    nothing = jnp.zeros((mid, pixels // 2), BF16)
+    for i, part in enumerate(arrived):
+        last = part.shape[0] - 1
+        if i in SPLIT_TERMS:
+            came = joined(part[last], nothing)
+        else:
+            came = jnp.concatenate([part[last - 1], part[last]], axis=1)
+        total = total + came.astype(F32)
     high, low = halves(jnp.concatenate([sum_ref[...], total], axis=1))
     out_ref[...] = (product(proj_ref[...], high, TN) + product(proj_ref[...], low, TN)) * factor
     parts, share, width = kept_ref.shape
@@ -222,16 +264,17 @@
     vmem = pl.BlockSpec(memory_space=pltpu.VMEM)
     spread = jnp.asarray(spread_matrix(pixels))
 
-    offsets = step_offsets(band)
-    steps = len(offsets[0])
+    table = step_table(band)
+    steps = len(table[0])
 
     def along_rows(x, step):
         pairs = []
-        for row in range(row_blocks):
-            for p in range(band):
-                to = row - offsets[p][step]
-                if 0 <= to < row_blocks:
-                    pairs.append((row * band + p, to * band + p))
+        for p in range(band):
+            distance, turn = table[p][step]
+            for row in range(row_blocks - distance):
+                if row // distance % 2 == turn:
+                    pairs.append((row * band + p, (row + distance) * band + p))
+                    pairs.append(((row + distance) * band + p, row * band + p))
         return lax.ppermute(x, ("rows", "band"), pairs)
 
     def across(x, k):
@@ -239,42 +282,56 @@
 
     rim = lax.ppermute(frames[:, -1:], "rows", [(i, i + 1) for i in range(row_blocks - 1)])
     other_grad = across(grad, 1)
-    lower, partial, picker = pl.pallas_call(
+    picker = pl.pallas_call(
+        picker_kernel,
+        out_shape=jax.ShapeDtypeStruct((columns, 3 * half), BF16),
+        compiler_params=params,
+        cost_estimate=pl.CostEstimate(flops=2**33, bytes_accessed=2**21, transcendentals=0),
+    )()
+    lower, partial = pl.pallas_call(
         local_rows_kernel,
         out_shape=(
             jax.ShapeDtypeStruct((mid, columns), BF16),
             jax.ShapeDtypeStruct((mid, columns), F32),
-            jax.ShapeDtypeStruct((columns, 3 * half), BF16),
         ),
         scratch_shapes=[pltpu.VMEM(frames.shape[:3] + (3 * half,), BF16)],
         compiler_params=params,
         cost_estimate=pl.CostEstimate(flops=2**31, bytes_accessed=2**21, transcendentals=0),
-    )(frames, conv_weight)
+    )(picker, frames, conv_weight)
 
     block = jax.ShapeDtypeStruct((mid, pixels), BF16)
-    message = jax.ShapeDtypeStruct((2, mid, pixels), BF16)
-    target, scaled, own_term, *messages = pl.pallas_call(
-        lambda *refs: target_kernel(band, offsets, factor, *refs),
+    piece = (mid, pixels // 2)
+    crossing = jax.ShapeDtypeStruct((len(SPLIT_TERMS),) + piece, BF16)
+    messages = [
+        jax.ShapeDtypeStruct(((1 if i in SPLIT_BLOCKS else 2) + (0 if i in SPLIT_TERMS else 2),) + piece, BF16)
+        for i in range(steps)
+    ]
+    target, scaled, own_term, terms, crossing, *messages = pl.pallas_call(
+        lambda *refs: target_kernel(band, table, factor, *refs),
         in_specs=[smem] * 2 + [vmem] * 9,
-        out_shape=(block, jax.ShapeDtypeStruct((3 * mid, pixels), BF16), block) + (message,) * steps,
+        out_shape=(block, jax.ShapeDtypeStruct((3 * mid, pixels), BF16), block, crossing, crossing, *messages),
         scratch_shapes=[pltpu.VMEM((slots, mid, pixels), BF16)],
         compiler_params=params,
         cost_estimate=pl.CostEstimate(flops=2**31, bytes_accessed=2**22, transcendentals=0),
     )(band_start, band_count, rim, conv_weight, lower, partial, picker, proj_weight, grad, other_grad, spread)
 
+    others = across(crossing, 2)
+    for j, i in enumerate(SPLIT_TERMS):
+        messages[i] = jnp.concatenate([messages[i], terms[j : j + 1] + others[j : j + 1]])
     arrived = [along_rows(messages[i], i) for i in range(steps)]
+    other_blocks = [across(arrived[i][0], 2) for i in SPLIT_BLOCKS]
 
     out_parts = 2 * pixels // half
     part = (out_parts, share, half)
     held, kept, *sent = pl.pallas_call(
-        lambda *refs: gradient_kernel(band, offsets, factor, *refs),
-        in_specs=[smem] * 2 + [vmem] * (6 + steps),
+        lambda *refs: gradient_kernel(band, table, factor, *refs),
+        in_specs=[smem] * 2 + [vmem] * (6 + steps + len(SPLIT_BLOCKS)),
         out_shape=(jax.ShapeDtypeStruct((slots, mid, pixels), BF16), jax.ShapeDtypeStruct(part, F32))
         + (jax.ShapeDtypeStruct(part, BF16),) * (band - 1),
         scratch_shapes=[pltpu.VMEM((mid, pixels), F32), pltpu.VMEM((channels, 2 * pixels), F32)],
         compiler_params=params,
         cost_estimate=pl.CostEstimate(flops=2**31, bytes_accessed=2**22, transcendentals=0),
-    )(band_start, band_count, grad, other_grad, spread, proj_weight, target, own_term, *arrived)
+    )(band_start, band_count, grad, other_grad, spread, proj_weight, target, own_term, *arrived, *other_blocks)
 
     received = [across(sent[k - 1], k) for k in reversed(range(1, band))]
     other = across(held, 1)

time: 46.7 us -> 45.3 us (0.970)
  the two profiles are of different devices: /device:TPU:19 before, /device:TPU:17 now
where the time goes in v5:
time: 45.3 us; the launch traced here: 44.7 us
  starting transfers between devices  17 us (38%)
  waiting for transfers between devices  14 us (31%)
  Pallas kernels  8.83 us (19%)
  local copies, waits for them, and re-layouts  2.68 us (6%)
  between operations  2.05 us (5%)
    ppermute x4, starting transfers between devices, along_rows(): return lax.ppermute(x, ('rows', 'band'), pairs)  9.1 us
    ppermute x7, waiting for transfers between devices, across(): return lax.ppermute(x, 'band', [(p, p ^ k) for p in range(band)])  6.97 us
    ppermute x4, waiting for transfers between devices, along_rows(): return lax.ppermute(x, ('rows', 'band'), pairs)  4.8 us
    ppermute x7, starting transfers between devices, across(): return lax.ppermute(x, 'band', [(p, p ^ k) for p in range(band)])  4.79 us
    ppermute x1, starting transfers between devices, shards(): lax.ppermute(frames[:, -1:], 'rows', [(i, i + 1) for i in range(row_block...  3.15 us
    pallas_call x1, Pallas kernels, shards(): pl.pallas_call(lambda *refs: pyramid_kernel(band, *refs), grid=(slots,),...  2.83 us
    pallas_call x1, Pallas kernels, shards(): pl.pallas_call(lambda *refs: target_kernel(band, table, factor, *refs), i...  2.26 us
    ppermute x1, waiting for transfers between devices, shards(): lax.ppermute(frames[:, -1:], 'rows', [(i, i + 1) for i in range(row_block...  2.23 us
  transfers between devices with their start and end apart: 12, of which 7 were waited for; matrix products, arithmetic and copies ran while one was open for 2% of the time, Pallas kernels for 10%

profile of v5, /device:TPU:17, one launch (start us, length us, event | category | flops | bytes accessed | tf_op | source)
XLA Modules:
  0.0 44.7 jit_solution(15275368899907497963)
XLA Ops:
  0.6 0.7 %collective-permute-start = (bf16[1,2,1,960,512]{4,3,2,1,0:T(8,128)(2,1)}, bf16[1,2,1,960,512]{4,3,2,1,0:T(8,128)(2,1)S(1)}, u32[]{:S(2)}, u32[]{:S(2)}) collective-permute-start(bf16[1,2,1,960,512]{4,3,2,1,0:T(8,128)(2,1)} %bitcast.9), channel_id=1, source_target_pairs={{0,1},{1,0},{2,3},{3,2},{4,5},{5,4},{6,7},{7,6},{8,9},{9,8},{10,11... | collective-permute-start | bytes 5898248 | tf_op jit(solution)/shard_map/ppermute | solution.py:281
  1.4 0.9 %slice.32 = bf16[2,1,96,512]{3,2,1,0:T(8,128)(2,1)S(1)} slice(bf16[2,4,96,512]{3,2,1,0:T(8,128)(2,1)} %bitcast.7), slice={[0:2], [3:4], [0:96], [0:512]} | slice | bytes 393216 | tf_op jit(solution)/shard_map/slice | solution.py:283
  2.3 3.1 %collective-permute-start.1 = (bf16[2,1,96,512]{3,2,1,0:T(8,128)(2,1)S(1)}, bf16[2,1,96,512]{3,2,1,0:T(8,128)(2,1)S(1)}, u32[]{:S(2)}, u32[]{:S(2)}) collective-permute-start(bf16[2,1,96,512]{3,2,1,0:T(8,128)(2,1)S(1)} %slice.32), channel_id=1, source_target_pairs={{0,4},{4,8},{8,12},{12,16},{16,20},{20,24},{24,28},{1,5},{5,9},{9,... | collective-permute-start | bytes 589832 | tf_op jit(solution)/shard_map/ppermute | solution.py:283
  6.8 0.0 copy-start
  6.8 0.0 copy-start.2
  6.8 0.1 shard_map.94.picker_ref.refs_6_
  6.9 1.0 %copy-done = bf16[2,4,512,96]{2,3,1,0:T(8,128)(2,1)S(1)} copy-done((bf16[2,4,512,96]{2,3,1,0:T(8,128)(2,1)S(1)}, bf16[2,4,512,96]{2,3,1,0:T(8,128)(2,1)}, u32[]{:S(2)}) %copy-start) | copy-done | bytes 786456
  7.9 0.0 copy-done.2
  7.9 0.0 copy-start.1
  7.9 0.0 copy-start.3
  7.9 0.0 copy-start.4
  7.9 1.4 %shard_map.95 = (bf16[128,512]{1,0:T(8,128)(2,1)S(1)}, f32[128,512]{1,0:T(8,128)S(1)}) custom-call(bf16[512,768]{1,0:T(8,128)(2,1)S(1)} %shard_map.94.picker_ref.refs_6_, bf16[2,4,96,512]{3,2,1,0:T(8,128)(2,1)S(1)} %bitcast.8, bf16[3,3,96,128]{3,2,1,0:T(8,128)(2,1)S(1)} %copy-done.2), custom_call_target="tpu_custom_call" | custom-call | flops 2147483648 | bytes 2097152 | tf_op jit(solution)/shard_map/pallas_call | solution.py:291
  9.4 2.2 %collective-permute-done.1.refs_2_ = bf16[2,1,96,512]{3,2,1,0:T(8,128)(2,1)S(1)} collective-permute-done((bf16[2,1,96,512]{3,2,1,0:T(8,128)(2,1)S(1)}, bf16[2,1,96,512]{3,2,1,0:T(8,128)(2,1)S(1)}, u32[]{:S(2)}, u32[]{:S(2)}) %collective-permute-start.1) | collective-permute-done | bytes 196640 | tf_op jit(solution)/shard_map/ppermute | solution.py:283
  11.6 0.0 collective-permute-done.refs_9_.refs_3_
  11.6 0.0 copy-done.1
  11.6 0.0 copy-done.3
  11.6 0.0 copy-done.4
  11.6 2.3 %shard_map.96 = (bf16[128,512]{1,0:T(8,128)(2,1)S(1)}, bf16[384,512]{1,0:T(8,128)(2,1)S(1)}, bf16[128,512]{1,0:T(8,128)(2,1)S(1)}, bf16[2,128,256]{2,1,0:T(8,128...) custom-call(s32[1]{0:T(128)S(6)} %copy.10.refs_0_, ...), custom_call_target="tpu_custom_call" | custom-call | flops 2147483648 | bytes 4194304 | tf_op jit(solution)/shard_map/pallas_call | solution.py:309
  13.9 0.6 %collective-permute-start.4 = (bf16[2,128,256]{2,1,0:T(8,128)(2,1)S(1)}, bf16[2,128,256]{2,1,0:T(8,128)(2,1)S(1)}, u32[]{:S(2)}, u32[]{:S(2)}) collective-permute-start(bf16[2,128,256]{2,1,0:T(8,128)(2,1)S(1)} %get-tuple-element.29), channel_id=1, source_target_pairs={{0,2},{1,3},{2,0},{3,1},{4,6},{5,7},{6,4},{7,5},{8,10},{9,11},{10,... | collective-permute-start | bytes 393224 | tf_op jit(solution)/shard_map/ppermute | solution.py:281
  14.5 2.0 %collective-permute-start.2 = (bf16[3,128,256]{2,1,0:T(8,128)(2,1)S(1)}, bf16[3,128,256]{2,1,0:T(8,128)(2,1)S(1)}, u32[]{:S(2)}, u32[]{:S(2)}) collective-permute-start(bf16[3,128,256]{2,1,0:T(8,128)(2,1)S(1)} %get-tuple-element.25), channel_id=1, source_target_pairs={{0,16},{16,0},{4,20},{20,4},{8,24},{24,8},{12,28},{28,12},{1,13},{... | collective-permute-start | bytes 589832 | tf_op jit(solution)/shard_map/ppermute | solution.py:278
  16.5 0.6 %collective-permute-start.3 = (bf16[4,128,256]{2,1,0:T(8,128)(2,1)S(1)}, bf16[4,128,256]{2,1,0:T(8,128)(2,1)S(1)}, u32[]{:S(2)}, u32[]{:S(2)}) collective-permute-start(bf16[4,128,256]{2,1,0:T(8,128)(2,1)S(1)} %get-tuple-element.26), channel_id=1, source_target_pairs={{0,8},{8,0},{4,12},{12,4},{16,24},{24,16},{20,28},{28,20},{1,5},{5... | collective-permute-start | bytes 786440 | tf_op jit(solution)/shard_map/ppermute | solution.py:278
  17.1 1.1 %collective-permute-done.4 = bf16[2,128,256]{2,1,0:T(8,128)(2,1)S(1)} collective-permute-done((bf16[2,128,256]{2,1,0:T(8,128)(2,1)S(1)}, bf16[2,128,256]{2,1,0:T(8,128)(2,1)S(1)}, u32[]{:S(2)}, u32[]{:S(2)}) %collective-permute-start.4) | collective-permute-done | bytes 131104 | tf_op jit(solution)/shard_map/ppermute | solution.py:281
  18.2 3.3 %collective-permute-start.5 = (bf16[3,128,256]{2,1,0:T(8,128)(2,1)S(1)}, bf16[3,128,256]{2,1,0:T(8,128)(2,1)S(1)}, u32[]{:S(2)}, u32[]{:S(2)}) collective-permute-start(bf16[3,128,256]{2,1,0:T(8,128)(2,1)S(1)} %pad_maximum_fusion), channel_id=1, source_target_pairs={{8,16},{16,8},{12,20},{20,12},{13,25},{25,13},{17,29},{29,17},{10,... | collective-permute-start | bytes 589832 | tf_op jit(solution)/shard_map/ppermute | solution.py:278
  21.5 3.2 %collective-permute-start.6 = (bf16[3,128,256]{2,1,0:T(8,128)(2,1)S(1)}, bf16[3,128,256]{2,1,0:T(8,128)(2,1)S(1)}, u32[]{:S(2)}, u32[]{:S(2)}) collective-permute-start(bf16[3,128,256]{2,1,0:T(8,128)(2,1)S(1)} %pad_maximum_fusion.1), channel_id=1, source_target_pairs={{5,9},{9,5},{13,17},{17,13},{21,25},{25,21},{7,11},{11,7},{15,19},... | collective-permute-start | bytes 589832 | tf_op jit(solution)/shard_map/ppermute | solution.py:278
  24.8 0.1 collective-permute-done.2.refs_8_
  24.9 1.2 %collective-permute-start.7 = (bf16[128,256]{1,0:T(8,128)(2,1)S(1)}, bf16[128,256]{1,0:T(8,128)(2,1)S(1)}, u32[]{:S(2)}, u32[]{:S(2)}) collective-permute-start(bf16[128,256]{1,0:T(8,128)(2,1)S(1)} %slice_bitcast_fusion), channel_id=1, source_target_pairs={{0,2},{1,3},{2,0},{3,1},{4,6},{5,7},{6,4},{7,5},{8,10},{9,11},{10,... | collective-permute-start | bytes 196616 | tf_op jit(solution)/shard_map/ppermute | solution.py:281
  26.1 0.0 collective-permute-done.3.refs_9_
  26.1 2.5 %collective-permute-done.7.refs_12_ = bf16[128,256]{1,0:T(8,128)(2,1)S(1)} collective-permute-done((bf16[128,256]{1,0:T(8,128)(2,1)S(1)}, bf16[128,256]{1,0:T(8,128)(2,1)S(1)}, u32[]{:S(2)}, u32[]{:S(2)}) %collective-permute-start.7) | collective-permute-done | bytes 65568 | tf_op jit(solution)/shard_map/ppermute | solution.py:281
  28.5 0.0 collective-permute-done.5.refs_10_
  28.6 4.7 %collective-permute-done.6.refs_11_ = bf16[3,128,256]{2,1,0:T(8,128)(2,1)S(1)} collective-permute-done((bf16[3,128,256]{2,1,0:T(8,128)(2,1)S(1)}, bf16[3,128,256]{2,1,0:T(8,128)(2,1)S(1)}, u32[]{:S(2)}, u32[]{:S(2)}) %collective-permute-start.6) | collective-permute-done | bytes 196640 | tf_op jit(solution)/shard_map/ppermute | solution.py:278
  33.2 2.1 %shard_map.97 = (bf16[2,128,512]{2,1,0:T(8,128)(2,1)S(1)}, f32[4,64,256]{2,1,0:T(8,128)S(1)}, bf16[4,64,256]{2,1,0:T(8,128)(2,1)S(1)}, bf16[4,64,256]{2,1,0:T(8,128)(2,1)S(1)}, bf16[4,64,256]{2,1,0:T(8,128)(2,1)S(1)}) custom-call(s32[1]{0:T(128)S(6)} %copy.10.refs_0_, s32[1]{0:T(128)S(6)} %copy.11.refs_1_, bf16[1,2,1,960,512]{4,3,2,1,0:T(8,128)(2,1)S(1)} %bitcast.11, ...), custom_call_target="tpu_custom_call" | custom-call | flops 2147483648 | bytes 4194304 | tf_op jit(solution)/shard_map/pallas_call | solution.py:326
  35.4 0.1 collective-permute-start.8
  35.5 0.6 %collective-permute-start.9 = (bf16[4,64,256]{2,1,0:T(8,128)(2,1)S(1)}, bf16[4,64,256]{2,1,0:T(8,128)(2,1)S(1)}, u32[]{:S(2)}, u32[]{:S(2)}) collective-permute-start(bf16[4,64,256]{2,1,0:T(8,128)(2,1)S(1)} %get-tuple-element.36), channel_id=1, source_target_pairs={{0,3},{1,2},{2,1},{3,0},{4,7},{5,6},{6,5},{7,4},{8,11},{9,10},{10,... | collective-permute-start | bytes 393224 | tf_op jit(solution)/shard_map/ppermute | solution.py:281
  36.1 1.2 %collective-permute-start.10 = (bf16[4,64,256]{2,1,0:T(8,128)(2,1)S(1)}, bf16[4,64,256]{2,1,0:T(8,128)(2,1)S(1)}, u32[]{:S(2)}, u32[]{:S(2)}) collective-permute-start(bf16[4,64,256]{2,1,0:T(8,128)(2,1)S(1)} %get-tuple-element.37), channel_id=1, source_target_pairs={{0,2},{1,3},{2,0},{3,1},{4,6},{5,7},{6,4},{7,5},{8,10},{9,11},{10,... | collective-permute-start | bytes 393224 | tf_op jit(solution)/shard_map/ppermute | solution.py:281
  37.3 0.3 collective-permute-start.11
  37.7 0.0 collective-permute-done.8.refs_3_
  37.7 2.8 %shard_map.98 = bf16[1,2,1,960,512]{4,3,2,1,0:T(8,128)(2,1)} custom-call(s32[1]{0:T(128)S(6)} %copy.10.refs_0_, s32[1]{0:T(128)S(6)} %copy.11.refs_1_, bf16[2,128,512]{2,1,0:T(8,128)(2,1)S(1)} %get-tuple-element.32.refs_2_, bf16[2,128,512]{2,1,0:T(8,128)(2,1)S(1)} %collective-permute-done.8.refs_3_, bf16[384,512]{1,0:T(8,128)(2,1)S(1)} %get-tuple-element.33.refs_4_, ...), custom_call_target="tpu_custom_call" | custom-call | flops 2147483648 | bytes 4194304 | tf_op jit(solution)/shard_map/pallas_call | solution.py:344
  40.5 0.8 %collective-permute-done.9 = bf16[4,64,256]{2,1,0:T(8,128)(2,1)S(1)} collective-permute-done((bf16[4,64,256]{2,1,0:T(8,128)(2,1)S(1)}, bf16[4,64,256]{2,1,0:T(8,128)(2,1)S(1)}, u32[]{:S(2)}, u32[]{:S(2)}) %collective-permute-start.9) | collective-permute-done | bytes 131104 | tf_op jit(solution)/shard_map/ppermute | solution.py:281
  41.3 2.6 %collective-permute-done.10 = bf16[4,64,256]{2,1,0:T(8,128)(2,1)S(1)} collective-permute-done((bf16[4,64,256]{2,1,0:T(8,128)(2,1)S(1)}, bf16[4,64,256]{2,1,0:T(8,128)(2,1)S(1)}, u32[]{:S(2)}, u32[]{:S(2)}) %collective-permute-start.10) | collective-permute-done | bytes 131104 | tf_op jit(solution)/shard_map/ppermute | solution.py:281
  43.9 0.0 collective-permute-done.11
  43.9 0.1 add_bitcast_fusion
  44.0 0.7 %fusion = (f32[2,256,64]{1,2,0:T(8,128)}, f32[2,256,64]{1,2,0:T(8,128)}) fusion(f32[4,256,64]{1,2,0:T(8,128)S(1)} %add_bitcast_fusion), kind=kLoop, calls=%fused_computation.6 | loop fusion | bytes 524288 | tf_op jit(solution)/shard_map/slice | solution.py:358
  (4 shorter events, 0.1 us)
Async XLA Ops:
  0.6 11.0 %collective-permute-start = (bf16[1,2,1,960,512]{4,3,2,1,0:T(8,128)(2,1)}, bf16[1,2,1,960,512]{4,3,2,1,0:T(8,128)(2,1)S(1)}, u32[]{:S(2)}, u32[]{:S(2)}) collective-permute-start(bf16[1,2,1,960,512]{4,3,2,1,0:T(8,128)(2,1)} %bitcast.9), channel_id=1, source_target_pairs={{0,1},{1,0},{2,3},{3,2},{4,5},{5,4},{6,7},{7,6},{8,9},{9,8},{10,11... | collective-permute-start | bytes 5898248 | tf_op jit(solution)/shard_map/ppermute | solution.py:281
  2.3 9.3 %collective-permute-start.1 = (bf16[2,1,96,512]{3,2,1,0:T(8,128)(2,1)S(1)}, bf16[2,1,96,512]{3,2,1,0:T(8,128)(2,1)S(1)}, u32[]{:S(2)}, u32[]{:S(2)}) collective-permute-start(bf16[2,1,96,512]{3,2,1,0:T(8,128)(2,1)S(1)} %slice.32), channel_id=1, source_target_pairs={{0,4},{4,8},{8,12},{12,16},{16,20},{20,24},{24,28},{1,5},{5,9},{9,... | collective-permute-start | bytes 589832 | tf_op jit(solution)/shard_map/ppermute | solution.py:283
  6.8 1.1 %copy-start = (bf16[2,4,512,96]{2,3,1,0:T(8,128)(2,1)S(1)}, bf16[2,4,512,96]{2,3,1,0:T(8,128)(2,1)}, u32[]{:S(2)}) copy-start(bf16[2,4,512,96]{2,3,1,0:T(8,128)(2,1)} %param.7) | copy-start | bytes 2359300
  6.8 1.2 %copy-start.2 = (bf16[3,3,96,128]{3,2,1,0:T(8,128)(2,1)S(1)}, bf16[3,3,96,128]{3,2,1,0:T(8,128)(2,1)}, u32[]{:S(2)}) copy-start(bf16[3,3,96,128]{3,2,1,0:T(8,128)(2,1)} %refs_3_.1) | copy-start | bytes 663556
  7.9 3.7 %copy-start.1 = (bf16[1,2,1,512,960]{3,4,2,1,0:T(8,128)(2,1)S(1)}, bf16[1,2,1,512,960]{3,4,2,1,0:T(8,128)(2,1)}, u32[]{:S(2)}) copy-start(bf16[1,2,1,512,960]{3,4,2,1,0:T(8,128)(2,1)} %param.12) | copy-start | bytes 5898244
  7.9 3.7 %copy-start.3 = (bf16[128,256]{1,0:T(8,128)(2,1)S(1)}, bf16[128,256]{1,0:T(8,128)(2,1)}, u32[]{:S(2)}) copy-start(bf16[128,256]{1,0:T(8,128)(2,1)} %refs_5_.2) | copy-start | bytes 196612
  7.9 3.7 %copy-start.4 = (bf16[960,512]{1,0:T(8,128)(2,1)S(1)}, bf16[960,512]{1,0:T(8,128)(2,1)}, u32[]{:S(2)}) copy-start(bf16[960,512]{1,0:T(8,128)(2,1)} %constant.2.clone.refs_10_.refs_4_.refs_5_) | copy-start | bytes 2949124
  13.9 4.3 %collective-permute-start.4 = (bf16[2,128,256]{2,1,0:T(8,128)(2,1)S(1)}, bf16[2,128,256]{2,1,0:T(8,128)(2,1)S(1)}, u32[]{:S(2)}, u32[]{:S(2)}) collective-permute-start(bf16[2,128,256]{2,1,0:T(8,128)(2,1)S(1)} %get-tuple-element.29), channel_id=1, source_target_pairs={{0,2},{1,3},{2,0},{3,1},{4,6},{5,7},{6,4},{7,5},{8,10},{9,11},{10,... | collective-permute-start | bytes 393224 | tf_op jit(solution)/shard_map/ppermute | solution.py:281
  14.5 10.4 %collective-permute-start.2 = (bf16[3,128,256]{2,1,0:T(8,128)(2,1)S(1)}, bf16[3,128,256]{2,1,0:T(8,128)(2,1)S(1)}, u32[]{:S(2)}, u32[]{:S(2)}) collective-permute-start(bf16[3,128,256]{2,1,0:T(8,128)(2,1)S(1)} %get-tuple-element.25), channel_id=1, source_target_pairs={{0,16},{16,0},{4,20},{20,4},{8,24},{24,8},{12,28},{28,12},{1,13},{... | collective-permute-start | bytes 589832 | tf_op jit(solution)/shard_map/ppermute | solution.py:278
  16.5 9.6 %collective-permute-start.3 = (bf16[4,128,256]{2,1,0:T(8,128)(2,1)S(1)}, bf16[4,128,256]{2,1,0:T(8,128)(2,1)S(1)}, u32[]{:S(2)}, u32[]{:S(2)}) collective-permute-start(bf16[4,128,256]{2,1,0:T(8,128)(2,1)S(1)} %get-tuple-element.26), channel_id=1, source_target_pairs={{0,8},{8,0},{4,12},{12,4},{16,24},{24,16},{20,28},{28,20},{1,5},{5... | collective-permute-start | bytes 786440 | tf_op jit(solution)/shard_map/ppermute | solution.py:278
  18.2 10.3 %collective-permute-start.5 = (bf16[3,128,256]{2,1,0:T(8,128)(2,1)S(1)}, bf16[3,128,256]{2,1,0:T(8,128)(2,1)S(1)}, u32[]{:S(2)}, u32[]{:S(2)}) collective-permute-start(bf16[3,128,256]{2,1,0:T(8,128)(2,1)S(1)} %pad_maximum_fusion), channel_id=1, source_target_pairs={{8,16},{16,8},{12,20},{20,12},{13,25},{25,13},{17,29},{29,17},{10,... | collective-permute-start | bytes 589832 | tf_op jit(solution)/shard_map/ppermute | solution.py:278
  21.5 11.7 %collective-permute-start.6 = (bf16[3,128,256]{2,1,0:T(8,128)(2,1)S(1)}, bf16[3,128,256]{2,1,0:T(8,128)(2,1)S(1)}, u32[]{:S(2)}, u32[]{:S(2)}) collective-permute-start(bf16[3,128,256]{2,1,0:T(8,128)(2,1)S(1)} %pad_maximum_fusion.1), channel_id=1, source_target_pairs={{5,9},{9,5},{13,17},{17,13},{21,25},{25,21},{7,11},{11,7},{15,19},... | collective-permute-start | bytes 589832 | tf_op jit(solution)/shard_map/ppermute | solution.py:278
  24.9 3.7 %collective-permute-start.7 = (bf16[128,256]{1,0:T(8,128)(2,1)S(1)}, bf16[128,256]{1,0:T(8,128)(2,1)S(1)}, u32[]{:S(2)}, u32[]{:S(2)}) collective-permute-start(bf16[128,256]{1,0:T(8,128)(2,1)S(1)} %slice_bitcast_fusion), channel_id=1, source_target_pairs={{0,2},{1,3},{2,0},{3,1},{4,6},{5,7},{6,4},{7,5},{8,10},{9,11},{10,... | collective-permute-start | bytes 196616 | tf_op jit(solution)/shard_map/ppermute | solution.py:281
  35.4 2.3 %collective-permute-start.8 = (bf16[2,128,512]{2,1,0:T(8,128)(2,1)S(1)}, bf16[2,128,512]{2,1,0:T(8,128)(2,1)S(1)}, u32[]{:S(2)}, u32[]{:S(2)}) collective-permute-start(bf16[2,128,512]{2,1,0:T(8,128)(2,1)S(1)} %get-tuple-element.32.refs_2_), channel_id=1, source_target_pairs={{0,1},{1,0},{2,3},{3,2},{4,5},{5,4},{6,7},{7,6},{8,9},{9,8},{10,11... | collective-permute-start | bytes 786440 | tf_op jit(solution)/shard_map/ppermute | solution.py:281
  35.5 5.9 %collective-permute-start.9 = (bf16[4,64,256]{2,1,0:T(8,128)(2,1)S(1)}, bf16[4,64,256]{2,1,0:T(8,128)(2,1)S(1)}, u32[]{:S(2)}, u32[]{:S(2)}) collective-permute-start(bf16[4,64,256]{2,1,0:T(8,128)(2,1)S(1)} %get-tuple-element.36), channel_id=1, source_target_pairs={{0,3},{1,2},{2,1},{3,0},{4,7},{5,6},{6,5},{7,4},{8,11},{9,10},{10,... | collective-permute-start | bytes 393224 | tf_op jit(solution)/shard_map/ppermute | solution.py:281
  36.1 7.8 %collective-permute-start.10 = (bf16[4,64,256]{2,1,0:T(8,128)(2,1)S(1)}, bf16[4,64,256]{2,1,0:T(8,128)(2,1)S(1)}, u32[]{:S(2)}, u32[]{:S(2)}) collective-permute-start(bf16[4,64,256]{2,1,0:T(8,128)(2,1)S(1)} %get-tuple-element.37), channel_id=1, source_target_pairs={{0,2},{1,3},{2,0},{3,1},{4,6},{5,7},{6,4},{7,5},{8,10},{9,11},{10,... | collective-permute-start | bytes 393224 | tf_op jit(solution)/shard_map/ppermute | solution.py:281
  37.3 6.6 %collective-permute-start.11 = (bf16[4,64,256]{2,1,0:T(8,128)(2,1)S(1)}, bf16[4,64,256]{2,1,0:T(8,128)(2,1)S(1)}, u32[]{:S(2)}, u32[]{:S(2)}) collective-permute-start(bf16[4,64,256]{2,1,0:T(8,128)(2,1)S(1)} %get-tuple-element.38), channel_id=1, source_target_pairs={{0,1},{1,0},{2,3},{3,2},{4,5},{5,4},{6,7},{7,6},{8,9},{9,8},{10,11... | collective-permute-start | bytes 393224 | tf_op jit(solution)/shard_map/ppermute | solution.py:281

commit v6 on v5

--- a/solution.py
+++ b/solution.py
@@ -82,7 +82,7 @@
 
 def step_table(band):
     even = [(4, 0), (2, 0), (2, 1), (4, 1)]
-    odd = [(3, 0), (1, 0), (3, 1), (1, 1)]
+    odd = [(1, 1), (1, 0), (3, 0), (3, 1)]
     table = [even, odd]
     return [table[p % len(table)] for p in range(band)]
 
@@ -125,7 +125,7 @@
 
 def target_kernel(
     band, table, factor, start_ref, count_ref, rim_ref, weight_ref, lower_ref, partial_ref, picker_ref, proj_ref,
-    grad_ref, other_ref, spread_ref, target_ref, scaled_ref, own_ref, kept_ref, crossing_ref, *refs
+    grad_ref, other_ref, spread_ref, target_ref, scaled_ref, own_ref, terms_ref, *refs
 ):
     message_refs, tile_ref = refs[:-1], refs[-1]
     half = lower_ref.shape[1] // 2
@@ -170,8 +170,8 @@
         blocks = [own_half(target)] if i in SPLIT_BLOCKS else pixel_halves(target)
         tile = chosen(step)
         if i in SPLIT_TERMS:
-            kept_ref[SPLIT_TERMS.index(i)] = own_half(tile)
-            crossing_ref[SPLIT_TERMS.index(i)] = own_half(tile, True)
+            for j, part in enumerate(pixel_halves(tile)):
+                terms_ref[SPLIT_TERMS.index(i), j] = part
         else:
             blocks = [*blocks, *pixel_halves(tile)]
         for j, part in enumerate(blocks):
@@ -301,21 +301,23 @@
 
     block = jax.ShapeDtypeStruct((mid, pixels), BF16)
     piece = (mid, pixels // 2)
-    crossing = jax.ShapeDtypeStruct((len(SPLIT_TERMS),) + piece, BF16)
+    split_terms = jax.ShapeDtypeStruct((len(SPLIT_TERMS), 2) + piece, BF16)
     messages = [
         jax.ShapeDtypeStruct(((1 if i in SPLIT_BLOCKS else 2) + (0 if i in SPLIT_TERMS else 2),) + piece, BF16)
         for i in range(steps)
     ]
-    target, scaled, own_term, terms, crossing, *messages = pl.pallas_call(
+    target, scaled, own_term, terms, *messages = pl.pallas_call(
         lambda *refs: target_kernel(band, table, factor, *refs),
         in_specs=[smem] * 2 + [vmem] * 9,
-        out_shape=(block, jax.ShapeDtypeStruct((3 * mid, pixels), BF16), block, crossing, crossing, *messages),
+        out_shape=(block, jax.ShapeDtypeStruct((3 * mid, pixels), BF16), block, split_terms, *messages),
         scratch_shapes=[pltpu.VMEM((slots, mid, pixels), BF16)],
         compiler_params=params,
         cost_estimate=pl.CostEstimate(flops=2**31, bytes_accessed=2**22, transcendentals=0),
     )(band_start, band_count, rim, conv_weight, lower, partial, picker, proj_weight, grad, other_grad, spread)
 
-    others = across(crossing, 2)
+    first = lax.axis_index("band") // 2 == 0
+    others = across(jnp.where(first, terms[:, 1], terms[:, 0]), 2)
+    terms = jnp.where(first, terms[:, 0], terms[:, 1])
     for j, i in enumerate(SPLIT_TERMS):
         messages[i] = jnp.concatenate([messages[i], terms[j : j + 1] + others[j : j + 1]])
     arrived = [along_rows(messages[i], i) for i in range(steps)]

time: 45.3 us -> 42.6 us (0.940)
  the two profiles are of different devices: /device:TPU:17 before, /device:TPU:31 now
where the time goes in v6:
time: 42.6 us; the launch traced here: 42.3 us
  starting transfers between devices  17.4 us (41%)
  waiting for transfers between devices  11.2 us (26%)
  Pallas kernels  8.82 us (21%)
  local copies, waits for them, and re-layouts  2.69 us (6%)
  between operations  2.08 us (5%)
    ppermute x7, starting transfers between devices, across(): return lax.ppermute(x, 'band', [(p, p ^ k) for p in range(band)])  8.83 us
    ppermute x4, starting transfers between devices, along_rows(): return lax.ppermute(x, ('rows', 'band'), pairs)  7.24 us
    ppermute x7, waiting for transfers between devices, across(): return lax.ppermute(x, 'band', [(p, p ^ k) for p in range(band)])  6.66 us
    ppermute x1, waiting for transfers between devices, shards(): lax.ppermute(frames[:, -1:], 'rows', [(i, i + 1) for i in range(row_block...  3.17 us
    pallas_call x1, Pallas kernels, shards(): pl.pallas_call(lambda *refs: pyramid_kernel(band, *refs), grid=(slots,),...  2.84 us
    pallas_call x1, Pallas kernels, shards(): pl.pallas_call(lambda *refs: target_kernel(band, table, factor, *refs), i...  2.25 us
    pallas_call x1, Pallas kernels, shards(): pl.pallas_call(lambda *refs: gradient_kernel(band, table, factor, *refs),...  2.15 us
    pallas_call x1, Pallas kernels, shards(): pl.pallas_call(local_rows_kernel, out_shape=(jax.ShapeDtypeStruct((mid, c...  1.44 us
  transfers between devices with their start and end apart: 12, of which 5 were waited for; matrix products, arithmetic and copies ran while one was open for 2% of the time, Pallas kernels for 10%

profile of v6, /device:TPU:31, one launch (start us, length us, event | category | flops | bytes accessed | tf_op | source)
XLA Modules:
  0.0 42.3 jit_solution(9910408895467784919)
XLA Ops:
  0.6 0.7 %collective-permute-start = (bf16[1,2,1,960,512]{4,3,2,1,0:T(8,128)(2,1)}, bf16[1,2,1,960,512]{4,3,2,1,0:T(8,128)(2,1)S(1)}, u32[]{:S(2)}, u32[]{:S(2)}) collective-permute-start(bf16[1,2,1,960,512]{4,3,2,1,0:T(8,128)(2,1)} %bitcast.19), channel_id=1, source_target_pairs={{0,1},{1,0},{2,3},{3,2},{4,5},{5,4},{6,7},{7,6},{8,9},{9,8},{10,11... | collective-permute-start | bytes 5898248 | tf_op jit(solution)/shard_map/ppermute | solution.py:281
  1.4 0.9 %slice.50 = bf16[2,1,96,512]{3,2,1,0:T(8,128)(2,1)S(1)} slice(bf16[2,4,96,512]{3,2,1,0:T(8,128)(2,1)} %bitcast.17), slice={[0:2], [3:4], [0:96], [0:512]} | slice | bytes 393216 | tf_op jit(solution)/shard_map/slice | solution.py:283
  2.3 1.3 %collective-permute-start.1 = (bf16[2,1,96,512]{3,2,1,0:T(8,128)(2,1)S(1)}, bf16[2,1,96,512]{3,2,1,0:T(8,128)(2,1)S(1)}, u32[]{:S(2)}, u32[]{:S(2)}) collective-permute-start(bf16[2,1,96,512]{3,2,1,0:T(8,128)(2,1)S(1)} %slice.50), channel_id=1, source_target_pairs={{0,4},{4,8},{8,12},{12,16},{16,20},{20,24},{24,28},{1,5},{5,9},{9,... | collective-permute-start | bytes 589832 | tf_op jit(solution)/shard_map/ppermute | solution.py:283
  4.9 0.0 copy-start
  4.9 0.0 copy-start.2
  4.9 0.1 shard_map.94.picker_ref.refs_6_
  5.1 1.0 %copy-done = bf16[2,4,512,96]{2,3,1,0:T(8,128)(2,1)S(1)} copy-done((bf16[2,4,512,96]{2,3,1,0:T(8,128)(2,1)S(1)}, bf16[2,4,512,96]{2,3,1,0:T(8,128)(2,1)}, u32[]{:S(2)}) %copy-start) | copy-done | bytes 786456
  6.1 0.0 copy-done.2
  6.1 0.0 copy-start.1
  6.1 0.0 copy-start.3
  6.1 0.0 copy-start.4
  6.1 1.4 %shard_map.95 = (bf16[128,512]{1,0:T(8,128)(2,1)S(1)}, f32[128,512]{1,0:T(8,128)S(1)}) custom-call(bf16[512,768]{1,0:T(8,128)(2,1)S(1)} %shard_map.94.picker_ref.refs_6_, bf16[2,4,96,512]{3,2,1,0:T(8,128)(2,1)S(1)} %bitcast.18, bf16[3,3,96,128]{3,2,1,0:T(8,128)(2,1)S(1)} %copy-done.2), custom_call_target="tpu_custom_call" | custom-call | flops 2147483648 | bytes 2097152 | tf_op jit(solution)/shard_map/pallas_call | solution.py:291
  7.5 3.2 %collective-permute-done.1.refs_2_ = bf16[2,1,96,512]{3,2,1,0:T(8,128)(2,1)S(1)} collective-permute-done((bf16[2,1,96,512]{3,2,1,0:T(8,128)(2,1)S(1)}, bf16[2,1,96,512]{3,2,1,0:T(8,128)(2,1)S(1)}, u32[]{:S(2)}, u32[]{:S(2)}) %collective-permute-start.1) | collective-permute-done | bytes 196640 | tf_op jit(solution)/shard_map/ppermute | solution.py:283
  10.7 0.0 collective-permute-done.refs_9_.refs_3_
  10.7 0.0 copy-done.1
  10.7 0.0 copy-done.3
  10.7 0.0 copy-done.4
  10.7 2.2 %shard_map.96 = (bf16[128,512]{1,0:T(8,128)(2,1)S(1)}, bf16[384,512]{1,0:T(8,128)(2,1)S(1)}, bf16[128,512]{1,0:T(8,128)(2,1)S(1)}, bf16[2,2,128,256]{3,2,1,0:T(8...) custom-call(s32[1]{0:T(128)S(6)} %copy.10.refs_0_, ...), custom_call_target="tpu_custom_call" | custom-call | flops 2147483648 | bytes 4194304 | tf_op jit(solution)/shard_map/pallas_call | solution.py:309
  13.0 0.3 collective-permute-start.4
  13.3 0.7 %collective-permute-start.2 = (bf16[3,128,256]{2,1,0:T(8,128)(2,1)S(1)}, bf16[3,128,256]{2,1,0:T(8,128)(2,1)S(1)}, u32[]{:S(2)}, u32[]{:S(2)}) collective-permute-start(bf16[3,128,256]{2,1,0:T(8,128)(2,1)S(1)} %get-tuple-element.24), channel_id=1, source_target_pairs={{0,16},{16,0},{4,20},{20,4},{8,24},{24,8},{12,28},{28,12},{5,9},{9... | collective-permute-start | bytes 589832 | tf_op jit(solution)/shard_map/ppermute | solution.py:278
  14.0 1.9 %collective-permute-start.3 = (bf16[4,128,256]{2,1,0:T(8,128)(2,1)S(1)}, bf16[4,128,256]{2,1,0:T(8,128)(2,1)S(1)}, u32[]{:S(2)}, u32[]{:S(2)}) collective-permute-start(bf16[4,128,256]{2,1,0:T(8,128)(2,1)S(1)} %get-tuple-element.25), channel_id=1, source_target_pairs={{0,8},{8,0},{4,12},{12,4},{16,24},{24,16},{20,28},{28,20},{1,5},{5... | collective-permute-start | bytes 786440 | tf_op jit(solution)/shard_map/ppermute | solution.py:278
  16.0 1.3 %collective-permute-done.4 = bf16[2,128,256]{2,1,0:T(8,128)(2,1)S(1)} collective-permute-done((bf16[2,128,256]{2,1,0:T(8,128)(2,1)S(1)}, bf16[2,128,256]{2,1,0:T(8,128)(2,1)S(1)}, u32[]{:S(2)}, u32[]{:S(2)}) %collective-permute-start.4) | collective-permute-done | bytes 131104 | tf_op jit(solution)/shard_map/ppermute | solution.py:281
  17.3 0.7 %collective-permute-start.5 = (bf16[3,128,256]{2,1,0:T(8,128)(2,1)S(1)}, bf16[3,128,256]{2,1,0:T(8,128)(2,1)S(1)}, u32[]{:S(2)}, u32[]{:S(2)}) collective-permute-start(bf16[3,128,256]{2,1,0:T(8,128)(2,1)S(1)} %pad_maximum_fusion), channel_id=1, source_target_pairs={{8,16},{16,8},{12,20},{20,12},{1,13},{13,1},{5,17},{17,5},{9,21},{... | collective-permute-start | bytes 589832 | tf_op jit(solution)/shard_map/ppermute | solution.py:278
  18.1 4.0 %collective-permute-start.6 = (bf16[3,128,256]{2,1,0:T(8,128)(2,1)S(1)}, bf16[3,128,256]{2,1,0:T(8,128)(2,1)S(1)}, u32[]{:S(2)}, u32[]{:S(2)}) collective-permute-start(bf16[3,128,256]{2,1,0:T(8,128)(2,1)S(1)} %pad_maximum_fusion.1), channel_id=1, source_target_pairs={{13,25},{25,13},{17,29},{29,17},{15,27},{27,15},{19,31},{31,19}} | collective-permute-start | bytes 589832 | tf_op jit(solution)/shard_map/ppermute | solution.py:278
  22.0 0.0 collective-permute-done.2.refs_8_
  22.1 1.3 %collective-permute-start.7 = (bf16[128,256]{1,0:T(8,128)(2,1)S(1)}, bf16[128,256]{1,0:T(8,128)(2,1)S(1)}, u32[]{:S(2)}, u32[]{:S(2)}) collective-permute-start(bf16[128,256]{1,0:T(8,128)(2,1)S(1)} %slice_bitcast_fusion), channel_id=1, source_target_pairs={{0,2},{1,3},{2,0},{3,1},{4,6},{5,7},{6,4},{7,5},{8,10},{9,11},{10,... | collective-permute-start | bytes 196616 | tf_op jit(solution)/shard_map/ppermute | solution.py:281
  23.3 0.0 collective-permute-done.3.refs_9_
  23.3 2.2 %collective-permute-done.7.refs_12_ = bf16[128,256]{1,0:T(8,128)(2,1)S(1)} collective-permute-done((bf16[128,256]{1,0:T(8,128)(2,1)S(1)}, bf16[128,256]{1,0:T(8,128)(2,1)S(1)}, u32[]{:S(2)}, u32[]{:S(2)}) %collective-permute-start.7) | collective-permute-done | bytes 65568 | tf_op jit(solution)/shard_map/ppermute | solution.py:281
  25.5 0.0 collective-permute-done.5.refs_10_
  25.5 1.4 %collective-permute-done.6.refs_11_ = bf16[3,128,256]{2,1,0:T(8,128)(2,1)S(1)} collective-permute-done((bf16[3,128,256]{2,1,0:T(8,128)(2,1)S(1)}, bf16[3,128,256]{2,1,0:T(8,128)(2,1)S(1)}, u32[]{:S(2)}, u32[]{:S(2)}) %collective-permute-start.6) | collective-permute-done | bytes 196640 | tf_op jit(solution)/shard_map/ppermute | solution.py:278
  26.9 2.2 %shard_map.97 = (bf16[2,128,512]{2,1,0:T(8,128)(2,1)S(1)}, f32[4,64,256]{2,1,0:T(8,128)S(1)}, bf16[4,64,256]{2,1,0:T(8,128)(2,1)S(1)}, bf16[4,64,256]{2,1,0:T(8,128)(2,1)S(1)}, bf16[4,64,256]{2,1,0:T(8,128)(2,1)S(1)}) custom-call(s32[1]{0:T(128)S(6)} %copy.10.refs_0_, s32[1]{0:T(128)S(6)} %copy.11.refs_1_, bf16[1,2,1,960,512]{4,3,2,1,0:T(8,128)(2,1)S(1)} %bitcast.21, ...), custom_call_target="tpu_custom_call" | custom-call | flops 2147483648 | bytes 4194304 | tf_op jit(solution)/shard_map/pallas_call | solution.py:328
  29.1 4.3 %collective-permute-start.8 = (bf16[2,128,512]{2,1,0:T(8,128)(2,1)S(1)}, bf16[2,128,512]{2,1,0:T(8,128)(2,1)S(1)}, u32[]{:S(2)}, u32[]{:S(2)}) collective-permute-start(bf16[2,128,512]{2,1,0:T(8,128)(2,1)S(1)} %get-tuple-element.30.refs_2_), channel_id=1, source_target_pairs={{0,1},{1,0},{2,3},{3,2},{4,5},{5,4},{6,7},{7,6},{8,9},{9,8},{10,11... | collective-permute-start | bytes 786440 | tf_op jit(solution)/shard_map/ppermute | solution.py:281
  33.4 0.1 collective-permute-start.11
  33.5 0.1 collective-permute-start.10
  33.6 2.0 %collective-permute-start.9 = (bf16[4,64,256]{2,1,0:T(8,128)(2,1)S(1)}, bf16[4,64,256]{2,1,0:T(8,128)(2,1)S(1)}, u32[]{:S(2)}, u32[]{:S(2)}) collective-permute-start(bf16[4,64,256]{2,1,0:T(8,128)(2,1)S(1)} %get-tuple-element.34), channel_id=1, source_target_pairs={{0,3},{1,2},{2,1},{3,0},{4,7},{5,6},{6,5},{7,4},{8,11},{9,10},{10,... | collective-permute-start | bytes 393224 | tf_op jit(solution)/shard_map/ppermute | solution.py:281
  35.6 0.0 collective-permute-done.8.refs_3_
  35.6 2.8 %shard_map.98 = bf16[1,2,1,960,512]{4,3,2,1,0:T(8,128)(2,1)} custom-call(s32[1]{0:T(128)S(6)} %copy.10.refs_0_, s32[1]{0:T(128)S(6)} %copy.11.refs_1_, bf16[2,128,512]{2,1,0:T(8,128)(2,1)S(1)} %get-tuple-element.30.refs_2_, bf16[2,128,512]{2,1,0:T(8,128)(2,1)S(1)} %collective-permute-done.8.refs_3_, bf16[384,512]{1,0:T(8,128)(2,1)S(1)} %get-tuple-element.31.refs_4_, ...), custom_call_target="tpu_custom_call" | custom-call | flops 2147483648 | bytes 4194304 | tf_op jit(solution)/shard_map/pallas_call | solution.py:346
  38.4 0.0 collective-permute-done.11
  38.4 0.0 collective-permute-done.10
  38.4 3.1 %collective-permute-done.9 = bf16[4,64,256]{2,1,0:T(8,128)(2,1)S(1)} collective-permute-done((bf16[4,64,256]{2,1,0:T(8,128)(2,1)S(1)}, bf16[4,64,256]{2,1,0:T(8,128)(2,1)S(1)}, u32[]{:S(2)}, u32[]{:S(2)}) %collective-permute-start.9) | collective-permute-done | bytes 131104 | tf_op jit(solution)/shard_map/ppermute | solution.py:281
  41.5 0.1 add_bitcast_fusion
  41.6 0.7 %fusion = (f32[2,256,64]{1,2,0:T(8,128)}, f32[2,256,64]{1,2,0:T(8,128)}) fusion(f32[4,256,64]{1,2,0:T(8,128)S(1)} %add_bitcast_fusion), kind=kLoop, calls=%fused_computation.10 | loop fusion | bytes 524288 | tf_op jit(solution)/shard_map/slice | solution.py:360
  (5 shorter events, 0.1 us)
Async XLA Ops:
  0.6 10.1 %collective-permute-start = (bf16[1,2,1,960,512]{4,3,2,1,0:T(8,128)(2,1)}, bf16[1,2,1,960,512]{4,3,2,1,0:T(8,128)(2,1)S(1)}, u32[]{:S(2)}, u32[]{:S(2)}) collective-permute-start(bf16[1,2,1,960,512]{4,3,2,1,0:T(8,128)(2,1)} %bitcast.19), channel_id=1, source_target_pairs={{0,1},{1,0},{2,3},{3,2},{4,5},{5,4},{6,7},{7,6},{8,9},{9,8},{10,11... | collective-permute-start | bytes 5898248 | tf_op jit(solution)/shard_map/ppermute | solution.py:281
  2.3 8.4 %collective-permute-start.1 = (bf16[2,1,96,512]{3,2,1,0:T(8,128)(2,1)S(1)}, bf16[2,1,96,512]{3,2,1,0:T(8,128)(2,1)S(1)}, u32[]{:S(2)}, u32[]{:S(2)}) collective-permute-start(bf16[2,1,96,512]{3,2,1,0:T(8,128)(2,1)S(1)} %slice.50), channel_id=1, source_target_pairs={{0,4},{4,8},{8,12},{12,16},{16,20},{20,24},{24,28},{1,5},{5,9},{9,... | collective-permute-start | bytes 589832 | tf_op jit(solution)/shard_map/ppermute | solution.py:283
  4.9 1.1 %copy-start = (bf16[2,4,512,96]{2,3,1,0:T(8,128)(2,1)S(1)}, bf16[2,4,512,96]{2,3,1,0:T(8,128)(2,1)}, u32[]{:S(2)}) copy-start(bf16[2,4,512,96]{2,3,1,0:T(8,128)(2,1)} %param.7) | copy-start | bytes 2359300
  4.9 1.2 %copy-start.2 = (bf16[3,3,96,128]{3,2,1,0:T(8,128)(2,1)S(1)}, bf16[3,3,96,128]{3,2,1,0:T(8,128)(2,1)}, u32[]{:S(2)}) copy-start(bf16[3,3,96,128]{3,2,1,0:T(8,128)(2,1)} %refs_3_.1) | copy-start | bytes 663556
  6.1 4.6 %copy-start.1 = (bf16[1,2,1,512,960]{3,4,2,1,0:T(8,128)(2,1)S(1)}, bf16[1,2,1,512,960]{3,4,2,1,0:T(8,128)(2,1)}, u32[]{:S(2)}) copy-start(bf16[1,2,1,512,960]{3,4,2,1,0:T(8,128)(2,1)} %param.12) | copy-start | bytes 5898244
  6.1 4.6 %copy-start.3 = (bf16[128,256]{1,0:T(8,128)(2,1)S(1)}, bf16[128,256]{1,0:T(8,128)(2,1)}, u32[]{:S(2)}) copy-start(bf16[128,256]{1,0:T(8,128)(2,1)} %refs_5_.2) | copy-start | bytes 196612
  6.1 4.6 %copy-start.4 = (bf16[960,512]{1,0:T(8,128)(2,1)S(1)}, bf16[960,512]{1,0:T(8,128)(2,1)}, u32[]{:S(2)}) copy-start(bf16[960,512]{1,0:T(8,128)(2,1)} %constant.21.clone.refs_10_.refs_4_.refs_5_) | copy-start | bytes 2949124
  13.0 4.3 %collective-permute-start.4 = (bf16[2,128,256]{2,1,0:T(8,128)(2,1)S(1)}, bf16[2,128,256]{2,1,0:T(8,128)(2,1)S(1)}, u32[]{:S(2)}, u32[]{:S(2)}) collective-permute-start(bf16[2,128,256]{2,1,0:T(8,128)(2,1)S(1)} %get-tuple-element.42), channel_id=1, source_target_pairs={{0,2},{1,3},{2,0},{3,1},{4,6},{5,7},{6,4},{7,5},{8,10},{9,11},{10,... | collective-permute-start | bytes 393224 | tf_op jit(solution)/shard_map/ppermute | solution.py:281
  13.3 8.7 %collective-permute-start.2 = (bf16[3,128,256]{2,1,0:T(8,128)(2,1)S(1)}, bf16[3,128,256]{2,1,0:T(8,128)(2,1)S(1)}, u32[]{:S(2)}, u32[]{:S(2)}) collective-permute-start(bf16[3,128,256]{2,1,0:T(8,128)(2,1)S(1)} %get-tuple-element.24), channel_id=1, source_target_pairs={{0,16},{16,0},{4,20},{20,4},{8,24},{24,8},{12,28},{28,12},{5,9},{9... | collective-permute-start | bytes 589832 | tf_op jit(solution)/shard_map/ppermute | solution.py:278
  14.0 9.3 %collective-permute-start.3 = (bf16[4,128,256]{2,1,0:T(8,128)(2,1)S(1)}, bf16[4,128,256]{2,1,0:T(8,128)(2,1)S(1)}, u32[]{:S(2)}, u32[]{:S(2)}) collective-permute-start(bf16[4,128,256]{2,1,0:T(8,128)(2,1)S(1)} %get-tuple-element.25), channel_id=1, source_target_pairs={{0,8},{8,0},{4,12},{12,4},{16,24},{24,16},{20,28},{28,20},{1,5},{5... | collective-permute-start | bytes 786440 | tf_op jit(solution)/shard_map/ppermute | solution.py:278
  17.3 8.2 %collective-permute-start.5 = (bf16[3,128,256]{2,1,0:T(8,128)(2,1)S(1)}, bf16[3,128,256]{2,1,0:T(8,128)(2,1)S(1)}, u32[]{:S(2)}, u32[]{:S(2)}) collective-permute-start(bf16[3,128,256]{2,1,0:T(8,128)(2,1)S(1)} %pad_maximum_fusion), channel_id=1, source_target_pairs={{8,16},{16,8},{12,20},{20,12},{1,13},{13,1},{5,17},{17,5},{9,21},{... | collective-permute-start | bytes 589832 | tf_op jit(solution)/shard_map/ppermute | solution.py:278
  18.1 8.8 %collective-permute-start.6 = (bf16[3,128,256]{2,1,0:T(8,128)(2,1)S(1)}, bf16[3,128,256]{2,1,0:T(8,128)(2,1)S(1)}, u32[]{:S(2)}, u32[]{:S(2)}) collective-permute-start(bf16[3,128,256]{2,1,0:T(8,128)(2,1)S(1)} %pad_maximum_fusion.1), channel_id=1, source_target_pairs={{13,25},{25,13},{17,29},{29,17},{15,27},{27,15},{19,31},{31,19}} | collective-permute-start | bytes 589832 | tf_op jit(solution)/shard_map/ppermute | solution.py:278
  22.1 3.5 %collective-permute-start.7 = (bf16[128,256]{1,0:T(8,128)(2,1)S(1)}, bf16[128,256]{1,0:T(8,128)(2,1)S(1)}, u32[]{:S(2)}, u32[]{:S(2)}) collective-permute-start(bf16[128,256]{1,0:T(8,128)(2,1)S(1)} %slice_bitcast_fusion), channel_id=1, source_target_pairs={{0,2},{1,3},{2,0},{3,1},{4,6},{5,7},{6,4},{7,5},{8,10},{9,11},{10,... | collective-permute-start | bytes 196616 | tf_op jit(solution)/shard_map/ppermute | solution.py:281
  29.1 6.5 %collective-permute-start.8 = (bf16[2,128,512]{2,1,0:T(8,128)(2,1)S(1)}, bf16[2,128,512]{2,1,0:T(8,128)(2,1)S(1)}, u32[]{:S(2)}, u32[]{:S(2)}) collective-permute-start(bf16[2,128,512]{2,1,0:T(8,128)(2,1)S(1)} %get-tuple-element.30.refs_2_), channel_id=1, source_target_pairs={{0,1},{1,0},{2,3},{3,2},{4,5},{5,4},{6,7},{7,6},{8,9},{9,8},{10,11... | collective-permute-start | bytes 786440 | tf_op jit(solution)/shard_map/ppermute | solution.py:281
  33.4 5.0 %collective-permute-start.11 = (bf16[4,64,256]{2,1,0:T(8,128)(2,1)S(1)}, bf16[4,64,256]{2,1,0:T(8,128)(2,1)S(1)}, u32[]{:S(2)}, u32[]{:S(2)}) collective-permute-start(bf16[4,64,256]{2,1,0:T(8,128)(2,1)S(1)} %get-tuple-element.36), channel_id=1, source_target_pairs={{0,1},{1,0},{2,3},{3,2},{4,5},{5,4},{6,7},{7,6},{8,9},{9,8},{10,11... | collective-permute-start | bytes 393224 | tf_op jit(solution)/shard_map/ppermute | solution.py:281
  33.5 4.9 %collective-permute-start.10 = (bf16[4,64,256]{2,1,0:T(8,128)(2,1)S(1)}, bf16[4,64,256]{2,1,0:T(8,128)(2,1)S(1)}, u32[]{:S(2)}, u32[]{:S(2)}) collective-permute-start(bf16[4,64,256]{2,1,0:T(8,128)(2,1)S(1)} %get-tuple-element.35), channel_id=1, source_target_pairs={{0,2},{1,3},{2,0},{3,1},{4,6},{5,7},{6,4},{7,5},{8,10},{9,11},{10,... | collective-permute-start | bytes 393224 | tf_op jit(solution)/shard_map/ppermute | solution.py:281
  33.6 8.0 %collective-permute-start.9 = (bf16[4,64,256]{2,1,0:T(8,128)(2,1)S(1)}, bf16[4,64,256]{2,1,0:T(8,128)(2,1)S(1)}, u32[]{:S(2)}, u32[]{:S(2)}) collective-permute-start(bf16[4,64,256]{2,1,0:T(8,128)(2,1)S(1)} %get-tuple-element.34), channel_id=1, source_target_pairs={{0,3},{1,2},{2,1},{3,0},{4,7},{5,6},{6,5},{7,4},{8,11},{9,10},{10,... | collective-permute-start | bytes 393224 | tf_op jit(solution)/shard_map/ppermute | solution.py:281

commit v7 on v6

--- a/solution.py
+++ b/solution.py
@@ -29,7 +29,7 @@
 
 def spread_matrix(pixels):
     parts = []
-    for level in range(LEVELS):
+    for level in range(1, LEVELS):
         group = 2**level
         parts.append(np.repeat(np.eye(pixels // group, dtype=np.float32), group, axis=1) / group)
     return np.concatenate(parts, axis=0).astype(jnp.bfloat16)
@@ -124,8 +124,8 @@
 
 
 def target_kernel(
-    band, table, factor, start_ref, count_ref, rim_ref, weight_ref, lower_ref, partial_ref, picker_ref, proj_ref,
-    grad_ref, other_ref, spread_ref, target_ref, scaled_ref, own_ref, terms_ref, *refs
+    band, table, factor, start_ref, count_ref, rim_ref, weight_ref, lower_ref, partial_ref, picker_ref,
+    grad_ref, other_ref, spread_ref, target_ref, source_ref, own_ref, terms_ref, *refs
 ):
     message_refs, tile_ref = refs[:-1], refs[-1]
     half = lower_ref.shape[1] // 2
@@ -141,18 +141,14 @@
     upper = jnp.maximum(upper, 0.0).astype(BF16)
     source = jnp.concatenate([upper[:, :half], lower_ref[:, :half]], axis=1)
     target = jnp.concatenate([upper[:, half:], lower_ref[:, half:]], axis=1)
-    gram = product(proj_ref[...], proj_ref[...], NT)
-    both = product(jnp.concatenate(halves(gram), axis=0), source)
-    high, low = halves((both[:mid] + both[mid:]) * factor)
-    scaled_ref[:mid, :] = high
-    scaled_ref[mid : 2 * mid, :] = low
-    scaled_ref[2 * mid :, :] = high
+    source_ref[...] = source
     same, held, active, steps = held_class(band, start_ref, count_ref, table, slots)
 
     def term(slot, block_ref):
-        high, low = halves(product(source, block_ref[0, slot, 0], NT))
-        both = product(jnp.concatenate([high, low], axis=0), spread_ref[...])
-        tile_ref[slot] = (both[:mid] + both[mid:]).astype(BF16)
+        entries = product(source, block_ref[0, slot, 0], NT)
+        pixels = tile_ref.shape[2]
+        both = product(jnp.concatenate(halves(entries[:, pixels:]), axis=0), spread_ref[...])
+        tile_ref[slot] = (entries[:, :pixels] + both[:mid] + both[mid:]).astype(BF16)
 
     for slot in range(slots):
         pl.when(jnp.logical_and(active[slot], same))(lambda: term(slot, grad_ref))
@@ -191,9 +187,10 @@
     sum_ref[...] = jnp.zeros(sum_ref.shape, F32)
 
     def add(slot, block_ref):
-        high, low = halves(product(held_ref[slot], spread_ref[...], NT))
-        both = product(jnp.concatenate([high, low], axis=0), block_ref[0, slot, 0])
-        sum_ref[...] += both[:mid] + both[mid:]
+        block = held_ref[slot]
+        pooled = halves(product(block, spread_ref[...], NT))
+        both = product(jnp.concatenate(pooled, axis=0), block_ref[0, slot, 0, pixels:, :])
+        sum_ref[...] += product(block, block_ref[0, slot, 0, :pixels, :]) + (both[:mid] + both[mid:])
 
     for slot in range(slots):
         block = target_ref[...]
@@ -230,17 +227,32 @@
                 sent_refs[k - 1][part] = out.astype(BF16)
 
 
-def pyramid_kernel(band, start_ref, count_ref, held_ref, other_ref, scaled_ref, spread_ref, pyramid_ref):
+def pyramid_kernel(
+    band, factor, start_ref, count_ref, held_ref, other_ref, source_ref, proj_ref, spread_ref, pyramid_ref, scaled_ref
+):
+    mid = source_ref.shape[0]
     slot = pl.program_id(0)
     active = slot * band + lax.axis_index("band") < count_ref[0]
     same = lax.rem(start_ref[0] + 2 * BAND_REACH, 2) == 0
 
+    @pl.when(slot == 0)
+    def _():
+        gram = product(proj_ref[...], proj_ref[...], NT)
+        both = product(jnp.concatenate(halves(gram), axis=0), source_ref[...])
+        high, low = halves((both[:mid] + both[mid:]) * factor)
+        scaled_ref[:mid, :] = high
+        scaled_ref[mid : 2 * mid, :] = low
+        scaled_ref[2 * mid :, :] = high
+
     @pl.when(active)
     def _():
         target = jnp.where(same, held_ref[0], other_ref[0])
+        pixels = target.shape[1]
+        finest = product(jnp.concatenate([target, target], axis=0), scaled_ref[: 2 * mid, :], TN)
+        pyramid_ref[0, 0, 0, :pixels, :] = finest.astype(BF16)
         high, low = halves(product(spread_ref[...], target, NT))
-        corr = product(jnp.concatenate([high, high, low], axis=1), scaled_ref[...])
-        pyramid_ref[0, 0, 0] = corr.astype(BF16)
+        coarser = product(jnp.concatenate([high, high, low], axis=1), scaled_ref[...])
+        pyramid_ref[0, 0, 0, pixels:, :] = coarser.astype(BF16)
 
     @pl.when(jnp.logical_not(active))
     def _():
@@ -306,14 +318,14 @@
         jax.ShapeDtypeStruct(((1 if i in SPLIT_BLOCKS else 2) + (0 if i in SPLIT_TERMS else 2),) + piece, BF16)
         for i in range(steps)
     ]
-    target, scaled, own_term, terms, *messages = pl.pallas_call(
+    target, source, own_term, terms, *messages = pl.pallas_call(
         lambda *refs: target_kernel(band, table, factor, *refs),
-        in_specs=[smem] * 2 + [vmem] * 9,
-        out_shape=(block, jax.ShapeDtypeStruct((3 * mid, pixels), BF16), block, split_terms, *messages),
+        in_specs=[smem] * 2 + [vmem] * 8,
+        out_shape=(block, block, block, split_terms, *messages),
         scratch_shapes=[pltpu.VMEM((slots, mid, pixels), BF16)],
         compiler_params=params,
         cost_estimate=pl.CostEstimate(flops=2**31, bytes_accessed=2**22, transcendentals=0),
-    )(band_start, band_count, rim, conv_weight, lower, partial, picker, proj_weight, grad, other_grad, spread)
+    )(band_start, band_count, rim, conv_weight, lower, partial, picker, grad, other_grad, spread)
 
     first = lax.axis_index("band") // 2 == 0
     others = across(jnp.where(first, terms[:, 1], terms[:, 0]), 2)
@@ -344,14 +356,16 @@
     target_spec = pl.BlockSpec((1, mid, pixels), lambda j: (j, 0, 0))
     grad_spec = pl.BlockSpec((1, 1, 1, entries, pixels), lambda j: (0, j, 0, 0, 0))
     pyramid = pl.pallas_call(
-        lambda *refs: pyramid_kernel(band, *refs),
+        lambda *refs: pyramid_kernel(band, factor, *refs),
         grid=(slots,),
-        in_specs=[smem, smem, target_spec, target_spec, whole((3 * mid, pixels)), whole((entries, pixels))],
+        in_specs=[smem, smem, target_spec, target_spec, whole((mid, pixels)), whole((mid, channels))]
+        + [whole(spread.shape)],
         out_specs=grad_spec,
         out_shape=jax.ShapeDtypeStruct(grad.shape, BF16),
+        scratch_shapes=[pltpu.VMEM((3 * mid, pixels), BF16)],
         compiler_params=params,
         cost_estimate=pl.CostEstimate(flops=2**31, bytes_accessed=2**22, transcendentals=0),
-    )(band_start, band_count, held, other, scaled, spread)
+    )(band_start, band_count, held, other, source, proj_weight, spread)
 
     total, pyramid = lax.optimization_barrier((kept, pyramid))
     for x in received:

time: 42.6 us -> 42.4 us (level)
  the two profiles are of different devices: /device:TPU:31 before, /device:TPU:1 now
where the time goes in v7:
time: 42.4 us; the launch traced here: 42 us
  starting transfers between devices  21.1 us (50%)
  waiting for transfers between devices  9.34 us (22%)
  Pallas kernels  6.61 us (16%)
  local copies, waits for them, and re-layouts  2.69 us (6%)
  between operations  2.08 us (5%)
    ppermute x4, starting transfers between devices, along_rows(): return lax.ppermute(x, ('rows', 'band'), pairs)  9.93 us
    ppermute x7, starting transfers between devices, across(): return lax.ppermute(x, 'band', [(p, p ^ k) for p in range(band)])  6.58 us
    ppermute x7, waiting for transfers between devices, across(): return lax.ppermute(x, 'band', [(p, p ^ k) for p in range(band)])  6.12 us
    ppermute x1, starting transfers between devices, shards(): lax.ppermute(frames[:, -1:], 'rows', [(i, i + 1) for i in range(row_block...  4.6 us
    ppermute x4, waiting for transfers between devices, along_rows(): return lax.ppermute(x, ('rows', 'band'), pairs)  2.88 us
    pallas_call x1, Pallas kernels, shards(): pl.pallas_call(lambda *refs: pyramid_kernel(band, factor, *refs), grid=(s...  2.33 us
    pallas_call x1, Pallas kernels, shards(): pl.pallas_call(local_rows_kernel, out_shape=(jax.ShapeDtypeStruct((mid, c...  1.44 us
    pallas_call x1, Pallas kernels, shards(): pl.pallas_call(lambda *refs: target_kernel(band, table, factor, *refs), i...  1.38 us
  transfers between devices with their start and end apart: 12, of which 5 were waited for; matrix products, arithmetic and copies ran while one was open for 2% of the time, Pallas kernels for 9%

profile of v7, /device:TPU:1, one launch (start us, length us, event | category | flops | bytes accessed | tf_op | source)
XLA Modules:
  0.0 42.0 jit_solution(275481730252058510)
XLA Ops:
  0.6 0.1 collective-permute-start
  0.8 0.9 %slice.50 = bf16[2,1,96,512]{3,2,1,0:T(8,128)(2,1)S(1)} slice(bf16[2,4,96,512]{3,2,1,0:T(8,128)(2,1)} %bitcast.17), slice={[0:2], [3:4], [0:96], [0:512]} | slice | bytes 393216 | tf_op jit(solution)/shard_map/slice | solution.py:295
  1.7 4.6 %collective-permute-start.1 = (bf16[2,1,96,512]{3,2,1,0:T(8,128)(2,1)S(1)}, bf16[2,1,96,512]{3,2,1,0:T(8,128)(2,1)S(1)}, u32[]{:S(2)}, u32[]{:S(2)}) collective-permute-start(bf16[2,1,96,512]{3,2,1,0:T(8,128)(2,1)S(1)} %slice.50), channel_id=1, source_target_pairs={{0,4},{4,8},{8,12},{12,16},{16,20},{20,24},{24,28},{1,5},{5,9},{9,... | collective-permute-start | bytes 589832 | tf_op jit(solution)/shard_map/ppermute | solution.py:295
  7.6 0.0 copy-start
  7.6 0.0 copy-start.2
  7.6 0.1 shard_map.94.picker_ref.refs_6_
  7.8 1.0 %copy-done = bf16[2,4,512,96]{2,3,1,0:T(8,128)(2,1)S(1)} copy-done((bf16[2,4,512,96]{2,3,1,0:T(8,128)(2,1)S(1)}, bf16[2,4,512,96]{2,3,1,0:T(8,128)(2,1)}, u32[]{:S(2)}) %copy-start) | copy-done | bytes 786456
  8.8 0.0 copy-done.2
  8.8 0.0 copy-start.1
  8.8 0.0 copy-start.4
  8.8 1.4 %shard_map.95 = (bf16[128,512]{1,0:T(8,128)(2,1)S(1)}, f32[128,512]{1,0:T(8,128)S(1)}) custom-call(bf16[512,768]{1,0:T(8,128)(2,1)S(1)} %shard_map.94.picker_ref.refs_6_, bf16[2,4,96,512]{3,2,1,0:T(8,128)(2,1)S(1)} %bitcast.18, bf16[3,3,96,128]{3,2,1,0:T(8,128)(2,1)S(1)} %copy-done.2), custom_call_target="tpu_custom_call" | custom-call | flops 2147483648 | bytes 2097152 | tf_op jit(solution)/shard_map/pallas_call | solution.py:303
  10.2 0.3 collective-permute-done.1.refs_2_
  10.6 0.0 collective-permute-done.refs_8_.refs_3_
  10.6 0.0 copy-done.1
  10.6 0.0 copy-done.4
  10.6 0.0 copy-start.3
  10.6 1.4 %shard_map.96 = (bf16[128,512]{1,0:T(8,128)(2,1)S(1)}, bf16[128,512]{1,0:T(8,128)(2,1)S(1)}, bf16[128,512]{1,0:T(8,128)(2,1)S(1)}, bf16[2,2,128,256]{3,2,1,0:T(8...) custom-call(s32[1]{0:T(128)S(6)} %copy.10.refs_0_, ...), custom_call_target="tpu_custom_call" | custom-call | flops 2147483648 | bytes 4194304 | tf_op jit(solution)/shard_map/pallas_call | solution.py:321
  12.0 0.6 %collective-permute-start.4 = (bf16[2,128,256]{2,1,0:T(8,128)(2,1)S(1)}, bf16[2,128,256]{2,1,0:T(8,128)(2,1)S(1)}, u32[]{:S(2)}, u32[]{:S(2)}) collective-permute-start(bf16[2,128,256]{2,1,0:T(8,128)(2,1)S(1)} %get-tuple-element.42), channel_id=1, source_target_pairs={{0,2},{1,3},{2,0},{3,1},{4,6},{5,7},{6,4},{7,5},{8,10},{9,11},{10,... | collective-permute-start | bytes 393224 | tf_op jit(solution)/shard_map/ppermute | solution.py:293
  12.6 0.7 %collective-permute-start.2 = (bf16[3,128,256]{2,1,0:T(8,128)(2,1)S(1)}, bf16[3,128,256]{2,1,0:T(8,128)(2,1)S(1)}, u32[]{:S(2)}, u32[]{:S(2)}) collective-permute-start(bf16[3,128,256]{2,1,0:T(8,128)(2,1)S(1)} %get-tuple-element.24), channel_id=1, source_target_pairs={{0,16},{16,0},{4,20},{20,4},{8,24},{24,8},{12,28},{28,12},{5,9},{9... | collective-permute-start | bytes 589832 | tf_op jit(solution)/shard_map/ppermute | solution.py:290
  13.3 5.6 %collective-permute-start.3 = (bf16[4,128,256]{2,1,0:T(8,128)(2,1)S(1)}, bf16[4,128,256]{2,1,0:T(8,128)(2,1)S(1)}, u32[]{:S(2)}, u32[]{:S(2)}) collective-permute-start(bf16[4,128,256]{2,1,0:T(8,128)(2,1)S(1)} %get-tuple-element.25), channel_id=1, source_target_pairs={{0,8},{8,0},{4,12},{12,4},{16,24},{24,16},{20,28},{28,20},{1,5},{5... | collective-permute-start | bytes 786440 | tf_op jit(solution)/shard_map/ppermute | solution.py:290
  18.9 0.0 collective-permute-done.4
  19.0 3.0 %collective-permute-start.5 = (bf16[3,128,256]{2,1,0:T(8,128)(2,1)S(1)}, bf16[3,128,256]{2,1,0:T(8,128)(2,1)S(1)}, u32[]{:S(2)}, u32[]{:S(2)}) collective-permute-start(bf16[3,128,256]{2,1,0:T(8,128)(2,1)S(1)} %pad_maximum_fusion), channel_id=1, source_target_pairs={{8,16},{16,8},{12,20},{20,12},{1,13},{13,1},{5,17},{17,5},{9,21},{... | collective-permute-start | bytes 589832 | tf_op jit(solution)/shard_map/ppermute | solution.py:290
  22.0 0.7 %collective-permute-start.6 = (bf16[3,128,256]{2,1,0:T(8,128)(2,1)S(1)}, bf16[3,128,256]{2,1,0:T(8,128)(2,1)S(1)}, u32[]{:S(2)}, u32[]{:S(2)}) collective-permute-start(bf16[3,128,256]{2,1,0:T(8,128)(2,1)S(1)} %pad_maximum_fusion.1), channel_id=1, source_target_pairs={{13,25},{25,13},{17,29},{29,17},{15,27},{27,15},{19,31},{31,19}} | collective-permute-start | bytes 589832 | tf_op jit(solution)/shard_map/ppermute | solution.py:290
  22.7 0.0 collective-permute-done.2.refs_8_
  22.7 1.0 %collective-permute-start.7 = (bf16[128,256]{1,0:T(8,128)(2,1)S(1)}, bf16[128,256]{1,0:T(8,128)(2,1)S(1)}, u32[]{:S(2)}, u32[]{:S(2)}) collective-permute-start(bf16[128,256]{1,0:T(8,128)(2,1)S(1)} %slice_bitcast_fusion), channel_id=1, source_target_pairs={{0,2},{1,3},{2,0},{3,1},{4,6},{5,7},{6,4},{7,5},{8,10},{9,11},{10,... | collective-permute-start | bytes 196616 | tf_op jit(solution)/shard_map/ppermute | solution.py:293
  23.7 0.0 collective-permute-done.3.refs_9_
  23.7 2.5 %collective-permute-done.7.refs_12_ = bf16[128,256]{1,0:T(8,128)(2,1)S(1)} collective-permute-done((bf16[128,256]{1,0:T(8,128)(2,1)S(1)}, bf16[128,256]{1,0:T(8,128)(2,1)S(1)}, u32[]{:S(2)}, u32[]{:S(2)}) %collective-permute-start.7) | collective-permute-done | bytes 65568 | tf_op jit(solution)/shard_map/ppermute | solution.py:293
  26.2 2.9 %collective-permute-done.5.refs_10_ = bf16[3,128,256]{2,1,0:T(8,128)(2,1)S(1)} collective-permute-done((bf16[3,128,256]{2,1,0:T(8,128)(2,1)S(1)}, bf16[3,128,256]{2,1,0:T(8,128)(2,1)S(1)}, u32[]{:S(2)}, u32[]{:S(2)}) %collective-permute-start.5) | collective-permute-done | bytes 196640 | tf_op jit(solution)/shard_map/ppermute | solution.py:290
  29.0 0.0 collective-permute-done.6.refs_11_
  29.0 0.0 copy-done.3
  29.0 1.3 %shard_map.97 = (bf16[2,128,512]{2,1,0:T(8,128)(2,1)S(1)}, f32[4,64,256]{2,1,0:T(8,128)S(1)}, bf16[4,64,256]{2,1,0:T(8,128)(2,1)S(1)}, bf16[4,64,256]{2,1,0:T(8,128)(2,1)S(1)}, bf16[4,64,256]{2,1,0:T(8,128)(2,1)S(1)}) custom-call(s32[1]{0:T(128)S(6)} %copy.10.refs_0_, s32[1]{0:T(128)S(6)} %copy.11.refs_1_, bf16[1,2,1,960,512]{4,3,2,1,0:T(8,128)(2,1)S(1)} %bitcast.21, ...), custom_call_target="tpu_custom_call" | custom-call | flops 2147483648 | bytes 4194304 | tf_op jit(solution)/shard_map/pallas_call | solution.py:340
  30.4 2.7 %collective-permute-start.8 = (bf16[2,128,512]{2,1,0:T(8,128)(2,1)S(1)}, bf16[2,128,512]{2,1,0:T(8,128)(2,1)S(1)}, u32[]{:S(2)}, u32[]{:S(2)}) collective-permute-start(bf16[2,128,512]{2,1,0:T(8,128)(2,1)S(1)} %get-tuple-element.30.refs_2_), channel_id=1, source_target_pairs={{0,1},{1,0},{2,3},{3,2},{4,5},{5,4},{6,7},{7,6},{8,9},{9,8},{10,11... | collective-permute-start | bytes 786440 | tf_op jit(solution)/shard_map/ppermute | solution.py:293
  33.1 0.1 collective-permute-start.11
  33.2 0.9 %collective-permute-start.10 = (bf16[4,64,256]{2,1,0:T(8,128)(2,1)S(1)}, bf16[4,64,256]{2,1,0:T(8,128)(2,1)S(1)}, u32[]{:S(2)}, u32[]{:S(2)}) collective-permute-start(bf16[4,64,256]{2,1,0:T(8,128)(2,1)S(1)} %get-tuple-element.35), channel_id=1, source_target_pairs={{0,2},{1,3},{2,0},{3,1},{4,6},{5,7},{6,4},{7,5},{8,10},{9,11},{10,... | collective-permute-start | bytes 393224 | tf_op jit(solution)/shard_map/ppermute | solution.py:293
  34.1 1.1 %collective-permute-start.9 = (bf16[4,64,256]{2,1,0:T(8,128)(2,1)S(1)}, bf16[4,64,256]{2,1,0:T(8,128)(2,1)S(1)}, u32[]{:S(2)}, u32[]{:S(2)}) collective-permute-start(bf16[4,64,256]{2,1,0:T(8,128)(2,1)S(1)} %get-tuple-element.34), channel_id=1, source_target_pairs={{0,3},{1,2},{2,1},{3,0},{4,7},{5,6},{6,5},{7,4},{8,11},{9,10},{10,... | collective-permute-start | bytes 393224 | tf_op jit(solution)/shard_map/ppermute | solution.py:293
  35.2 0.0 collective-permute-done.8.refs_3_
  35.2 2.3 %shard_map.98 = bf16[1,2,1,960,512]{4,3,2,1,0:T(8,128)(2,1)} custom-call(s32[1]{0:T(128)S(6)} %copy.10.refs_0_, s32[1]{0:T(128)S(6)} %copy.11.refs_1_, bf16[2,128,512]{2,1,0:T(8,128)(2,1)S(1)} %get-tuple-element.30.refs_2_, bf16[2,128,512]{2,1,0:T(8,128)(2,1)S(1)} %collective-permute-done.8.refs_3_, bf16[128,512]{1,0:T(8,128)(2,1)S(1)} %get-tuple-element.31.refs_4_, ...), custom_call_target="tpu_custom_call" | custom-call | flops 2147483648 | bytes 4194304 | tf_op jit(solution)/shard_map/pallas_call | solution.py:358
  37.6 0.0 collective-permute-done.11
  37.6 0.2 collective-permute-done.10
  37.8 3.4 %collective-permute-done.9 = bf16[4,64,256]{2,1,0:T(8,128)(2,1)S(1)} collective-permute-done((bf16[4,64,256]{2,1,0:T(8,128)(2,1)S(1)}, bf16[4,64,256]{2,1,0:T(8,128)(2,1)S(1)}, u32[]{:S(2)}, u32[]{:S(2)}) %collective-permute-start.9) | collective-permute-done | bytes 131104 | tf_op jit(solution)/shard_map/ppermute | solution.py:293
  41.2 0.1 add_bitcast_fusion
  41.3 0.7 %fusion = (f32[2,256,64]{1,2,0:T(8,128)}, f32[2,256,64]{1,2,0:T(8,128)}) fusion(f32[4,256,64]{1,2,0:T(8,128)S(1)} %add_bitcast_fusion), kind=kLoop, calls=%fused_computation.10 | loop fusion | bytes 524288 | tf_op jit(solution)/shard_map/slice | solution.py:374
  (5 shorter events, 0.1 us)
Async XLA Ops:
  0.6 10.0 %collective-permute-start = (bf16[1,2,1,960,512]{4,3,2,1,0:T(8,128)(2,1)}, bf16[1,2,1,960,512]{4,3,2,1,0:T(8,128)(2,1)S(1)}, u32[]{:S(2)}, u32[]{:S(2)}) collective-permute-start(bf16[1,2,1,960,512]{4,3,2,1,0:T(8,128)(2,1)} %bitcast.19), channel_id=1, source_target_pairs={{0,1},{1,0},{2,3},{3,2},{4,5},{5,4},{6,7},{7,6},{8,9},{9,8},{10,11... | collective-permute-start | bytes 5898248 | tf_op jit(solution)/shard_map/ppermute | solution.py:293
  1.7 8.9 %collective-permute-start.1 = (bf16[2,1,96,512]{3,2,1,0:T(8,128)(2,1)S(1)}, bf16[2,1,96,512]{3,2,1,0:T(8,128)(2,1)S(1)}, u32[]{:S(2)}, u32[]{:S(2)}) collective-permute-start(bf16[2,1,96,512]{3,2,1,0:T(8,128)(2,1)S(1)} %slice.50), channel_id=1, source_target_pairs={{0,4},{4,8},{8,12},{12,16},{16,20},{20,24},{24,28},{1,5},{5,9},{9,... | collective-permute-start | bytes 589832 | tf_op jit(solution)/shard_map/ppermute | solution.py:295
  7.6 1.1 %copy-start = (bf16[2,4,512,96]{2,3,1,0:T(8,128)(2,1)S(1)}, bf16[2,4,512,96]{2,3,1,0:T(8,128)(2,1)}, u32[]{:S(2)}) copy-start(bf16[2,4,512,96]{2,3,1,0:T(8,128)(2,1)} %param.7) | copy-start | bytes 2359300
  7.6 1.2 %copy-start.2 = (bf16[3,3,96,128]{3,2,1,0:T(8,128)(2,1)S(1)}, bf16[3,3,96,128]{3,2,1,0:T(8,128)(2,1)}, u32[]{:S(2)}) copy-start(bf16[3,3,96,128]{3,2,1,0:T(8,128)(2,1)} %refs_3_.1) | copy-start | bytes 663556
  8.8 1.8 %copy-start.1 = (bf16[1,2,1,512,960]{3,4,2,1,0:T(8,128)(2,1)S(1)}, bf16[1,2,1,512,960]{3,4,2,1,0:T(8,128)(2,1)}, u32[]{:S(2)}) copy-start(bf16[1,2,1,512,960]{3,4,2,1,0:T(8,128)(2,1)} %param.12) | copy-start | bytes 5898244
  8.8 1.8 %copy-start.4 = (bf16[448,512]{1,0:T(8,128)(2,1)S(1)}, bf16[448,512]{1,0:T(8,128)(2,1)}, u32[]{:S(2)}) copy-start(bf16[448,512]{1,0:T(8,128)(2,1)} %constant.21.clone.refs_9_.refs_4_.refs_6_) | copy-start | bytes 1376260
  10.6 18.4 %copy-start.3 = (bf16[128,256]{1,0:T(8,128)(2,1)S(1)}, bf16[128,256]{1,0:T(8,128)(2,1)}, u32[]{:S(2)}) copy-start(bf16[128,256]{1,0:T(8,128)(2,1)} %refs_5_.3) | copy-start | bytes 196612
  12.0 6.9 %collective-permute-start.4 = (bf16[2,128,256]{2,1,0:T(8,128)(2,1)S(1)}, bf16[2,128,256]{2,1,0:T(8,128)(2,1)S(1)}, u32[]{:S(2)}, u32[]{:S(2)}) collective-permute-start(bf16[2,128,256]{2,1,0:T(8,128)(2,1)S(1)} %get-tuple-element.42), channel_id=1, source_target_pairs={{0,2},{1,3},{2,0},{3,1},{4,6},{5,7},{6,4},{7,5},{8,10},{9,11},{10,... | collective-permute-start | bytes 393224 | tf_op jit(solution)/shard_map/ppermute | solution.py:293
  12.6 10.0 %collective-permute-start.2 = (bf16[3,128,256]{2,1,0:T(8,128)(2,1)S(1)}, bf16[3,128,256]{2,1,0:T(8,128)(2,1)S(1)}, u32[]{:S(2)}, u32[]{:S(2)}) collective-permute-start(bf16[3,128,256]{2,1,0:T(8,128)(2,1)S(1)} %get-tuple-element.24), channel_id=1, source_target_pairs={{0,16},{16,0},{4,20},{20,4},{8,24},{24,8},{12,28},{28,12},{5,9},{9... | collective-permute-start | bytes 589832 | tf_op jit(solution)/shard_map/ppermute | solution.py:290
  13.3 10.4 %collective-permute-start.3 = (bf16[4,128,256]{2,1,0:T(8,128)(2,1)S(1)}, bf16[4,128,256]{2,1,0:T(8,128)(2,1)S(1)}, u32[]{:S(2)}, u32[]{:S(2)}) collective-permute-start(bf16[4,128,256]{2,1,0:T(8,128)(2,1)S(1)} %get-tuple-element.25), channel_id=1, source_target_pairs={{0,8},{8,0},{4,12},{12,4},{16,24},{24,16},{20,28},{28,20},{1,5},{5... | collective-permute-start | bytes 786440 | tf_op jit(solution)/shard_map/ppermute | solution.py:290
  19.0 10.0 %collective-permute-start.5 = (bf16[3,128,256]{2,1,0:T(8,128)(2,1)S(1)}, bf16[3,128,256]{2,1,0:T(8,128)(2,1)S(1)}, u32[]{:S(2)}, u32[]{:S(2)}) collective-permute-start(bf16[3,128,256]{2,1,0:T(8,128)(2,1)S(1)} %pad_maximum_fusion), channel_id=1, source_target_pairs={{8,16},{16,8},{12,20},{20,12},{1,13},{13,1},{5,17},{17,5},{9,21},{... | collective-permute-start | bytes 589832 | tf_op jit(solution)/shard_map/ppermute | solution.py:290
  22.0 7.1 %collective-permute-start.6 = (bf16[3,128,256]{2,1,0:T(8,128)(2,1)S(1)}, bf16[3,128,256]{2,1,0:T(8,128)(2,1)S(1)}, u32[]{:S(2)}, u32[]{:S(2)}) collective-permute-start(bf16[3,128,256]{2,1,0:T(8,128)(2,1)S(1)} %pad_maximum_fusion.1), channel_id=1, source_target_pairs={{13,25},{25,13},{17,29},{29,17},{15,27},{27,15},{19,31},{31,19}} | collective-permute-start | bytes 589832 | tf_op jit(solution)/shard_map/ppermute | solution.py:290
  22.7 3.5 %collective-permute-start.7 = (bf16[128,256]{1,0:T(8,128)(2,1)S(1)}, bf16[128,256]{1,0:T(8,128)(2,1)S(1)}, u32[]{:S(2)}, u32[]{:S(2)}) collective-permute-start(bf16[128,256]{1,0:T(8,128)(2,1)S(1)} %slice_bitcast_fusion), channel_id=1, source_target_pairs={{0,2},{1,3},{2,0},{3,1},{4,6},{5,7},{6,4},{7,5},{8,10},{9,11},{10,... | collective-permute-start | bytes 196616 | tf_op jit(solution)/shard_map/ppermute | solution.py:293
  30.4 4.9 %collective-permute-start.8 = (bf16[2,128,512]{2,1,0:T(8,128)(2,1)S(1)}, bf16[2,128,512]{2,1,0:T(8,128)(2,1)S(1)}, u32[]{:S(2)}, u32[]{:S(2)}) collective-permute-start(bf16[2,128,512]{2,1,0:T(8,128)(2,1)S(1)} %get-tuple-element.30.refs_2_), channel_id=1, source_target_pairs={{0,1},{1,0},{2,3},{3,2},{4,5},{5,4},{6,7},{7,6},{8,9},{9,8},{10,11... | collective-permute-start | bytes 786440 | tf_op jit(solution)/shard_map/ppermute | solution.py:293
  33.1 4.5 %collective-permute-start.11 = (bf16[4,64,256]{2,1,0:T(8,128)(2,1)S(1)}, bf16[4,64,256]{2,1,0:T(8,128)(2,1)S(1)}, u32[]{:S(2)}, u32[]{:S(2)}) collective-permute-start(bf16[4,64,256]{2,1,0:T(8,128)(2,1)S(1)} %get-tuple-element.36), channel_id=1, source_target_pairs={{0,1},{1,0},{2,3},{3,2},{4,5},{5,4},{6,7},{7,6},{8,9},{9,8},{10,11... | collective-permute-start | bytes 393224 | tf_op jit(solution)/shard_map/ppermute | solution.py:293
  33.2 4.6 %collective-permute-start.10 = (bf16[4,64,256]{2,1,0:T(8,128)(2,1)S(1)}, bf16[4,64,256]{2,1,0:T(8,128)(2,1)S(1)}, u32[]{:S(2)}, u32[]{:S(2)}) collective-permute-start(bf16[4,64,256]{2,1,0:T(8,128)(2,1)S(1)} %get-tuple-element.35), channel_id=1, source_target_pairs={{0,2},{1,3},{2,0},{3,1},{4,6},{5,7},{6,4},{7,5},{8,10},{9,11},{10,... | collective-permute-start | bytes 393224 | tf_op jit(solution)/shard_map/ppermute | solution.py:293
  34.1 7.1 %collective-permute-start.9 = (bf16[4,64,256]{2,1,0:T(8,128)(2,1)S(1)}, bf16[4,64,256]{2,1,0:T(8,128)(2,1)S(1)}, u32[]{:S(2)}, u32[]{:S(2)}) collective-permute-start(bf16[4,64,256]{2,1,0:T(8,128)(2,1)S(1)} %get-tuple-element.34), channel_id=1, source_target_pairs={{0,3},{1,2},{2,1},{3,0},{4,7},{5,6},{6,5},{7,4},{8,11},{9,10},{10,... | collective-permute-start | bytes 393224 | tf_op jit(solution)/shard_map/ppermute | solution.py:293

commit v8 on v7

--- a/solution.py
+++ b/solution.py
@@ -82,7 +82,7 @@
 
 def step_table(band):
     even = [(4, 0), (2, 0), (2, 1), (4, 1)]
-    odd = [(1, 1), (1, 0), (3, 0), (3, 1)]
+    odd = [(1, 0), (1, 1), (3, 0), (3, 1)]
     table = [even, odd]
     return [table[p % len(table)] for p in range(band)]
 
@@ -162,16 +162,20 @@
 
     target_ref[...] = target
     own_ref[...] = chosen(0)
-    for i, (step, message_ref) in enumerate(zip(steps, message_refs)):
-        blocks = [own_half(target)] if i in SPLIT_BLOCKS else pixel_halves(target)
+    for i, step in enumerate(steps):
         tile = chosen(step)
         if i in SPLIT_TERMS:
             for j, part in enumerate(pixel_halves(tile)):
                 terms_ref[SPLIT_TERMS.index(i), j] = part
         else:
-            blocks = [*blocks, *pixel_halves(tile)]
-        for j, part in enumerate(blocks):
-            message_ref[j] = part
+            blocks = [own_half(target)] if i in SPLIT_BLOCKS else []
+            for j, part in enumerate([*blocks, *pixel_halves(tile)]):
+                message_refs[i][j] = part
+
+
+def pieces_kernel(target_ref, pieces_ref):
+    for j, part in enumerate(pixel_halves(target_ref[...])):
+        pieces_ref[j] = part
 
 
 def gradient_kernel(
@@ -315,8 +319,9 @@
     piece = (mid, pixels // 2)
     split_terms = jax.ShapeDtypeStruct((len(SPLIT_TERMS), 2) + piece, BF16)
     messages = [
-        jax.ShapeDtypeStruct(((1 if i in SPLIT_BLOCKS else 2) + (0 if i in SPLIT_TERMS else 2),) + piece, BF16)
+        jax.ShapeDtypeStruct(((1 if i in SPLIT_BLOCKS else 0) + 2,) + piece, BF16)
         for i in range(steps)
+        if i not in SPLIT_TERMS
     ]
     target, source, own_term, terms, *messages = pl.pallas_call(
         lambda *refs: target_kernel(band, table, factor, *refs),
@@ -330,8 +335,17 @@
     first = lax.axis_index("band") // 2 == 0
     others = across(jnp.where(first, terms[:, 1], terms[:, 0]), 2)
     terms = jnp.where(first, terms[:, 0], terms[:, 1])
+    pieces = pl.pallas_call(
+        pieces_kernel,
+        out_shape=jax.ShapeDtypeStruct((2,) + piece, BF16),
+        compiler_params=params,
+        cost_estimate=pl.CostEstimate(flops=2**31, bytes_accessed=2**20, transcendentals=0),
+    )(target)
+    for i in range(len(messages)):
+        if i not in SPLIT_BLOCKS:
+            messages[i] = jnp.concatenate([pieces, messages[i]])
     for j, i in enumerate(SPLIT_TERMS):
-        messages[i] = jnp.concatenate([messages[i], terms[j : j + 1] + others[j : j + 1]])
+        messages.insert(i, jnp.concatenate([pieces, terms[j : j + 1] + others[j : j + 1]]))
     arrived = [along_rows(messages[i], i) for i in range(steps)]
     other_blocks = [across(arrived[i][0], 2) for i in SPLIT_BLOCKS]
 

time: 42.4 us -> 42.1 us (level)
  the two profiles are of different devices: /device:TPU:1 before, /device:TPU:25 now
where the time goes in v8:
time: 42.1 us; the launch traced here: 41.8 us
  waiting for transfers between devices  15.8 us (38%)
  starting transfers between devices  14.5 us (34%)
  Pallas kernels  6.62 us (16%)
  local copies, waits for them, and re-layouts  2.69 us (6%)
  between operations  2.08 us (5%)
    ppermute x4, waiting for transfers between devices, along_rows(): return lax.ppermute(x, ('rows', 'band'), pairs)  7.71 us
    ppermute x4, starting transfers between devices, along_rows(): return lax.ppermute(x, ('rows', 'band'), pairs)  6.09 us
    ppermute x7, waiting for transfers between devices, across(): return lax.ppermute(x, 'band', [(p, p ^ k) for p in range(band)])  5.9 us
    ppermute x7, starting transfers between devices, across(): return lax.ppermute(x, 'band', [(p, p ^ k) for p in range(band)])  5.23 us
    ppermute x1, starting transfers between devices, shards(): lax.ppermute(frames[:, -1:], 'rows', [(i, i + 1) for i in range(row_block...  3.15 us
    pallas_call x1, Pallas kernels, shards(): pl.pallas_call(lambda *refs: pyramid_kernel(band, factor, *refs), grid=(s...  2.33 us
    ppermute x1, waiting for transfers between devices, shards(): lax.ppermute(frames[:, -1:], 'rows', [(i, i + 1) for i in range(row_block...  2.21 us
    pallas_call x1, Pallas kernels, shards(): pl.pallas_call(local_rows_kernel, out_shape=(jax.ShapeDtypeStruct((mid, c...  1.44 us
  transfers between devices with their start and end apart: 12, of which 6 were waited for; matrix products, arithmetic and copies ran while one was open for 2% of the time, Pallas kernels for 9%

profile of v8, /device:TPU:25, one launch (start us, length us, event | category | flops | bytes accessed | tf_op | source)
XLA Modules:
  0.0 41.8 jit_solution(12409984948612855402)
XLA Ops:
  0.6 0.7 %collective-permute-start = (bf16[1,2,1,960,512]{4,3,2,1,0:T(8,128)(2,1)}, bf16[1,2,1,960,512]{4,3,2,1,0:T(8,128)(2,1)S(1)}, u32[]{:S(2)}, u32[]{:S(2)}) collective-permute-start(bf16[1,2,1,960,512]{4,3,2,1,0:T(8,128)(2,1)} %bitcast.19), channel_id=1, source_target_pairs={{0,1},{1,0},{2,3},{3,2},{4,5},{5,4},{6,7},{7,6},{8,9},{9,8},{10,11... | collective-permute-start | bytes 5898248 | tf_op jit(solution)/shard_map/ppermute | solution.py:297
  1.4 0.9 %slice.50 = bf16[2,1,96,512]{3,2,1,0:T(8,128)(2,1)S(1)} slice(bf16[2,4,96,512]{3,2,1,0:T(8,128)(2,1)} %bitcast.17), slice={[0:2], [3:4], [0:96], [0:512]} | slice | bytes 393216 | tf_op jit(solution)/shard_map/slice | solution.py:299
  2.3 3.1 %collective-permute-start.1 = (bf16[2,1,96,512]{3,2,1,0:T(8,128)(2,1)S(1)}, bf16[2,1,96,512]{3,2,1,0:T(8,128)(2,1)S(1)}, u32[]{:S(2)}, u32[]{:S(2)}) collective-permute-start(bf16[2,1,96,512]{3,2,1,0:T(8,128)(2,1)S(1)} %slice.50), channel_id=1, source_target_pairs={{0,4},{4,8},{8,12},{12,16},{16,20},{20,24},{24,28},{1,5},{5,9},{9,... | collective-permute-start | bytes 589832 | tf_op jit(solution)/shard_map/ppermute | solution.py:299
  6.8 0.0 copy-start
  6.8 0.0 copy-start.2
  6.8 0.1 shard_map.94.picker_ref.refs_6_
  7.0 1.0 %copy-done = bf16[2,4,512,96]{2,3,1,0:T(8,128)(2,1)S(1)} copy-done((bf16[2,4,512,96]{2,3,1,0:T(8,128)(2,1)S(1)}, bf16[2,4,512,96]{2,3,1,0:T(8,128)(2,1)}, u32[]{:S(2)}) %copy-start) | copy-done | bytes 786456
  7.9 0.0 copy-done.2
  8.0 0.0 copy-start.1
  8.0 0.0 copy-start.4
  8.0 1.4 %shard_map.95 = (bf16[128,512]{1,0:T(8,128)(2,1)S(1)}, f32[128,512]{1,0:T(8,128)S(1)}) custom-call(bf16[512,768]{1,0:T(8,128)(2,1)S(1)} %shard_map.94.picker_ref.refs_6_, bf16[2,4,96,512]{3,2,1,0:T(8,128)(2,1)S(1)} %bitcast.18, bf16[3,3,96,128]{3,2,1,0:T(8,128)(2,1)S(1)} %copy-done.2), custom_call_target="tpu_custom_call" | custom-call | flops 2147483648 | bytes 2097152 | tf_op jit(solution)/shard_map/pallas_call | solution.py:307
  9.4 2.2 %collective-permute-done.1.refs_2_ = bf16[2,1,96,512]{3,2,1,0:T(8,128)(2,1)S(1)} collective-permute-done((bf16[2,1,96,512]{3,2,1,0:T(8,128)(2,1)S(1)}, bf16[2,1,96,512]{3,2,1,0:T(8,128)(2,1)S(1)}, u32[]{:S(2)}, u32[]{:S(2)}) %collective-permute-start.1) | collective-permute-done | bytes 196640 | tf_op jit(solution)/shard_map/ppermute | solution.py:299
  11.6 0.0 collective-permute-done.refs_8_.refs_3_
  11.6 0.0 copy-done.1
  11.6 0.0 copy-done.4
  11.6 1.4 %shard_map.96 = (bf16[128,512]{1,0:T(8,128)(2,1)S(1)}, bf16[128,512]{1,0:T(8,128)(2,1)S(1)}, bf16[128,512]{1,0:T(8,128)(2,1)S(1)}, bf16[2,2,128,256]{3,2,1,0:T(8...) custom-call(s32[1]{0:T(128)S(6)} %copy.10.refs_0_, s32[1]{0:T(128)S(6)} %copy.11.refs_1_, ...), custom_call_target="tpu_custom_call" | custom-call | flops 2147483648 | bytes 4194304 | tf_op jit(solution)/shard_map/pallas_call | solution.py:326
  13.0 1.1 %collective-permute-start.2 = (bf16[3,128,256]{2,1,0:T(8,128)(2,1)S(1)}, bf16[3,128,256]{2,1,0:T(8,128)(2,1)S(1)}, u32[]{:S(2)}, u32[]{:S(2)}) collective-permute-start(bf16[3,128,256]{2,1,0:T(8,128)(2,1)S(1)} %get-tuple-element.22), channel_id=1, source_target_pairs={{0,16},{16,0},{4,20},{20,4},{8,24},{24,8},{12,28},{28,12},{1,5},{5... | collective-permute-start | bytes 589832 | tf_op jit(solution)/shard_map/ppermute | solution.py:294
  14.1 1.3 %collective-permute-start.4 = (bf16[2,128,256]{2,1,0:T(8,128)(2,1)S(1)}, bf16[2,128,256]{2,1,0:T(8,128)(2,1)S(1)}, u32[]{:S(2)}, u32[]{:S(2)}) collective-permute-start(bf16[2,128,256]{2,1,0:T(8,128)(2,1)S(1)} %get-tuple-element.38), channel_id=1, source_target_pairs={{0,2},{1,3},{2,0},{3,1},{4,6},{5,7},{6,4},{7,5},{8,10},{9,11},{10,... | collective-permute-start | bytes 393224 | tf_op jit(solution)/shard_map/ppermute | solution.py:297
  15.4 0.0 copy-start.3
  15.4 1.9 %collective-permute-start.3 = (bf16[4,128,256]{2,1,0:T(8,128)(2,1)S(1)}, bf16[4,128,256]{2,1,0:T(8,128)(2,1)S(1)}, u32[]{:S(2)}, u32[]{:S(2)}) collective-permute-start(bf16[4,128,256]{2,1,0:T(8,128)(2,1)S(1)} %pad_maximum_fusion), channel_id=1, source_target_pairs={{0,8},{8,0},{4,12},{12,4},{16,24},{24,16},{20,28},{28,20},{5,9},{9... | collective-permute-start | bytes 786440 | tf_op jit(solution)/shard_map/ppermute | solution.py:294
  17.4 1.9 %collective-permute-done.4 = bf16[2,128,256]{2,1,0:T(8,128)(2,1)S(1)} collective-permute-done((bf16[2,128,256]{2,1,0:T(8,128)(2,1)S(1)}, bf16[2,128,256]{2,1,0:T(8,128)(2,1)S(1)}, u32[]{:S(2)}, u32[]{:S(2)}) %collective-permute-start.4) | collective-permute-done | bytes 131104 | tf_op jit(solution)/shard_map/ppermute | solution.py:297
  19.3 0.7 %collective-permute-start.5 = (bf16[3,128,256]{2,1,0:T(8,128)(2,1)S(1)}, bf16[3,128,256]{2,1,0:T(8,128)(2,1)S(1)}, u32[]{:S(2)}, u32[]{:S(2)}) collective-permute-start(bf16[3,128,256]{2,1,0:T(8,128)(2,1)S(1)} %get-tuple-element.40), channel_id=1, source_target_pairs={{8,16},{16,8},{12,20},{20,12},{1,13},{13,1},{5,17},{17,5},{9,21},{... | collective-permute-start | bytes 589832 | tf_op jit(solution)/shard_map/ppermute | solution.py:294
  20.0 2.4 %collective-permute-start.6 = (bf16[3,128,256]{2,1,0:T(8,128)(2,1)S(1)}, bf16[3,128,256]{2,1,0:T(8,128)(2,1)S(1)}, u32[]{:S(2)}, u32[]{:S(2)}) collective-permute-start(bf16[3,128,256]{2,1,0:T(8,128)(2,1)S(1)} %get-tuple-element.39), channel_id=1, source_target_pairs={{13,25},{25,13},{17,29},{29,17},{15,27},{27,15},{19,31},{31,19}} | collective-permute-start | bytes 589832 | tf_op jit(solution)/shard_map/ppermute | solution.py:294
  22.4 0.0 collective-permute-done.2.refs_8_
  22.4 1.0 %collective-permute-start.7 = (bf16[128,256]{1,0:T(8,128)(2,1)S(1)}, bf16[128,256]{1,0:T(8,128)(2,1)S(1)}, u32[]{:S(2)}, u32[]{:S(2)}) collective-permute-start(bf16[128,256]{1,0:T(8,128)(2,1)S(1)} %slice_bitcast_fusion), channel_id=1, source_target_pairs={{0,2},{1,3},{2,0},{3,1},{4,6},{5,7},{6,4},{7,5},{8,10},{9,11},{10,... | collective-permute-start | bytes 196616 | tf_op jit(solution)/shard_map/ppermute | solution.py:297
  23.4 4.8 %collective-permute-done.3.refs_9_ = bf16[4,128,256]{2,1,0:T(8,128)(2,1)S(1)} collective-permute-done((bf16[4,128,256]{2,1,0:T(8,128)(2,1)S(1)}, bf16[4,128,256]{2,1,0:T(8,128)(2,1)S(1)}, u32[]{:S(2)}, u32[]{:S(2)}) %collective-permute-start.3) | collective-permute-done | bytes 262176 | tf_op jit(solution)/shard_map/ppermute | solution.py:294
  28.2 0.0 collective-permute-done.7.refs_12_
  28.2 0.0 collective-permute-done.5.refs_10_
  28.2 2.9 %collective-permute-done.6.refs_11_ = bf16[3,128,256]{2,1,0:T(8,128)(2,1)S(1)} collective-permute-done((bf16[3,128,256]{2,1,0:T(8,128)(2,1)S(1)}, bf16[3,128,256]{2,1,0:T(8,128)(2,1)S(1)}, u32[]{:S(2)}, u32[]{:S(2)}) %collective-permute-start.6) | collective-permute-done | bytes 196640 | tf_op jit(solution)/shard_map/ppermute | solution.py:294
  31.1 0.0 copy-done.3
  31.1 1.3 %shard_map.98 = (bf16[2,128,512]{2,1,0:T(8,128)(2,1)S(1)}, f32[4,64,256]{2,1,0:T(8,128)S(1)}, bf16[4,64,256]{2,1,0:T(8,128)(2,1)S(1)}, bf16[4,64,256]{2,1,0:T(8,128)(2,1)S(1)}, bf16[4,64,256]{2,1,0:T(8,128)(2,1)S(1)}) custom-call(s32[1]{0:T(128)S(6)} %copy.10.refs_0_, s32[1]{0:T(128)S(6)} %copy.11.refs_1_, bf16[1,2,1,960,512]{4,3,2,1,0:T(8,128)(2,1)S(1)} %bitcast.21, ...), custom_call_target="tpu_custom_call" | custom-call | flops 2147483648 | bytes 4194304 | tf_op jit(solution)/shard_map/pallas_call | solution.py:354
  32.4 0.1 collective-permute-start.8
  32.5 0.5 %collective-permute-start.11 = (bf16[4,64,256]{2,1,0:T(8,128)(2,1)S(1)}, bf16[4,64,256]{2,1,0:T(8,128)(2,1)S(1)}, u32[]{:S(2)}, u32[]{:S(2)}) collective-permute-start(bf16[4,64,256]{2,1,0:T(8,128)(2,1)S(1)} %get-tuple-element.32), channel_id=1, source_target_pairs={{0,1},{1,0},{2,3},{3,2},{4,5},{5,4},{6,7},{7,6},{8,9},{9,8},{10,11... | collective-permute-start | bytes 393224 | tf_op jit(solution)/shard_map/ppermute | solution.py:297
  33.0 0.9 %collective-permute-start.10 = (bf16[4,64,256]{2,1,0:T(8,128)(2,1)S(1)}, bf16[4,64,256]{2,1,0:T(8,128)(2,1)S(1)}, u32[]{:S(2)}, u32[]{:S(2)}) collective-permute-start(bf16[4,64,256]{2,1,0:T(8,128)(2,1)S(1)} %get-tuple-element.31), channel_id=1, source_target_pairs={{0,2},{1,3},{2,0},{3,1},{4,6},{5,7},{6,4},{7,5},{8,10},{9,11},{10,... | collective-permute-start | bytes 393224 | tf_op jit(solution)/shard_map/ppermute | solution.py:297
  33.9 0.8 %collective-permute-start.9 = (bf16[4,64,256]{2,1,0:T(8,128)(2,1)S(1)}, bf16[4,64,256]{2,1,0:T(8,128)(2,1)S(1)}, u32[]{:S(2)}, u32[]{:S(2)}) collective-permute-start(bf16[4,64,256]{2,1,0:T(8,128)(2,1)S(1)} %get-tuple-element.30), channel_id=1, source_target_pairs={{0,3},{1,2},{2,1},{3,0},{4,7},{5,6},{6,5},{7,4},{8,11},{9,10},{10,... | collective-permute-start | bytes 393224 | tf_op jit(solution)/shard_map/ppermute | solution.py:297
  34.7 0.0 collective-permute-done.8.refs_3_
  34.7 2.3 %shard_map.99 = bf16[1,2,1,960,512]{4,3,2,1,0:T(8,128)(2,1)} custom-call(s32[1]{0:T(128)S(6)} %copy.10.refs_0_, s32[1]{0:T(128)S(6)} %copy.11.refs_1_, bf16[2,128,512]{2,1,0:T(8,128)(2,1)S(1)} %get-tuple-element.26.refs_2_, bf16[2,128,512]{2,1,0:T(8,128)(2,1)S(1)} %collective-permute-done.8.refs_3_, bf16[128,512]{1,0:T(8,128)(2,1)S(1)} %get-tuple-element.27.refs_4_, ...), custom_call_target="tpu_custom_call" | custom-call | flops 2147483648 | bytes 4194304 | tf_op jit(solution)/shard_map/pallas_call | solution.py:372
  37.1 0.0 collective-permute-done.11
  37.1 1.0 %collective-permute-done.10 = bf16[4,64,256]{2,1,0:T(8,128)(2,1)S(1)} collective-permute-done((bf16[4,64,256]{2,1,0:T(8,128)(2,1)S(1)}, bf16[4,64,256]{2,1,0:T(8,128)(2,1)S(1)}, u32[]{:S(2)}, u32[]{:S(2)}) %collective-permute-start.10) | collective-permute-done | bytes 131104 | tf_op jit(solution)/shard_map/ppermute | solution.py:297
  38.1 3.0 %collective-permute-done.9 = bf16[4,64,256]{2,1,0:T(8,128)(2,1)S(1)} collective-permute-done((bf16[4,64,256]{2,1,0:T(8,128)(2,1)S(1)}, bf16[4,64,256]{2,1,0:T(8,128)(2,1)S(1)}, u32[]{:S(2)}, u32[]{:S(2)}) %collective-permute-start.9) | collective-permute-done | bytes 131104 | tf_op jit(solution)/shard_map/ppermute | solution.py:297
  41.1 0.1 add_bitcast_fusion
  41.1 0.7 %fusion = (f32[2,256,64]{1,2,0:T(8,128)}, f32[2,256,64]{1,2,0:T(8,128)}) fusion(f32[4,256,64]{1,2,0:T(8,128)S(1)} %add_bitcast_fusion), kind=kLoop, calls=%fused_computation.11 | loop fusion | bytes 524288 | tf_op jit(solution)/shard_map/slice | solution.py:388
  (6 shorter events, 0.1 us)
Async XLA Ops:
  0.6 11.0 %collective-permute-start = (bf16[1,2,1,960,512]{4,3,2,1,0:T(8,128)(2,1)}, bf16[1,2,1,960,512]{4,3,2,1,0:T(8,128)(2,1)S(1)}, u32[]{:S(2)}, u32[]{:S(2)}) collective-permute-start(bf16[1,2,1,960,512]{4,3,2,1,0:T(8,128)(2,1)} %bitcast.19), channel_id=1, source_target_pairs={{0,1},{1,0},{2,3},{3,2},{4,5},{5,4},{6,7},{7,6},{8,9},{9,8},{10,11... | collective-permute-start | bytes 5898248 | tf_op jit(solution)/shard_map/ppermute | solution.py:297
  2.3 9.3 %collective-permute-start.1 = (bf16[2,1,96,512]{3,2,1,0:T(8,128)(2,1)S(1)}, bf16[2,1,96,512]{3,2,1,0:T(8,128)(2,1)S(1)}, u32[]{:S(2)}, u32[]{:S(2)}) collective-permute-start(bf16[2,1,96,512]{3,2,1,0:T(8,128)(2,1)S(1)} %slice.50), channel_id=1, source_target_pairs={{0,4},{4,8},{8,12},{12,16},{16,20},{20,24},{24,28},{1,5},{5,9},{9,... | collective-permute-start | bytes 589832 | tf_op jit(solution)/shard_map/ppermute | solution.py:299
  6.8 1.1 %copy-start = (bf16[2,4,512,96]{2,3,1,0:T(8,128)(2,1)S(1)}, bf16[2,4,512,96]{2,3,1,0:T(8,128)(2,1)}, u32[]{:S(2)}) copy-start(bf16[2,4,512,96]{2,3,1,0:T(8,128)(2,1)} %param.7) | copy-start | bytes 2359300
  6.8 1.2 %copy-start.2 = (bf16[3,3,96,128]{3,2,1,0:T(8,128)(2,1)S(1)}, bf16[3,3,96,128]{3,2,1,0:T(8,128)(2,1)}, u32[]{:S(2)}) copy-start(bf16[3,3,96,128]{3,2,1,0:T(8,128)(2,1)} %refs_3_.1) | copy-start | bytes 663556
  8.0 3.7 %copy-start.1 = (bf16[1,2,1,512,960]{3,4,2,1,0:T(8,128)(2,1)S(1)}, bf16[1,2,1,512,960]{3,4,2,1,0:T(8,128)(2,1)}, u32[]{:S(2)}) copy-start(bf16[1,2,1,512,960]{3,4,2,1,0:T(8,128)(2,1)} %param.12) | copy-start | bytes 5898244
  8.0 3.7 %copy-start.4 = (bf16[448,512]{1,0:T(8,128)(2,1)S(1)}, bf16[448,512]{1,0:T(8,128)(2,1)}, u32[]{:S(2)}) copy-start(bf16[448,512]{1,0:T(8,128)(2,1)} %constant.21.clone.refs_9_.refs_4_.refs_6_) | copy-start | bytes 1376260
  13.0 9.4 %collective-permute-start.2 = (bf16[3,128,256]{2,1,0:T(8,128)(2,1)S(1)}, bf16[3,128,256]{2,1,0:T(8,128)(2,1)S(1)}, u32[]{:S(2)}, u32[]{:S(2)}) collective-permute-start(bf16[3,128,256]{2,1,0:T(8,128)(2,1)S(1)} %get-tuple-element.22), channel_id=1, source_target_pairs={{0,16},{16,0},{4,20},{20,4},{8,24},{24,8},{12,28},{28,12},{1,5},{5... | collective-permute-start | bytes 589832 | tf_op jit(solution)/shard_map/ppermute | solution.py:294
  14.1 5.1 %collective-permute-start.4 = (bf16[2,128,256]{2,1,0:T(8,128)(2,1)S(1)}, bf16[2,128,256]{2,1,0:T(8,128)(2,1)S(1)}, u32[]{:S(2)}, u32[]{:S(2)}) collective-permute-start(bf16[2,128,256]{2,1,0:T(8,128)(2,1)S(1)} %get-tuple-element.38), channel_id=1, source_target_pairs={{0,2},{1,3},{2,0},{3,1},{4,6},{5,7},{6,4},{7,5},{8,10},{9,11},{10,... | collective-permute-start | bytes 393224 | tf_op jit(solution)/shard_map/ppermute | solution.py:297
  15.4 15.7 %copy-start.3 = (bf16[128,256]{1,0:T(8,128)(2,1)S(1)}, bf16[128,256]{1,0:T(8,128)(2,1)}, u32[]{:S(2)}) copy-start(bf16[128,256]{1,0:T(8,128)(2,1)} %refs_5_.3) | copy-start | bytes 196612
  15.4 12.8 %collective-permute-start.3 = (bf16[4,128,256]{2,1,0:T(8,128)(2,1)S(1)}, bf16[4,128,256]{2,1,0:T(8,128)(2,1)S(1)}, u32[]{:S(2)}, u32[]{:S(2)}) collective-permute-start(bf16[4,128,256]{2,1,0:T(8,128)(2,1)S(1)} %pad_maximum_fusion), channel_id=1, source_target_pairs={{0,8},{8,0},{4,12},{12,4},{16,24},{24,16},{20,28},{28,20},{5,9},{9... | collective-permute-start | bytes 786440 | tf_op jit(solution)/shard_map/ppermute | solution.py:294
  19.3 8.9 %collective-permute-start.5 = (bf16[3,128,256]{2,1,0:T(8,128)(2,1)S(1)}, bf16[3,128,256]{2,1,0:T(8,128)(2,1)S(1)}, u32[]{:S(2)}, u32[]{:S(2)}) collective-permute-start(bf16[3,128,256]{2,1,0:T(8,128)(2,1)S(1)} %get-tuple-element.40), channel_id=1, source_target_pairs={{8,16},{16,8},{12,20},{20,12},{1,13},{13,1},{5,17},{17,5},{9,21},{... | collective-permute-start | bytes 589832 | tf_op jit(solution)/shard_map/ppermute | solution.py:294
  20.0 11.1 %collective-permute-start.6 = (bf16[3,128,256]{2,1,0:T(8,128)(2,1)S(1)}, bf16[3,128,256]{2,1,0:T(8,128)(2,1)S(1)}, u32[]{:S(2)}, u32[]{:S(2)}) collective-permute-start(bf16[3,128,256]{2,1,0:T(8,128)(2,1)S(1)} %get-tuple-element.39), channel_id=1, source_target_pairs={{13,25},{25,13},{17,29},{29,17},{15,27},{27,15},{19,31},{31,19}} | collective-permute-start | bytes 589832 | tf_op jit(solution)/shard_map/ppermute | solution.py:294
  22.4 5.8 %collective-permute-start.7 = (bf16[128,256]{1,0:T(8,128)(2,1)S(1)}, bf16[128,256]{1,0:T(8,128)(2,1)S(1)}, u32[]{:S(2)}, u32[]{:S(2)}) collective-permute-start(bf16[128,256]{1,0:T(8,128)(2,1)S(1)} %slice_bitcast_fusion), channel_id=1, source_target_pairs={{0,2},{1,3},{2,0},{3,1},{4,6},{5,7},{6,4},{7,5},{8,10},{9,11},{10,... | collective-permute-start | bytes 196616 | tf_op jit(solution)/shard_map/ppermute | solution.py:297
  32.4 2.3 %collective-permute-start.8 = (bf16[2,128,512]{2,1,0:T(8,128)(2,1)S(1)}, bf16[2,128,512]{2,1,0:T(8,128)(2,1)S(1)}, u32[]{:S(2)}, u32[]{:S(2)}) collective-permute-start(bf16[2,128,512]{2,1,0:T(8,128)(2,1)S(1)} %get-tuple-element.26.refs_2_), channel_id=1, source_target_pairs={{0,1},{1,0},{2,3},{3,2},{4,5},{5,4},{6,7},{7,6},{8,9},{9,8},{10,11... | collective-permute-start | bytes 786440 | tf_op jit(solution)/shard_map/ppermute | solution.py:297
  32.5 4.5 %collective-permute-start.11 = (bf16[4,64,256]{2,1,0:T(8,128)(2,1)S(1)}, bf16[4,64,256]{2,1,0:T(8,128)(2,1)S(1)}, u32[]{:S(2)}, u32[]{:S(2)}) collective-permute-start(bf16[4,64,256]{2,1,0:T(8,128)(2,1)S(1)} %get-tuple-element.32), channel_id=1, source_target_pairs={{0,1},{1,0},{2,3},{3,2},{4,5},{5,4},{6,7},{7,6},{8,9},{9,8},{10,11... | collective-permute-start | bytes 393224 | tf_op jit(solution)/shard_map/ppermute | solution.py:297
  33.0 5.1 %collective-permute-start.10 = (bf16[4,64,256]{2,1,0:T(8,128)(2,1)S(1)}, bf16[4,64,256]{2,1,0:T(8,128)(2,1)S(1)}, u32[]{:S(2)}, u32[]{:S(2)}) collective-permute-start(bf16[4,64,256]{2,1,0:T(8,128)(2,1)S(1)} %get-tuple-element.31), channel_id=1, source_target_pairs={{0,2},{1,3},{2,0},{3,1},{4,6},{5,7},{6,4},{7,5},{8,10},{9,11},{10,... | collective-permute-start | bytes 393224 | tf_op jit(solution)/shard_map/ppermute | solution.py:297
  33.9 7.2 %collective-permute-start.9 = (bf16[4,64,256]{2,1,0:T(8,128)(2,1)S(1)}, bf16[4,64,256]{2,1,0:T(8,128)(2,1)S(1)}, u32[]{:S(2)}, u32[]{:S(2)}) collective-permute-start(bf16[4,64,256]{2,1,0:T(8,128)(2,1)S(1)} %get-tuple-element.30), channel_id=1, source_target_pairs={{0,3},{1,2},{2,1},{3,0},{4,7},{5,6},{6,5},{7,4},{8,11},{9,10},{10,... | collective-permute-start | bytes 393224 | tf_op jit(solution)/shard_map/ppermute | solution.py:297

commit v9 on v8

--- a/solution.py
+++ b/solution.py
@@ -231,6 +231,16 @@
                 sent_refs[k - 1][part] = out.astype(BF16)
 
 
+def total_kernel(kept_ref, *refs):
+    received, out_refs = refs[:-2], refs[-2:]
+    rows = out_refs[0].shape[0]
+    for i, out_ref in enumerate(out_refs):
+        total = kept_ref[i * rows : (i + 1) * rows]
+        for part in received:
+            total = total + part[i * rows : (i + 1) * rows].astype(F32)
+        out_ref[...] = total
+
+
 def pyramid_kernel(
     band, factor, start_ref, count_ref, held_ref, other_ref, source_ref, proj_ref, spread_ref, pyramid_ref, scaled_ref
 ):
@@ -381,11 +391,14 @@
         cost_estimate=pl.CostEstimate(flops=2**31, bytes_accessed=2**22, transcendentals=0),
     )(band_start, band_count, held, other, source, proj_weight, spread)
 
-    total, pyramid = lax.optimization_barrier((kept, pyramid))
-    for x in received:
-        total = total + x.astype(F32)
-    total = jnp.swapaxes(total, 1, 2)
-    return (jnp.swapaxes(pyramid, 3, 4), total[: out_parts // 2], total[out_parts // 2 :])
+    kept, pyramid = lax.optimization_barrier((kept, pyramid))
+    half_part = jax.ShapeDtypeStruct((out_parts // 2, share, half), F32)
+    source_grad, target_grad = pl.pallas_call(
+        total_kernel,
+        out_shape=(half_part, half_part),
+        compiler_params=params,
+    )(kept, *received)
+    return (jnp.swapaxes(pyramid, 3, 4), jnp.swapaxes(source_grad, 1, 2), jnp.swapaxes(target_grad, 1, 2))
 
 
 def solution(mesh):

time: 42.1 us -> 42.2 us (level)
  local copies, waits for them, and re-layouts: 2.69 us -> 1.97 us
  Pallas kernels: 6.62 us -> 7.34 us
    pallas_call x0 -> x1, Pallas kernels: none -> 0.73 us  [shards(): pl.pallas_call(total_kernel, out_shape=(half_part, half_part), compiler_p...]
    slice x1 -> x0, local copies, waits for them, and re-layouts: 0.72 us -> none  [shards(): total[out_parts // 2:]]
  transfers between devices with their start and end apart: 12 -> 12, of which waited for: 6 -> 6; matrix products, arithmetic and copies ran while one was open for 2% -> 3% of each run, Pallas kernels for 9% -> 9%
where the time goes in v9:
time: 42.2 us; the launch traced here: 41.5 us
  waiting for transfers between devices  15.6 us (37%)
  starting transfers between devices  14.5 us (34%)
  Pallas kernels  7.34 us (17%)
  between operations  2.08 us (5%)
  local copies, waits for them, and re-layouts  1.97 us (5%)
    ppermute x4, waiting for transfers between devices, along_rows(): return lax.ppermute(x, ('rows', 'band'), pairs)  7.54 us
    ppermute x4, starting transfers between devices, along_rows(): return lax.ppermute(x, ('rows', 'band'), pairs)  6 us
    ppermute x7, waiting for transfers between devices, across(): return lax.ppermute(x, 'band', [(p, p ^ k) for p in range(band)])  5.81 us
    ppermute x7, starting transfers between devices, across(): return lax.ppermute(x, 'band', [(p, p ^ k) for p in range(band)])  5.32 us
    ppermute x1, starting transfers between devices, shards(): lax.ppermute(frames[:, -1:], 'rows', [(i, i + 1) for i in range(row_block...  3.15 us
    pallas_call x1, Pallas kernels, shards(): pl.pallas_call(lambda *refs: pyramid_kernel(band, factor, *refs), grid=(s...  2.33 us
    ppermute x1, waiting for transfers between devices, shards(): lax.ppermute(frames[:, -1:], 'rows', [(i, i + 1) for i in range(row_block...  2.21 us
    pallas_call x1, Pallas kernels, shards(): pl.pallas_call(local_rows_kernel, out_shape=(jax.ShapeDtypeStruct((mid, c...  1.44 us
  transfers between devices with their start and end apart: 12, of which 6 were waited for; matrix products, arithmetic and copies ran while one was open for 3% of the time, Pallas kernels for 9%

profile of v9, /device:TPU:25, one launch (start us, length us, event | category | flops | bytes accessed | tf_op | source)
XLA Modules:
  0.0 41.5 jit_solution(15244269641609345181)
XLA Ops:
  0.6 0.7 %collective-permute-start = (bf16[1,2,1,960,512]{4,3,2,1,0:T(8,128)(2,1)}, bf16[1,2,1,960,512]{4,3,2,1,0:T(8,128)(2,1)S(1)}, u32[]{:S(2)}, u32[]{:S(2)}) collective-permute-start(bf16[1,2,1,960,512]{4,3,2,1,0:T(8,128)(2,1)} %bitcast.19), channel_id=1, source_target_pairs={{0,1},{1,0},{2,3},{3,2},{4,5},{5,4},{6,7},{7,6},{8,9},{9,8},{10,11... | collective-permute-start | bytes 5898248 | tf_op jit(solution)/shard_map/ppermute | solution.py:307
  1.4 0.9 %slice.42 = bf16[2,1,96,512]{3,2,1,0:T(8,128)(2,1)S(1)} slice(bf16[2,4,96,512]{3,2,1,0:T(8,128)(2,1)} %bitcast.17), slice={[0:2], [3:4], [0:96], [0:512]} | slice | bytes 393216 | tf_op jit(solution)/shard_map/slice | solution.py:309
  2.3 3.1 %collective-permute-start.1 = (bf16[2,1,96,512]{3,2,1,0:T(8,128)(2,1)S(1)}, bf16[2,1,96,512]{3,2,1,0:T(8,128)(2,1)S(1)}, u32[]{:S(2)}, u32[]{:S(2)}) collective-permute-start(bf16[2,1,96,512]{3,2,1,0:T(8,128)(2,1)S(1)} %slice.42), channel_id=1, source_target_pairs={{0,4},{4,8},{8,12},{12,16},{16,20},{20,24},{24,28},{1,5},{5,9},{9,... | collective-permute-start | bytes 589832 | tf_op jit(solution)/shard_map/ppermute | solution.py:309
  6.8 0.0 copy-start
  6.8 0.0 copy-start.2
  6.8 0.1 shard_map.94.picker_ref.refs_6_
  7.0 1.0 %copy-done = bf16[2,4,512,96]{2,3,1,0:T(8,128)(2,1)S(1)} copy-done((bf16[2,4,512,96]{2,3,1,0:T(8,128)(2,1)S(1)}, bf16[2,4,512,96]{2,3,1,0:T(8,128)(2,1)}, u32[]{:S(2)}) %copy-start) | copy-done | bytes 786456
  7.9 0.0 copy-done.2
  8.0 0.0 copy-start.1
  8.0 0.0 copy-start.4
  8.0 1.4 %shard_map.95 = (bf16[128,512]{1,0:T(8,128)(2,1)S(1)}, f32[128,512]{1,0:T(8,128)S(1)}) custom-call(bf16[512,768]{1,0:T(8,128)(2,1)S(1)} %shard_map.94.picker_ref.refs_6_, bf16[2,4,96,512]{3,2,1,0:T(8,128)(2,1)S(1)} %bitcast.18, bf16[3,3,96,128]{3,2,1,0:T(8,128)(2,1)S(1)} %copy-done.2), custom_call_target="tpu_custom_call" | custom-call | flops 2147483648 | bytes 2097152 | tf_op jit(solution)/shard_map/pallas_call | solution.py:317
  9.4 2.2 %collective-permute-done.1.refs_2_ = bf16[2,1,96,512]{3,2,1,0:T(8,128)(2,1)S(1)} collective-permute-done((bf16[2,1,96,512]{3,2,1,0:T(8,128)(2,1)S(1)}, bf16[2,1,96,512]{3,2,1,0:T(8,128)(2,1)S(1)}, u32[]{:S(2)}, u32[]{:S(2)}) %collective-permute-start.1) | collective-permute-done | bytes 196640 | tf_op jit(solution)/shard_map/ppermute | solution.py:309
  11.6 0.0 collective-permute-done.refs_8_.refs_3_
  11.6 0.0 copy-done.1
  11.6 0.0 copy-done.4
  11.6 1.4 %shard_map.96 = (bf16[128,512]{1,0:T(8,128)(2,1)S(1)}, bf16[128,512]{1,0:T(8,128)(2,1)S(1)}, bf16[128,512]{1,0:T(8,128)(2,1)S(1)}, bf16[2,2,128,256]{3,2,1,0:T(8...) custom-call(s32[1]{0:T(128)S(6)} %copy.10.refs_0_, s32[1]{0:T(128)S(6)} %copy.11.refs_1_, ...), custom_call_target="tpu_custom_call" | custom-call | flops 2147483648 | bytes 4194304 | tf_op jit(solution)/shard_map/pallas_call | solution.py:336
  13.0 1.1 %collective-permute-start.2 = (bf16[3,128,256]{2,1,0:T(8,128)(2,1)S(1)}, bf16[3,128,256]{2,1,0:T(8,128)(2,1)S(1)}, u32[]{:S(2)}, u32[]{:S(2)}) collective-permute-start(bf16[3,128,256]{2,1,0:T(8,128)(2,1)S(1)} %get-tuple-element.24), channel_id=1, source_target_pairs={{0,16},{16,0},{4,20},{20,4},{8,24},{24,8},{12,28},{28,12},{1,5},{5... | collective-permute-start | bytes 589832 | tf_op jit(solution)/shard_map/ppermute | solution.py:304
  14.1 1.3 %collective-permute-start.4 = (bf16[2,128,256]{2,1,0:T(8,128)(2,1)S(1)}, bf16[2,128,256]{2,1,0:T(8,128)(2,1)S(1)}, u32[]{:S(2)}, u32[]{:S(2)}) collective-permute-start(bf16[2,128,256]{2,1,0:T(8,128)(2,1)S(1)} %get-tuple-element.40), channel_id=1, source_target_pairs={{0,2},{1,3},{2,0},{3,1},{4,6},{5,7},{6,4},{7,5},{8,10},{9,11},{10,... | collective-permute-start | bytes 393224 | tf_op jit(solution)/shard_map/ppermute | solution.py:307
  15.4 0.0 copy-start.3
  15.4 1.9 %collective-permute-start.3 = (bf16[4,128,256]{2,1,0:T(8,128)(2,1)S(1)}, bf16[4,128,256]{2,1,0:T(8,128)(2,1)S(1)}, u32[]{:S(2)}, u32[]{:S(2)}) collective-permute-start(bf16[4,128,256]{2,1,0:T(8,128)(2,1)S(1)} %pad_maximum_fusion), channel_id=1, source_target_pairs={{0,8},{8,0},{4,12},{12,4},{16,24},{24,16},{20,28},{28,20},{5,9},{9... | collective-permute-start | bytes 786440 | tf_op jit(solution)/shard_map/ppermute | solution.py:304
  17.4 1.9 %collective-permute-done.4 = bf16[2,128,256]{2,1,0:T(8,128)(2,1)S(1)} collective-permute-done((bf16[2,128,256]{2,1,0:T(8,128)(2,1)S(1)}, bf16[2,128,256]{2,1,0:T(8,128)(2,1)S(1)}, u32[]{:S(2)}, u32[]{:S(2)}) %collective-permute-start.4) | collective-permute-done | bytes 131104 | tf_op jit(solution)/shard_map/ppermute | solution.py:307
  19.3 0.7 %collective-permute-start.5 = (bf16[3,128,256]{2,1,0:T(8,128)(2,1)S(1)}, bf16[3,128,256]{2,1,0:T(8,128)(2,1)S(1)}, u32[]{:S(2)}, u32[]{:S(2)}) collective-permute-start(bf16[3,128,256]{2,1,0:T(8,128)(2,1)S(1)} %get-tuple-element.42), channel_id=1, source_target_pairs={{8,16},{16,8},{12,20},{20,12},{1,13},{13,1},{5,17},{17,5},{9,21},{... | collective-permute-start | bytes 589832 | tf_op jit(solution)/shard_map/ppermute | solution.py:304
  20.0 2.3 %collective-permute-start.6 = (bf16[3,128,256]{2,1,0:T(8,128)(2,1)S(1)}, bf16[3,128,256]{2,1,0:T(8,128)(2,1)S(1)}, u32[]{:S(2)}, u32[]{:S(2)}) collective-permute-start(bf16[3,128,256]{2,1,0:T(8,128)(2,1)S(1)} %get-tuple-element.41), channel_id=1, source_target_pairs={{13,25},{25,13},{17,29},{29,17},{15,27},{27,15},{19,31},{31,19}} | collective-permute-start | bytes 589832 | tf_op jit(solution)/shard_map/ppermute | solution.py:304
  22.3 0.0 collective-permute-done.2.refs_8_
  22.3 1.0 %collective-permute-start.7 = (bf16[128,256]{1,0:T(8,128)(2,1)S(1)}, bf16[128,256]{1,0:T(8,128)(2,1)S(1)}, u32[]{:S(2)}, u32[]{:S(2)}) collective-permute-start(bf16[128,256]{1,0:T(8,128)(2,1)S(1)} %slice_bitcast_fusion), channel_id=1, source_target_pairs={{0,2},{1,3},{2,0},{3,1},{4,6},{5,7},{6,4},{7,5},{8,10},{9,11},{10,... | collective-permute-start | bytes 196616 | tf_op jit(solution)/shard_map/ppermute | solution.py:307
  23.4 5.0 %collective-permute-done.3.refs_9_ = bf16[4,128,256]{2,1,0:T(8,128)(2,1)S(1)} collective-permute-done((bf16[4,128,256]{2,1,0:T(8,128)(2,1)S(1)}, bf16[4,128,256]{2,1,0:T(8,128)(2,1)S(1)}, u32[]{:S(2)}, u32[]{:S(2)}) %collective-permute-start.3) | collective-permute-done | bytes 262176 | tf_op jit(solution)/shard_map/ppermute | solution.py:304
  28.4 0.0 collective-permute-done.7.refs_12_
  28.4 0.0 collective-permute-done.5.refs_10_
  28.4 2.5 %collective-permute-done.6.refs_11_ = bf16[3,128,256]{2,1,0:T(8,128)(2,1)S(1)} collective-permute-done((bf16[3,128,256]{2,1,0:T(8,128)(2,1)S(1)}, bf16[3,128,256]{2,1,0:T(8,128)(2,1)S(1)}, u32[]{:S(2)}, u32[]{:S(2)}) %collective-permute-start.6) | collective-permute-done | bytes 196640 | tf_op jit(solution)/shard_map/ppermute | solution.py:304
  30.9 0.0 copy-done.3
  30.9 1.3 %shard_map.98 = (bf16[2,128,512]{2,1,0:T(8,128)(2,1)S(1)}, f32[4,64,256]{2,1,0:T(8,128)S(1)}, bf16[4,64,256]{2,1,0:T(8,128)(2,1)S(1)}, bf16[4,64,256]{2,1,0:T(8,128)(2,1)S(1)}, bf16[4,64,256]{2,1,0:T(8,128)(2,1)S(1)}) custom-call(s32[1]{0:T(128)S(6)} %copy.10.refs_0_, s32[1]{0:T(128)S(6)} %copy.11.refs_1_, bf16[1,2,1,960,512]{4,3,2,1,0:T(8,128)(2,1)S(1)} %bitcast.21, ...), custom_call_target="tpu_custom_call" | custom-call | flops 2147483648 | bytes 4194304 | tf_op jit(solution)/shard_map/pallas_call | solution.py:364
  32.3 0.1 collective-permute-start.8
  32.3 1.4 %collective-permute-start.9 = (bf16[4,64,256]{2,1,0:T(8,128)(2,1)S(1)}, bf16[4,64,256]{2,1,0:T(8,128)(2,1)S(1)}, u32[]{:S(2)}, u32[]{:S(2)}) collective-permute-start(bf16[4,64,256]{2,1,0:T(8,128)(2,1)S(1)} %get-tuple-element.32), channel_id=1, source_target_pairs={{0,3},{1,2},{2,1},{3,0},{4,7},{5,6},{6,5},{7,4},{8,11},{9,10},{10,... | collective-permute-start | bytes 393224 | tf_op jit(solution)/shard_map/ppermute | solution.py:307
  33.7 0.5 %collective-permute-start.10 = (bf16[4,64,256]{2,1,0:T(8,128)(2,1)S(1)}, bf16[4,64,256]{2,1,0:T(8,128)(2,1)S(1)}, u32[]{:S(2)}, u32[]{:S(2)}) collective-permute-start(bf16[4,64,256]{2,1,0:T(8,128)(2,1)S(1)} %get-tuple-element.33), channel_id=1, source_target_pairs={{0,2},{1,3},{2,0},{3,1},{4,6},{5,7},{6,4},{7,5},{8,10},{9,11},{10,... | collective-permute-start | bytes 393224 | tf_op jit(solution)/shard_map/ppermute | solution.py:307
  34.2 0.3 collective-permute-start.11
  34.5 0.0 collective-permute-done.8.refs_3_
  34.5 2.3 %shard_map.99 = bf16[1,2,1,960,512]{4,3,2,1,0:T(8,128)(2,1)} custom-call(s32[1]{0:T(128)S(6)} %copy.10.refs_0_, s32[1]{0:T(128)S(6)} %copy.11.refs_1_, bf16[2,128,512]{2,1,0:T(8,128)(2,1)S(1)} %get-tuple-element.28.refs_2_, bf16[2,128,512]{2,1,0:T(8,128)(2,1)S(1)} %collective-permute-done.8.refs_3_, bf16[128,512]{1,0:T(8,128)(2,1)S(1)} %get-tuple-element.29.refs_4_, ...), custom_call_target="tpu_custom_call" | custom-call | flops 2147483648 | bytes 4194304 | tf_op jit(solution)/shard_map/pallas_call | solution.py:382
  36.9 1.3 %collective-permute-done.9.refs_0_ = bf16[4,64,256]{2,1,0:T(8,128)(2,1)S(1)} collective-permute-done((bf16[4,64,256]{2,1,0:T(8,128)(2,1)S(1)}, bf16[4,64,256]{2,1,0:T(8,128)(2,1)S(1)}, u32[]{:S(2)}, u32[]{:S(2)}) %collective-permute-start.9) | collective-permute-done | bytes 131104 | tf_op jit(solution)/shard_map/ppermute | solution.py:307
  38.2 2.6 %collective-permute-done.10.refs_1_ = bf16[4,64,256]{2,1,0:T(8,128)(2,1)S(1)} collective-permute-done((bf16[4,64,256]{2,1,0:T(8,128)(2,1)S(1)}, bf16[4,64,256]{2,1,0:T(8,128)(2,1)S(1)}, u32[]{:S(2)}, u32[]{:S(2)}) %collective-permute-start.10) | collective-permute-done | bytes 131104 | tf_op jit(solution)/shard_map/ppermute | solution.py:307
  40.8 0.0 collective-permute-done.11.refs_2_
  40.8 0.7 %shard_map.100 = (f32[2,64,256]{2,1,0:T(8,128)}, f32[2,64,256]{2,1,0:T(8,128)}) custom-call(f32[4,64,256]{2,1,0:T(8,128)S(1)} %get-tuple-element.31.kept_ref, bf16[4,64,256]{2,1,0:T(8,128)(2,1)S(1)} %collective-permute-done.9.refs_0_, bf16[4,64,256]{2,1,0:T(8,128)(2,1)S(1)} %collective-permute-done.10.refs_1_, ...), custom_call_target="tpu_custom_call" | custom-call | tf_op jit(solution)/shard_map/pallas_call | solution.py:396
  (6 shorter events, 0.1 us)
Async XLA Ops:
  0.6 11.0 %collective-permute-start = (bf16[1,2,1,960,512]{4,3,2,1,0:T(8,128)(2,1)}, bf16[1,2,1,960,512]{4,3,2,1,0:T(8,128)(2,1)S(1)}, u32[]{:S(2)}, u32[]{:S(2)}) collective-permute-start(bf16[1,2,1,960,512]{4,3,2,1,0:T(8,128)(2,1)} %bitcast.19), channel_id=1, source_target_pairs={{0,1},{1,0},{2,3},{3,2},{4,5},{5,4},{6,7},{7,6},{8,9},{9,8},{10,11... | collective-permute-start | bytes 5898248 | tf_op jit(solution)/shard_map/ppermute | solution.py:307
  2.3 9.3 %collective-permute-start.1 = (bf16[2,1,96,512]{3,2,1,0:T(8,128)(2,1)S(1)}, bf16[2,1,96,512]{3,2,1,0:T(8,128)(2,1)S(1)}, u32[]{:S(2)}, u32[]{:S(2)}) collective-permute-start(bf16[2,1,96,512]{3,2,1,0:T(8,128)(2,1)S(1)} %slice.42), channel_id=1, source_target_pairs={{0,4},{4,8},{8,12},{12,16},{16,20},{20,24},{24,28},{1,5},{5,9},{9,... | collective-permute-start | bytes 589832 | tf_op jit(solution)/shard_map/ppermute | solution.py:309
  6.8 1.1 %copy-start = (bf16[2,4,512,96]{2,3,1,0:T(8,128)(2,1)S(1)}, bf16[2,4,512,96]{2,3,1,0:T(8,128)(2,1)}, u32[]{:S(2)}) copy-start(bf16[2,4,512,96]{2,3,1,0:T(8,128)(2,1)} %param.7) | copy-start | bytes 2359300
  6.8 1.2 %copy-start.2 = (bf16[3,3,96,128]{3,2,1,0:T(8,128)(2,1)S(1)}, bf16[3,3,96,128]{3,2,1,0:T(8,128)(2,1)}, u32[]{:S(2)}) copy-start(bf16[3,3,96,128]{3,2,1,0:T(8,128)(2,1)} %refs_3_.1) | copy-start | bytes 663556
  8.0 3.7 %copy-start.1 = (bf16[1,2,1,512,960]{3,4,2,1,0:T(8,128)(2,1)S(1)}, bf16[1,2,1,512,960]{3,4,2,1,0:T(8,128)(2,1)}, u32[]{:S(2)}) copy-start(bf16[1,2,1,512,960]{3,4,2,1,0:T(8,128)(2,1)} %param.12) | copy-start | bytes 5898244
  8.0 3.7 %copy-start.4 = (bf16[448,512]{1,0:T(8,128)(2,1)S(1)}, bf16[448,512]{1,0:T(8,128)(2,1)}, u32[]{:S(2)}) copy-start(bf16[448,512]{1,0:T(8,128)(2,1)} %constant.21.clone.refs_9_.refs_4_.refs_6_) | copy-start | bytes 1376260
  13.0 9.3 %collective-permute-start.2 = (bf16[3,128,256]{2,1,0:T(8,128)(2,1)S(1)}, bf16[3,128,256]{2,1,0:T(8,128)(2,1)S(1)}, u32[]{:S(2)}, u32[]{:S(2)}) collective-permute-start(bf16[3,128,256]{2,1,0:T(8,128)(2,1)S(1)} %get-tuple-element.24), channel_id=1, source_target_pairs={{0,16},{16,0},{4,20},{20,4},{8,24},{24,8},{12,28},{28,12},{1,5},{5... | collective-permute-start | bytes 589832 | tf_op jit(solution)/shard_map/ppermute | solution.py:304
  14.1 5.1 %collective-permute-start.4 = (bf16[2,128,256]{2,1,0:T(8,128)(2,1)S(1)}, bf16[2,128,256]{2,1,0:T(8,128)(2,1)S(1)}, u32[]{:S(2)}, u32[]{:S(2)}) collective-permute-start(bf16[2,128,256]{2,1,0:T(8,128)(2,1)S(1)} %get-tuple-element.40), channel_id=1, source_target_pairs={{0,2},{1,3},{2,0},{3,1},{4,6},{5,7},{6,4},{7,5},{8,10},{9,11},{10,... | collective-permute-start | bytes 393224 | tf_op jit(solution)/shard_map/ppermute | solution.py:307
  15.4 15.5 %copy-start.3 = (bf16[128,256]{1,0:T(8,128)(2,1)S(1)}, bf16[128,256]{1,0:T(8,128)(2,1)}, u32[]{:S(2)}) copy-start(bf16[128,256]{1,0:T(8,128)(2,1)} %refs_5_.3) | copy-start | bytes 196612
  15.4 13.0 %collective-permute-start.3 = (bf16[4,128,256]{2,1,0:T(8,128)(2,1)S(1)}, bf16[4,128,256]{2,1,0:T(8,128)(2,1)S(1)}, u32[]{:S(2)}, u32[]{:S(2)}) collective-permute-start(bf16[4,128,256]{2,1,0:T(8,128)(2,1)S(1)} %pad_maximum_fusion), channel_id=1, source_target_pairs={{0,8},{8,0},{4,12},{12,4},{16,24},{24,16},{20,28},{28,20},{5,9},{9... | collective-permute-start | bytes 786440 | tf_op jit(solution)/shard_map/ppermute | solution.py:304
  19.3 9.1 %collective-permute-start.5 = (bf16[3,128,256]{2,1,0:T(8,128)(2,1)S(1)}, bf16[3,128,256]{2,1,0:T(8,128)(2,1)S(1)}, u32[]{:S(2)}, u32[]{:S(2)}) collective-permute-start(bf16[3,128,256]{2,1,0:T(8,128)(2,1)S(1)} %get-tuple-element.42), channel_id=1, source_target_pairs={{8,16},{16,8},{12,20},{20,12},{1,13},{13,1},{5,17},{17,5},{9,21},{... | collective-permute-start | bytes 589832 | tf_op jit(solution)/shard_map/ppermute | solution.py:304
  20.0 10.9 %collective-permute-start.6 = (bf16[3,128,256]{2,1,0:T(8,128)(2,1)S(1)}, bf16[3,128,256]{2,1,0:T(8,128)(2,1)S(1)}, u32[]{:S(2)}, u32[]{:S(2)}) collective-permute-start(bf16[3,128,256]{2,1,0:T(8,128)(2,1)S(1)} %get-tuple-element.41), channel_id=1, source_target_pairs={{13,25},{25,13},{17,29},{29,17},{15,27},{27,15},{19,31},{31,19}} | collective-permute-start | bytes 589832 | tf_op jit(solution)/shard_map/ppermute | solution.py:304
  22.3 6.1 %collective-permute-start.7 = (bf16[128,256]{1,0:T(8,128)(2,1)S(1)}, bf16[128,256]{1,0:T(8,128)(2,1)S(1)}, u32[]{:S(2)}, u32[]{:S(2)}) collective-permute-start(bf16[128,256]{1,0:T(8,128)(2,1)S(1)} %slice_bitcast_fusion), channel_id=1, source_target_pairs={{0,2},{1,3},{2,0},{3,1},{4,6},{5,7},{6,4},{7,5},{8,10},{9,11},{10,... | collective-permute-start | bytes 196616 | tf_op jit(solution)/shard_map/ppermute | solution.py:307
  32.3 2.3 %collective-permute-start.8 = (bf16[2,128,512]{2,1,0:T(8,128)(2,1)S(1)}, bf16[2,128,512]{2,1,0:T(8,128)(2,1)S(1)}, u32[]{:S(2)}, u32[]{:S(2)}) collective-permute-start(bf16[2,128,512]{2,1,0:T(8,128)(2,1)S(1)} %get-tuple-element.28.refs_2_), channel_id=1, source_target_pairs={{0,1},{1,0},{2,3},{3,2},{4,5},{5,4},{6,7},{7,6},{8,9},{9,8},{10,11... | collective-permute-start | bytes 786440 | tf_op jit(solution)/shard_map/ppermute | solution.py:307
  32.3 5.9 %collective-permute-start.9 = (bf16[4,64,256]{2,1,0:T(8,128)(2,1)S(1)}, bf16[4,64,256]{2,1,0:T(8,128)(2,1)S(1)}, u32[]{:S(2)}, u32[]{:S(2)}) collective-permute-start(bf16[4,64,256]{2,1,0:T(8,128)(2,1)S(1)} %get-tuple-element.32), channel_id=1, source_target_pairs={{0,3},{1,2},{2,1},{3,0},{4,7},{5,6},{6,5},{7,4},{8,11},{9,10},{10,... | collective-permute-start | bytes 393224 | tf_op jit(solution)/shard_map/ppermute | solution.py:307
  33.7 7.0 %collective-permute-start.10 = (bf16[4,64,256]{2,1,0:T(8,128)(2,1)S(1)}, bf16[4,64,256]{2,1,0:T(8,128)(2,1)S(1)}, u32[]{:S(2)}, u32[]{:S(2)}) collective-permute-start(bf16[4,64,256]{2,1,0:T(8,128)(2,1)S(1)} %get-tuple-element.33), channel_id=1, source_target_pairs={{0,2},{1,3},{2,0},{3,1},{4,6},{5,7},{6,4},{7,5},{8,10},{9,11},{10,... | collective-permute-start | bytes 393224 | tf_op jit(solution)/shard_map/ppermute | solution.py:307
  34.2 6.6 %collective-permute-start.11 = (bf16[4,64,256]{2,1,0:T(8,128)(2,1)S(1)}, bf16[4,64,256]{2,1,0:T(8,128)(2,1)S(1)}, u32[]{:S(2)}, u32[]{:S(2)}) collective-permute-start(bf16[4,64,256]{2,1,0:T(8,128)(2,1)S(1)} %get-tuple-element.34), channel_id=1, source_target_pairs={{0,1},{1,0},{2,3},{3,2},{4,5},{5,4},{6,7},{7,6},{8,9},{9,8},{10,11... | collective-permute-start | bytes 393224 | tf_op jit(solution)/shard_map/ppermute | solution.py:307

commit v10 on v9

--- a/solution.py
+++ b/solution.py
@@ -217,8 +217,9 @@
         else:
             came = jnp.concatenate([part[last - 1], part[last]], axis=1)
         total = total + came.astype(F32)
-    high, low = halves(jnp.concatenate([sum_ref[...], total], axis=1))
-    out_ref[...] = (product(proj_ref[...], high, TN) + product(proj_ref[...], low, TN)) * factor
+    parts = jnp.concatenate(halves(jnp.concatenate([sum_ref[...], total], axis=1)), axis=0)
+    weights = jnp.concatenate([proj_ref[...], proj_ref[...]], axis=0)
+    out_ref[...] = product(weights, parts, TN) * factor
     parts, share, width = kept_ref.shape
     place = lax.axis_index("band")
     for k in range(band):

time: 42.2 us -> 42 us (level)
  starting transfers between devices: 14.5 us -> 15 us
  waiting for transfers between devices: 15.6 us -> 15.1 us
    ppermute x4, starting transfers between devices: 6 us -> 6.83 us  [along_rows(): return lax.ppermute(x, ('rows', 'band'), pairs)]
    ppermute x7, waiting for transfers between devices: 5.81 us -> 5.19 us  [across(): return lax.ppermute(x, 'band', [(p, p ^ k) for p in range(band)])]
where the time goes in v10:
time: 42 us; the launch traced here: 41.4 us
  waiting for transfers between devices  15.1 us (36%)
  starting transfers between devices  15 us (36%)
  Pallas kernels  7.19 us (17%)
  between operations  2.08 us (5%)
  local copies, waits for them, and re-layouts  1.97 us (5%)
    ppermute x4, waiting for transfers between devices, along_rows(): return lax.ppermute(x, ('rows', 'band'), pairs)  7.68 us
    ppermute x4, starting transfers between devices, along_rows(): return lax.ppermute(x, ('rows', 'band'), pairs)  6.83 us
    ppermute x7, waiting for transfers between devices, across(): return lax.ppermute(x, 'band', [(p, p ^ k) for p in range(band)])  5.19 us
    ppermute x7, starting transfers between devices, across(): return lax.ppermute(x, 'band', [(p, p ^ k) for p in range(band)])  5.02 us
    ppermute x1, starting transfers between devices, shards(): lax.ppermute(frames[:, -1:], 'rows', [(i, i + 1) for i in range(row_block...  3.15 us
    pallas_call x1, Pallas kernels, shards(): pl.pallas_call(lambda *refs: pyramid_kernel(band, factor, *refs), grid=(s...  2.33 us
    ppermute x1, waiting for transfers between devices, shards(): lax.ppermute(frames[:, -1:], 'rows', [(i, i + 1) for i in range(row_block...  2.21 us
    pallas_call x1, Pallas kernels, shards(): pl.pallas_call(local_rows_kernel, out_shape=(jax.ShapeDtypeStruct((mid, c...  1.44 us
  transfers between devices with their start and end apart: 12, of which 6 were waited for; matrix products, arithmetic and copies ran while one was open for 3% of the time, Pallas kernels for 9%

profile of v10, /device:TPU:25, one launch (start us, length us, event | category | flops | bytes accessed | tf_op | source)
XLA Modules:
  0.0 41.4 jit_solution(2359450830658302969)
XLA Ops:
  0.6 0.7 %collective-permute-start = (bf16[1,2,1,960,512]{4,3,2,1,0:T(8,128)(2,1)}, bf16[1,2,1,960,512]{4,3,2,1,0:T(8,128)(2,1)S(1)}, u32[]{:S(2)}, u32[]{:S(2)}) collective-permute-start(bf16[1,2,1,960,512]{4,3,2,1,0:T(8,128)(2,1)} %bitcast.19), channel_id=1, source_target_pairs={{0,1},{1,0},{2,3},{3,2},{4,5},{5,4},{6,7},{7,6},{8,9},{9,8},{10,11... | collective-permute-start | bytes 5898248 | tf_op jit(solution)/shard_map/ppermute | solution.py:308
  1.4 0.9 %slice.42 = bf16[2,1,96,512]{3,2,1,0:T(8,128)(2,1)S(1)} slice(bf16[2,4,96,512]{3,2,1,0:T(8,128)(2,1)} %bitcast.17), slice={[0:2], [3:4], [0:96], [0:512]} | slice | bytes 393216 | tf_op jit(solution)/shard_map/slice | solution.py:310
  2.3 3.1 %collective-permute-start.1 = (bf16[2,1,96,512]{3,2,1,0:T(8,128)(2,1)S(1)}, bf16[2,1,96,512]{3,2,1,0:T(8,128)(2,1)S(1)}, u32[]{:S(2)}, u32[]{:S(2)}) collective-permute-start(bf16[2,1,96,512]{3,2,1,0:T(8,128)(2,1)S(1)} %slice.42), channel_id=1, source_target_pairs={{0,4},{4,8},{8,12},{12,16},{16,20},{20,24},{24,28},{1,5},{5,9},{9,... | collective-permute-start | bytes 589832 | tf_op jit(solution)/shard_map/ppermute | solution.py:310
  6.8 0.0 copy-start
  6.8 0.0 copy-start.2
  6.8 0.1 shard_map.94.picker_ref.refs_6_
  7.0 1.0 %copy-done = bf16[2,4,512,96]{2,3,1,0:T(8,128)(2,1)S(1)} copy-done((bf16[2,4,512,96]{2,3,1,0:T(8,128)(2,1)S(1)}, bf16[2,4,512,96]{2,3,1,0:T(8,128)(2,1)}, u32[]{:S(2)}) %copy-start) | copy-done | bytes 786456
  7.9 0.0 copy-done.2
  8.0 0.0 copy-start.1
  8.0 0.0 copy-start.4
  8.0 1.4 %shard_map.95 = (bf16[128,512]{1,0:T(8,128)(2,1)S(1)}, f32[128,512]{1,0:T(8,128)S(1)}) custom-call(bf16[512,768]{1,0:T(8,128)(2,1)S(1)} %shard_map.94.picker_ref.refs_6_, bf16[2,4,96,512]{3,2,1,0:T(8,128)(2,1)S(1)} %bitcast.18, bf16[3,3,96,128]{3,2,1,0:T(8,128)(2,1)S(1)} %copy-done.2), custom_call_target="tpu_custom_call" | custom-call | flops 2147483648 | bytes 2097152 | tf_op jit(solution)/shard_map/pallas_call | solution.py:318
  9.4 2.2 %collective-permute-done.1.refs_2_ = bf16[2,1,96,512]{3,2,1,0:T(8,128)(2,1)S(1)} collective-permute-done((bf16[2,1,96,512]{3,2,1,0:T(8,128)(2,1)S(1)}, bf16[2,1,96,512]{3,2,1,0:T(8,128)(2,1)S(1)}, u32[]{:S(2)}, u32[]{:S(2)}) %collective-permute-start.1) | collective-permute-done | bytes 196640 | tf_op jit(solution)/shard_map/ppermute | solution.py:310
  11.6 0.0 collective-permute-done.refs_8_.refs_3_
  11.6 0.0 copy-done.1
  11.6 0.0 copy-done.4
  11.6 1.4 %shard_map.96 = (bf16[128,512]{1,0:T(8,128)(2,1)S(1)}, bf16[128,512]{1,0:T(8,128)(2,1)S(1)}, bf16[128,512]{1,0:T(8,128)(2,1)S(1)}, bf16[2,2,128,256]{3,2,1,0:T(8...) custom-call(s32[1]{0:T(128)S(6)} %copy.10.refs_0_, s32[1]{0:T(128)S(6)} %copy.11.refs_1_, ...), custom_call_target="tpu_custom_call" | custom-call | flops 2147483648 | bytes 4194304 | tf_op jit(solution)/shard_map/pallas_call | solution.py:337
  13.0 1.1 %collective-permute-start.2 = (bf16[3,128,256]{2,1,0:T(8,128)(2,1)S(1)}, bf16[3,128,256]{2,1,0:T(8,128)(2,1)S(1)}, u32[]{:S(2)}, u32[]{:S(2)}) collective-permute-start(bf16[3,128,256]{2,1,0:T(8,128)(2,1)S(1)} %get-tuple-element.24), channel_id=1, source_target_pairs={{0,16},{16,0},{4,20},{20,4},{8,24},{24,8},{12,28},{28,12},{1,5},{5... | collective-permute-start | bytes 589832 | tf_op jit(solution)/shard_map/ppermute | solution.py:305
  14.1 1.3 %collective-permute-start.4 = (bf16[2,128,256]{2,1,0:T(8,128)(2,1)S(1)}, bf16[2,128,256]{2,1,0:T(8,128)(2,1)S(1)}, u32[]{:S(2)}, u32[]{:S(2)}) collective-permute-start(bf16[2,128,256]{2,1,0:T(8,128)(2,1)S(1)} %get-tuple-element.40), channel_id=1, source_target_pairs={{0,2},{1,3},{2,0},{3,1},{4,6},{5,7},{6,4},{7,5},{8,10},{9,11},{10,... | collective-permute-start | bytes 393224 | tf_op jit(solution)/shard_map/ppermute | solution.py:308
  15.4 0.0 copy-start.3
  15.4 2.2 %collective-permute-start.3 = (bf16[4,128,256]{2,1,0:T(8,128)(2,1)S(1)}, bf16[4,128,256]{2,1,0:T(8,128)(2,1)S(1)}, u32[]{:S(2)}, u32[]{:S(2)}) collective-permute-start(bf16[4,128,256]{2,1,0:T(8,128)(2,1)S(1)} %pad_maximum_fusion), channel_id=1, source_target_pairs={{0,8},{8,0},{4,12},{12,4},{16,24},{24,16},{20,28},{28,20},{5,9},{9... | collective-permute-start | bytes 786440 | tf_op jit(solution)/shard_map/ppermute | solution.py:305
  17.7 1.6 %collective-permute-done.4 = bf16[2,128,256]{2,1,0:T(8,128)(2,1)S(1)} collective-permute-done((bf16[2,128,256]{2,1,0:T(8,128)(2,1)S(1)}, bf16[2,128,256]{2,1,0:T(8,128)(2,1)S(1)}, u32[]{:S(2)}, u32[]{:S(2)}) %collective-permute-start.4) | collective-permute-done | bytes 131104 | tf_op jit(solution)/shard_map/ppermute | solution.py:308
  19.3 0.7 %collective-permute-start.5 = (bf16[3,128,256]{2,1,0:T(8,128)(2,1)S(1)}, bf16[3,128,256]{2,1,0:T(8,128)(2,1)S(1)}, u32[]{:S(2)}, u32[]{:S(2)}) collective-permute-start(bf16[3,128,256]{2,1,0:T(8,128)(2,1)S(1)} %get-tuple-element.42), channel_id=1, source_target_pairs={{8,16},{16,8},{12,20},{20,12},{1,13},{13,1},{5,17},{17,5},{9,21},{... | collective-permute-start | bytes 589832 | tf_op jit(solution)/shard_map/ppermute | solution.py:305
  20.0 2.8 %collective-permute-start.6 = (bf16[3,128,256]{2,1,0:T(8,128)(2,1)S(1)}, bf16[3,128,256]{2,1,0:T(8,128)(2,1)S(1)}, u32[]{:S(2)}, u32[]{:S(2)}) collective-permute-start(bf16[3,128,256]{2,1,0:T(8,128)(2,1)S(1)} %get-tuple-element.41), channel_id=1, source_target_pairs={{13,25},{25,13},{17,29},{29,17},{15,27},{27,15},{19,31},{31,19}} | collective-permute-start | bytes 589832 | tf_op jit(solution)/shard_map/ppermute | solution.py:305
  22.8 0.0 collective-permute-done.2.refs_8_
  22.9 0.5 %collective-permute-start.7 = (bf16[128,256]{1,0:T(8,128)(2,1)S(1)}, bf16[128,256]{1,0:T(8,128)(2,1)S(1)}, u32[]{:S(2)}, u32[]{:S(2)}) collective-permute-start(bf16[128,256]{1,0:T(8,128)(2,1)S(1)} %slice_bitcast_fusion), channel_id=1, source_target_pairs={{0,2},{1,3},{2,0},{3,1},{4,6},{5,7},{6,4},{7,5},{8,10},{9,11},{10,... | collective-permute-start | bytes 196616 | tf_op jit(solution)/shard_map/ppermute | solution.py:308
  23.4 4.6 %collective-permute-done.3.refs_9_ = bf16[4,128,256]{2,1,0:T(8,128)(2,1)S(1)} collective-permute-done((bf16[4,128,256]{2,1,0:T(8,128)(2,1)S(1)}, bf16[4,128,256]{2,1,0:T(8,128)(2,1)S(1)}, u32[]{:S(2)}, u32[]{:S(2)}) %collective-permute-start.3) | collective-permute-done | bytes 262176 | tf_op jit(solution)/shard_map/ppermute | solution.py:305
  28.0 0.0 collective-permute-done.7.refs_12_
  28.0 0.0 collective-permute-done.5.refs_10_
  28.0 3.1 %collective-permute-done.6.refs_11_ = bf16[3,128,256]{2,1,0:T(8,128)(2,1)S(1)} collective-permute-done((bf16[3,128,256]{2,1,0:T(8,128)(2,1)S(1)}, bf16[3,128,256]{2,1,0:T(8,128)(2,1)S(1)}, u32[]{:S(2)}, u32[]{:S(2)}) %collective-permute-start.6) | collective-permute-done | bytes 196640 | tf_op jit(solution)/shard_map/ppermute | solution.py:305
  31.1 0.0 copy-done.3
  31.1 1.2 %shard_map.98 = (bf16[2,128,512]{2,1,0:T(8,128)(2,1)S(1)}, f32[4,64,256]{2,1,0:T(8,128)S(1)}, bf16[4,64,256]{2,1,0:T(8,128)(2,1)S(1)}, bf16[4,64,256]{2,1,0:T(8,128)(2,1)S(1)}, bf16[4,64,256]{2,1,0:T(8,128)(2,1)S(1)}) custom-call(s32[1]{0:T(128)S(6)} %copy.10.refs_0_, s32[1]{0:T(128)S(6)} %copy.11.refs_1_, bf16[1,2,1,960,512]{4,3,2,1,0:T(8,128)(2,1)S(1)} %bitcast.21, ...), custom_call_target="tpu_custom_call" | custom-call | flops 2147483648 | bytes 4194304 | tf_op jit(solution)/shard_map/pallas_call | solution.py:365
  32.2 0.1 collective-permute-start.8
  32.3 2.0 %collective-permute-start.9 = (bf16[4,64,256]{2,1,0:T(8,128)(2,1)S(1)}, bf16[4,64,256]{2,1,0:T(8,128)(2,1)S(1)}, u32[]{:S(2)}, u32[]{:S(2)}) collective-permute-start(bf16[4,64,256]{2,1,0:T(8,128)(2,1)S(1)} %get-tuple-element.32), channel_id=1, source_target_pairs={{0,3},{1,2},{2,1},{3,0},{4,7},{5,6},{6,5},{7,4},{8,11},{9,10},{10,... | collective-permute-start | bytes 393224 | tf_op jit(solution)/shard_map/ppermute | solution.py:308
  34.3 0.0 collective-permute-start.10
  34.3 0.4 %collective-permute-start.11 = (bf16[4,64,256]{2,1,0:T(8,128)(2,1)S(1)}, bf16[4,64,256]{2,1,0:T(8,128)(2,1)S(1)}, u32[]{:S(2)}, u32[]{:S(2)}) collective-permute-start(bf16[4,64,256]{2,1,0:T(8,128)(2,1)S(1)} %get-tuple-element.34), channel_id=1, source_target_pairs={{0,1},{1,0},{2,3},{3,2},{4,5},{5,4},{6,7},{7,6},{8,9},{9,8},{10,11... | collective-permute-start | bytes 393224 | tf_op jit(solution)/shard_map/ppermute | solution.py:308
  34.7 0.0 collective-permute-done.8.refs_3_
  34.7 2.3 %shard_map.99 = bf16[1,2,1,960,512]{4,3,2,1,0:T(8,128)(2,1)} custom-call(s32[1]{0:T(128)S(6)} %copy.10.refs_0_, s32[1]{0:T(128)S(6)} %copy.11.refs_1_, bf16[2,128,512]{2,1,0:T(8,128)(2,1)S(1)} %get-tuple-element.28.refs_2_, bf16[2,128,512]{2,1,0:T(8,128)(2,1)S(1)} %collective-permute-done.8.refs_3_, bf16[128,512]{1,0:T(8,128)(2,1)S(1)} %get-tuple-element.29.refs_4_, ...), custom_call_target="tpu_custom_call" | custom-call | flops 2147483648 | bytes 4194304 | tf_op jit(solution)/shard_map/pallas_call | solution.py:383
  37.1 1.2 %collective-permute-done.9.refs_0_ = bf16[4,64,256]{2,1,0:T(8,128)(2,1)S(1)} collective-permute-done((bf16[4,64,256]{2,1,0:T(8,128)(2,1)S(1)}, bf16[4,64,256]{2,1,0:T(8,128)(2,1)S(1)}, u32[]{:S(2)}, u32[]{:S(2)}) %collective-permute-start.9) | collective-permute-done | bytes 131104 | tf_op jit(solution)/shard_map/ppermute | solution.py:308
  38.3 2.4 %collective-permute-done.10.refs_1_ = bf16[4,64,256]{2,1,0:T(8,128)(2,1)S(1)} collective-permute-done((bf16[4,64,256]{2,1,0:T(8,128)(2,1)S(1)}, bf16[4,64,256]{2,1,0:T(8,128)(2,1)S(1)}, u32[]{:S(2)}, u32[]{:S(2)}) %collective-permute-start.10) | collective-permute-done | bytes 131104 | tf_op jit(solution)/shard_map/ppermute | solution.py:308
  40.7 0.0 collective-permute-done.11.refs_2_
  40.7 0.7 %shard_map.100 = (f32[2,64,256]{2,1,0:T(8,128)}, f32[2,64,256]{2,1,0:T(8,128)}) custom-call(f32[4,64,256]{2,1,0:T(8,128)S(1)} %get-tuple-element.31.kept_ref, bf16[4,64,256]{2,1,0:T(8,128)(2,1)S(1)} %collective-permute-done.9.refs_0_, bf16[4,64,256]{2,1,0:T(8,128)(2,1)S(1)} %collective-permute-done.10.refs_1_, ...), custom_call_target="tpu_custom_call" | custom-call | tf_op jit(solution)/shard_map/pallas_call | solution.py:397
  (6 shorter events, 0.1 us)
Async XLA Ops:
  0.6 11.0 %collective-permute-start = (bf16[1,2,1,960,512]{4,3,2,1,0:T(8,128)(2,1)}, bf16[1,2,1,960,512]{4,3,2,1,0:T(8,128)(2,1)S(1)}, u32[]{:S(2)}, u32[]{:S(2)}) collective-permute-start(bf16[1,2,1,960,512]{4,3,2,1,0:T(8,128)(2,1)} %bitcast.19), channel_id=1, source_target_pairs={{0,1},{1,0},{2,3},{3,2},{4,5},{5,4},{6,7},{7,6},{8,9},{9,8},{10,11... | collective-permute-start | bytes 5898248 | tf_op jit(solution)/shard_map/ppermute | solution.py:308
  2.3 9.3 %collective-permute-start.1 = (bf16[2,1,96,512]{3,2,1,0:T(8,128)(2,1)S(1)}, bf16[2,1,96,512]{3,2,1,0:T(8,128)(2,1)S(1)}, u32[]{:S(2)}, u32[]{:S(2)}) collective-permute-start(bf16[2,1,96,512]{3,2,1,0:T(8,128)(2,1)S(1)} %slice.42), channel_id=1, source_target_pairs={{0,4},{4,8},{8,12},{12,16},{16,20},{20,24},{24,28},{1,5},{5,9},{9,... | collective-permute-start | bytes 589832 | tf_op jit(solution)/shard_map/ppermute | solution.py:310
  6.8 1.1 %copy-start = (bf16[2,4,512,96]{2,3,1,0:T(8,128)(2,1)S(1)}, bf16[2,4,512,96]{2,3,1,0:T(8,128)(2,1)}, u32[]{:S(2)}) copy-start(bf16[2,4,512,96]{2,3,1,0:T(8,128)(2,1)} %param.7) | copy-start | bytes 2359300
  6.8 1.2 %copy-start.2 = (bf16[3,3,96,128]{3,2,1,0:T(8,128)(2,1)S(1)}, bf16[3,3,96,128]{3,2,1,0:T(8,128)(2,1)}, u32[]{:S(2)}) copy-start(bf16[3,3,96,128]{3,2,1,0:T(8,128)(2,1)} %refs_3_.1) | copy-start | bytes 663556
  8.0 3.7 %copy-start.1 = (bf16[1,2,1,512,960]{3,4,2,1,0:T(8,128)(2,1)S(1)}, bf16[1,2,1,512,960]{3,4,2,1,0:T(8,128)(2,1)}, u32[]{:S(2)}) copy-start(bf16[1,2,1,512,960]{3,4,2,1,0:T(8,128)(2,1)} %param.12) | copy-start | bytes 5898244
  8.0 3.7 %copy-start.4 = (bf16[448,512]{1,0:T(8,128)(2,1)S(1)}, bf16[448,512]{1,0:T(8,128)(2,1)}, u32[]{:S(2)}) copy-start(bf16[448,512]{1,0:T(8,128)(2,1)} %constant.21.clone.refs_9_.refs_4_.refs_6_) | copy-start | bytes 1376260
  13.0 9.8 %collective-permute-start.2 = (bf16[3,128,256]{2,1,0:T(8,128)(2,1)S(1)}, bf16[3,128,256]{2,1,0:T(8,128)(2,1)S(1)}, u32[]{:S(2)}, u32[]{:S(2)}) collective-permute-start(bf16[3,128,256]{2,1,0:T(8,128)(2,1)S(1)} %get-tuple-element.24), channel_id=1, source_target_pairs={{0,16},{16,0},{4,20},{20,4},{8,24},{24,8},{12,28},{28,12},{1,5},{5... | collective-permute-start | bytes 589832 | tf_op jit(solution)/shard_map/ppermute | solution.py:305
  14.1 5.1 %collective-permute-start.4 = (bf16[2,128,256]{2,1,0:T(8,128)(2,1)S(1)}, bf16[2,128,256]{2,1,0:T(8,128)(2,1)S(1)}, u32[]{:S(2)}, u32[]{:S(2)}) collective-permute-start(bf16[2,128,256]{2,1,0:T(8,128)(2,1)S(1)} %get-tuple-element.40), channel_id=1, source_target_pairs={{0,2},{1,3},{2,0},{3,1},{4,6},{5,7},{6,4},{7,5},{8,10},{9,11},{10,... | collective-permute-start | bytes 393224 | tf_op jit(solution)/shard_map/ppermute | solution.py:308
  15.4 15.7 %copy-start.3 = (bf16[128,256]{1,0:T(8,128)(2,1)S(1)}, bf16[128,256]{1,0:T(8,128)(2,1)}, u32[]{:S(2)}) copy-start(bf16[128,256]{1,0:T(8,128)(2,1)} %refs_5_.3) | copy-start | bytes 196612
  15.4 12.5 %collective-permute-start.3 = (bf16[4,128,256]{2,1,0:T(8,128)(2,1)S(1)}, bf16[4,128,256]{2,1,0:T(8,128)(2,1)S(1)}, u32[]{:S(2)}, u32[]{:S(2)}) collective-permute-start(bf16[4,128,256]{2,1,0:T(8,128)(2,1)S(1)} %pad_maximum_fusion), channel_id=1, source_target_pairs={{0,8},{8,0},{4,12},{12,4},{16,24},{24,16},{20,28},{28,20},{5,9},{9... | collective-permute-start | bytes 786440 | tf_op jit(solution)/shard_map/ppermute | solution.py:305
  19.3 8.7 %collective-permute-start.5 = (bf16[3,128,256]{2,1,0:T(8,128)(2,1)S(1)}, bf16[3,128,256]{2,1,0:T(8,128)(2,1)S(1)}, u32[]{:S(2)}, u32[]{:S(2)}) collective-permute-start(bf16[3,128,256]{2,1,0:T(8,128)(2,1)S(1)} %get-tuple-element.42), channel_id=1, source_target_pairs={{8,16},{16,8},{12,20},{20,12},{1,13},{13,1},{5,17},{17,5},{9,21},{... | collective-permute-start | bytes 589832 | tf_op jit(solution)/shard_map/ppermute | solution.py:305
  20.0 11.1 %collective-permute-start.6 = (bf16[3,128,256]{2,1,0:T(8,128)(2,1)S(1)}, bf16[3,128,256]{2,1,0:T(8,128)(2,1)S(1)}, u32[]{:S(2)}, u32[]{:S(2)}) collective-permute-start(bf16[3,128,256]{2,1,0:T(8,128)(2,1)S(1)} %get-tuple-element.41), channel_id=1, source_target_pairs={{13,25},{25,13},{17,29},{29,17},{15,27},{27,15},{19,31},{31,19}} | collective-permute-start | bytes 589832 | tf_op jit(solution)/shard_map/ppermute | solution.py:305
  22.9 5.1 %collective-permute-start.7 = (bf16[128,256]{1,0:T(8,128)(2,1)S(1)}, bf16[128,256]{1,0:T(8,128)(2,1)S(1)}, u32[]{:S(2)}, u32[]{:S(2)}) collective-permute-start(bf16[128,256]{1,0:T(8,128)(2,1)S(1)} %slice_bitcast_fusion), channel_id=1, source_target_pairs={{0,2},{1,3},{2,0},{3,1},{4,6},{5,7},{6,4},{7,5},{8,10},{9,11},{10,... | collective-permute-start | bytes 196616 | tf_op jit(solution)/shard_map/ppermute | solution.py:308
  32.2 2.5 %collective-permute-start.8 = (bf16[2,128,512]{2,1,0:T(8,128)(2,1)S(1)}, bf16[2,128,512]{2,1,0:T(8,128)(2,1)S(1)}, u32[]{:S(2)}, u32[]{:S(2)}) collective-permute-start(bf16[2,128,512]{2,1,0:T(8,128)(2,1)S(1)} %get-tuple-element.28.refs_2_), channel_id=1, source_target_pairs={{0,1},{1,0},{2,3},{3,2},{4,5},{5,4},{6,7},{7,6},{8,9},{9,8},{10,11... | collective-permute-start | bytes 786440 | tf_op jit(solution)/shard_map/ppermute | solution.py:308
  32.3 6.0 %collective-permute-start.9 = (bf16[4,64,256]{2,1,0:T(8,128)(2,1)S(1)}, bf16[4,64,256]{2,1,0:T(8,128)(2,1)S(1)}, u32[]{:S(2)}, u32[]{:S(2)}) collective-permute-start(bf16[4,64,256]{2,1,0:T(8,128)(2,1)S(1)} %get-tuple-element.32), channel_id=1, source_target_pairs={{0,3},{1,2},{2,1},{3,0},{4,7},{5,6},{6,5},{7,4},{8,11},{9,10},{10,... | collective-permute-start | bytes 393224 | tf_op jit(solution)/shard_map/ppermute | solution.py:308
  34.3 6.4 %collective-permute-start.10 = (bf16[4,64,256]{2,1,0:T(8,128)(2,1)S(1)}, bf16[4,64,256]{2,1,0:T(8,128)(2,1)S(1)}, u32[]{:S(2)}, u32[]{:S(2)}) collective-permute-start(bf16[4,64,256]{2,1,0:T(8,128)(2,1)S(1)} %get-tuple-element.33), channel_id=1, source_target_pairs={{0,2},{1,3},{2,0},{3,1},{4,6},{5,7},{6,4},{7,5},{8,10},{9,11},{10,... | collective-permute-start | bytes 393224 | tf_op jit(solution)/shard_map/ppermute | solution.py:308
  34.3 6.4 %collective-permute-start.11 = (bf16[4,64,256]{2,1,0:T(8,128)(2,1)S(1)}, bf16[4,64,256]{2,1,0:T(8,128)(2,1)S(1)}, u32[]{:S(2)}, u32[]{:S(2)}) collective-permute-start(bf16[4,64,256]{2,1,0:T(8,128)(2,1)S(1)} %get-tuple-element.34), channel_id=1, source_target_pairs={{0,1},{1,0},{2,3},{3,2},{4,5},{5,4},{6,7},{7,6},{8,9},{9,8},{10,11... | collective-permute-start | bytes 393224 | tf_op jit(solution)/shard_map/ppermute | solution.py:308
